TPU v7x, 32 devices: a whole 2x2x4 slice. The times are simulated.
32 devices in a mesh: row: 8 (over z, y), col: 4 (over x, core).
Axes of the slice: x: 2, y: 2, z: 4, core: 2. Of those that a mesh axis runs over, the one named last changes fastest.
Arguments:
- factor: bfloat16 [8192, 8192], P('row', 'col'), may hold values from -0.078125 to 0.078125
- diag_inv: bfloat16 [8192, 1024], P('row'), may hold values from -1 to 1.5, as said below
- rhs: bfloat16 [8192, 256], P('row'), may hold values from -6 to 6
- forward_values: bfloat16 [8192, 256], P('row'), may hold values from -6 to 6
Outputs:
- forward_solved: bfloat16 [3072, 256], replicated
- forward_rest: float32 [8192, 256], P('row', 'col')
- back_sums: float32 [8192, 256], P('col', 'row')
- solution: float32 [8192, 256], P('row')
Inputs may be any that keep to these rules, and one draw needn't show every extreme that they name: Each 1024 x 1024 block of diag_inv is lower triangular with diagonal entries between 0.5 and 1.5.
All inputs are finite; a program needn't handle non-finite values.
Results may differ from a plain program's by a relative error of at most 0.0095.
Values may be sent and summed in bfloat16 or wider, within the bound.
No kernel may reach another device: no remote copies, remote signals or barrier semaphores. Data moves between devices by JAX's collectives and lax.ppermute only.
A program may use at most 64 MiB of HBM per device.

v0:
```python
import jax
import jax.numpy as jnp
from jax import lax
from jax.sharding import PartitionSpec as P

NB = 1024
STEPS = 3


def broadcast(array, axis, root):
    mine = lax.axis_index(axis) == root
    return lax.psum(jnp.where(mine, array, jnp.zeros_like(array)), axis)


def local(factor, diag_inv, rhs, forward_values):
    row_blocks = factor.shape[0] // NB
    col_blocks = factor.shape[1] // NB
    columns = rhs.shape[1]
    row_count = lax.axis_size("row")
    col_count = lax.axis_size("col")
    my_row = lax.axis_index("row")
    my_col = lax.axis_index("col")
    block_total = row_blocks * row_count
    col_share = columns // col_count
    row_share = columns // row_count
    blocks = factor.reshape(row_blocks, NB, col_blocks, NB)
    inverses = diag_inv.reshape(row_blocks, NB, NB)
    right_sides = rhs.reshape(row_blocks, NB, columns)
    starting = forward_values.reshape(row_blocks, NB, columns)
    row_ids = my_row * row_blocks + jnp.arange(row_blocks, dtype=jnp.int32)
    col_ids = my_col * col_blocks + jnp.arange(col_blocks, dtype=jnp.int32)
    partial_value = jnp.zeros((row_blocks, NB, columns), jnp.float32)
    solved_list = []
    for position in range(STEPS):
        owner_row = position // row_blocks
        local_row = position % row_blocks
        owner_col = position // col_blocks
        local_col = position % col_blocks
        own_part = partial_value[local_row]
        inverse = inverses[local_row]
        right_side = right_sides[local_row]
        summed = lax.psum_scatter(
            own_part.astype(jnp.bfloat16), "col", scatter_dimension=1, tiled=True
        ).astype(jnp.float32)
        side_share = lax.dynamic_slice_in_dim(right_side, my_col * col_share, col_share, 1)
        residue = (side_share.astype(jnp.float32) - summed).astype(jnp.bfloat16)
        gathered = lax.all_gather(residue, "col", axis=1, tiled=True)

        def solve_whole(operand):
            return jnp.dot(inverse, operand, preferred_element_type=jnp.float32).astype(
                jnp.bfloat16
            )

        def skip_whole(operand):
            return jnp.zeros_like(operand)

        local_value = lax.cond(my_row == owner_row, solve_whole, skip_whole, gathered)
        solved_block = broadcast(local_value, "row", owner_row)
        solved_list.append(solved_block)

        def update(totals):
            column = blocks[:, :, local_col, :]
            update_term = jnp.einsum(
                "anm,mr->anr", column, solved_block, preferred_element_type=jnp.float32
            )
            later_rows = (row_ids > position)[:, None, None]
            return totals + jnp.where(later_rows, update_term, 0.0)

        def keep_same(totals):
            return totals

        partial_value = lax.cond(my_col == owner_col, update, keep_same, partial_value)
    rest_sum = lax.psum_scatter(
        partial_value.astype(jnp.bfloat16), "col", scatter_dimension=2, tiled=True
    ).astype(jnp.float32)
    side_part = lax.dynamic_slice_in_dim(right_sides, my_col * col_share, col_share, 2)
    forward_rest = (side_part.astype(jnp.float32) - rest_sum).reshape(row_blocks * NB, col_share)
    forward_solved = jnp.concatenate(solved_list, axis=0)
    back_partial = jnp.zeros((col_blocks, NB, columns), jnp.float32)
    result = jnp.zeros((row_blocks, NB, columns), jnp.float32)
    for reverse_turn in range(STEPS):
        position = block_total - 1 - reverse_turn
        owner_row = position // row_blocks
        local_row = position % row_blocks
        owner_col = position // col_blocks
        local_col = position % col_blocks
        own_part = back_partial[local_col]
        summed = lax.psum_scatter(
            own_part.astype(jnp.bfloat16), "row", scatter_dimension=1, tiled=True
        ).astype(jnp.float32)
        rounded = summed.astype(jnp.bfloat16)
        collected = lax.all_gather(rounded, "row", axis=1, tiled=True)
        gathered_sum = broadcast(collected, "col", owner_col)
        inverse = inverses[local_row]
        earlier = starting[local_row]
        current = result[local_row]
        row_block = blocks[local_row]

        def solve_back(totals):
            centred = (earlier.astype(jnp.float32) - gathered_sum.astype(jnp.float32)).astype(
                jnp.bfloat16
            )
            answer = lax.dot_general(
                inverse, centred, (((0,), (0,)), ((), ())), preferred_element_type=jnp.float32
            )
            update_term = jnp.einsum(
                "nbm,nr->bmr",
                row_block,
                answer.astype(jnp.bfloat16),
                preferred_element_type=jnp.float32,
            )
            earlier_cols = (col_ids < position)[:, None, None]
            return (answer, totals + jnp.where(earlier_cols, update_term, 0.0))

        def keep_back(totals):
            return (current, totals)

        answer, back_partial = lax.cond(my_row == owner_row, solve_back, keep_back, back_partial)
        result = result.at[local_row].set(answer)
    back_sums = (
        lax.psum_scatter(back_partial.astype(jnp.bfloat16), "row", scatter_dimension=2, tiled=True)
        .astype(jnp.float32)
        .reshape(col_blocks * NB, row_share)
    )
    return (forward_solved, forward_rest, back_sums, result.reshape(row_blocks * NB, columns))


def solution(mesh):
    placed = (P("row", "col"), P("row", None), P("row", None), P("row", None))
    return jax.shard_map(
        local,
        mesh=mesh,
        in_specs=placed,
        out_specs=(P(), P("row", "col"), P("col", "row"), P("row", None)),
        check_vma=False,
    )
```

profile of v0, /device:TPU:16, one launch (start us, length us, event | category | flops | bytes accessed | tf_op | source)
XLA Modules:
  0.0 598.9 jit_solution(4747007674824197926)
XLA Ops:
  8.5 7.2 %all_gather.16 = bf16[1024,256]{0,1:T(8,128)(2,1)S(1)} all-gather(bf16[1024,64]{0,1:T(8,128)(2,1)S(1)} %copy.105), channel_id=1, replica_groups=mesh['row'=8,'col'=4] {'col'}, dimensions={1}, use_global_device_ids=true | all-gather | bytes 655360 | tf_op jit(solution)/shard_map/all_gather | solution.py:47
  16.7 6.5 %copy.56 = bf16[1024,2048]{0,1:T(8,128)(2,1)} copy(bf16[1024,2048]{1,0:T(8,128)(2,1)} %param.28) | data formatting | bytes 8388608 | tf_op args[0]
  26.8 1.9 fusion.17
  28.6 2.1 copy.93
  30.8 58.2 %all-reduce.6.cloned.1.call-done = bf16[1024,256]{0,1:T(8,128)(2,1)} async-done(((bf16[1024,256]{0,1:T(8,128)(2,1)}), bf16[1024,256]{0,1:T(8,128)(2,1)}) %all-reduce.6.cloned.1.call-update) | async-done | bytes 524304 | tf_op jit(solution)/shard_map/psum | solution.py:12
  89.0 9.6 %conditional.10 = (f32[1,1024,256]{2,1,0:T(8,128)}) conditional(s32[]{:T(128)} %convert_element_type.136, () %tuple.79, (s32[1]{0:T(128)}, bf16[1,1024,2,1024]{1,3,2,0:T(8,128)(2,1)}, bf16[1024,256]{0,1:T(8,128)(2,1)}) %tuple.173), branch_computations={%region_3.4_spmd, %region_4.5_spmd} | conditional | flops 537133056 | bytes 12059153 | solution.py:72
  89.0 6.3 %copy.57 = bf16[1,1024,2,1024]{3,1,2,0:T(8,128)(2,1)} copy(bf16[1,1024,2,1024]{1,3,2,0:T(8,128)(2,1)} %get-tuple-element.256) | data formatting | bytes 8388608 | tf_op jit(solution)/shard_map
  95.2 3.4 fusion.2
  98.6 2.2 copy.59
  100.9 52.8 %reduce-scatter.19.cloned.1.call-done = bf16[32,1024]{1,0:T(8,128)(2,1)} async-done(((bf16[256,1024]{1,0:T(8,128)(2,1)}), bf16[32,1024]{1,0:T(8,128)(2,1)}) %reduce-scatter.19.cloned.1.call-update) | async-done | bytes 65552
  153.7 28.1 %all_gather.19 = bf16[1024,256]{0,1:T(8,128)(2,1)S(1)} all-gather(bf16[1024,32]{0,1:T(8,128)(2,1)} %bitcast.113), channel_id=1, replica_groups=mesh['row'=8,'col'=4] {'row'}, dimensions={1}, use_global_device_ids=true | all-gather | bytes 589824 | tf_op jit(solution)/shard_map/all_gather | solution.py:92
  183.7 7.2 %all_gather.17 = bf16[1024,256]{0,1:T(8,128)(2,1)S(1)} all-gather(bf16[1024,64]{0,1:T(8,128)(2,1)S(1)} %fusion.19), channel_id=1, replica_groups=mesh['row'=8,'col'=4] {'col'}, dimensions={1}, use_global_device_ids=true | all-gather | bytes 655360 | tf_op jit(solution)/shard_map/all_gather | solution.py:47
  192.6 27.0 %all-reduce.12.cloned.1.call-done = bf16[1024,256]{0,1:T(8,128)(2,1)} async-done(((bf16[1024,256]{0,1:T(8,128)(2,1)}), bf16[1024,256]{0,1:T(8,128)(2,1)}) %all-reduce.12.cloned.1.call-update) | async-done | bytes 524304 | tf_op jit(solution)/shard_map/psum | solution.py:12
  221.0 1.9 fusion.18
  222.8 2.1 copy.95
  225.0 69.9 %all-reduce.8.cloned.1.call-done = bf16[1024,256]{0,1:T(8,128)(2,1)} async-done(((bf16[1024,256]{0,1:T(8,128)(2,1)}), bf16[1024,256]{0,1:T(8,128)(2,1)}) %all-reduce.8.cloned.1.call-update) | async-done | bytes 524304 | tf_op jit(solution)/shard_map/psum | solution.py:12
  294.9 10.0 %conditional.12 = (f32[1,1024,256]{2,1,0:T(8,128)}) conditional(s32[]{:T(128)} %convert_element_type.136, f32[1,1024,256]{2,1,0:T(8,128)} %get-tuple-element.315, (s32[1]{0:T(128)}, bf16[1,1024,2,1024]{1,3,2,0:T(8,128)(2,1)}, bf16[1024,256]{0,1:T(8,128)(2,1)}, f32[1,1024,256]{2,1,0:T(8,128)}) %tuple.175), branch_computations={%region_9.10_spmd, %region_10.11_spmd} | conditional | flops 537395200 | bytes 13107729 | solution.py:72
  294.9 6.3 %copy.62 = bf16[1,1024,2,1024]{3,1,2,0:T(8,128)(2,1)} copy(bf16[1,1024,2,1024]{1,3,2,0:T(8,128)(2,1)} %get-tuple-element.261) | data formatting | bytes 8388608 | tf_op jit(solution)/shard_map
  301.1 3.7 fusion.6
  304.9 2.2 copy.64
  307.2 51.9 %reduce-scatter.21.cloned.1.call-done = bf16[32,1024]{1,0:T(8,128)(2,1)} async-done(((bf16[256,1024]{1,0:T(8,128)(2,1)}), bf16[32,1024]{1,0:T(8,128)(2,1)}) %reduce-scatter.21.cloned.1.call-update) | async-done | bytes 65552
  359.1 28.3 %all_gather.20 = bf16[1024,256]{0,1:T(8,128)(2,1)S(1)} all-gather(bf16[1024,32]{0,1:T(8,128)(2,1)} %bitcast.114), channel_id=1, replica_groups=mesh['row'=8,'col'=4] {'row'}, dimensions={1}, use_global_device_ids=true | all-gather | bytes 589824 | tf_op jit(solution)/shard_map/all_gather | solution.py:92
  389.3 7.2 %all_gather.18 = bf16[1024,256]{0,1:T(8,128)(2,1)S(1)} all-gather(bf16[1024,64]{0,1:T(8,128)(2,1)S(1)} %fusion.20), channel_id=1, replica_groups=mesh['row'=8,'col'=4] {'col'}, dimensions={1}, use_global_device_ids=true | all-gather | bytes 655360 | tf_op jit(solution)/shard_map/all_gather | solution.py:47
  398.2 27.0 %all-reduce.14.cloned.1.call-done = bf16[1024,256]{0,1:T(8,128)(2,1)} async-done(((bf16[1024,256]{0,1:T(8,128)(2,1)}), bf16[1024,256]{0,1:T(8,128)(2,1)}) %all-reduce.14.cloned.1.call-update) | async-done | bytes 524304 | tf_op jit(solution)/shard_map/psum | solution.py:12
  425.2 2.5 conditional.17
  425.2 2.5 copy.103
  429.0 71.2 %all-reduce.10.cloned.1.call-done = bf16[1024,256]{0,1:T(8,128)(2,1)} async-done(((bf16[1024,256]{0,1:T(8,128)(2,1)}), bf16[1024,256]{0,1:T(8,128)(2,1)}) %all-reduce.10.cloned.1.call-update) | async-done | bytes 524304 | tf_op jit(solution)/shard_map/psum | solution.py:12
  500.2 2.3 copy.69
  503.8 1.6 copy.82
  505.3 61.2 %reduce-scatter.17.cloned.1.call-done = bf16[2,1024,32]{1,2,0:T(8,128)(2,1)} async-done(((bf16[2,1024,256]{1,2,0:T(8,128)(2,1)}), bf16[2,1024,32]{1,2,0:T(8,128)(2,1)}) %reduce-scatter.17.cloned.1.call-update) | async-done | bytes 131088 | tf_op jit(solution)/shard_map/reduce_scatter | solution.py:121
  568.2 22.6 %reduce-scatter.15.cloned.1.call-done = bf16[1,1024,64]{1,2,0:T(8,128)(2,1)} async-done(((bf16[1,1024,256]{1,2,0:T(8,128)(2,1)}), bf16[1,1024,64]{1,2,0:T(8,128)(2,1)}) %reduce-scatter.15.cloned.1.call-update) | async-done | bytes 131088 | tf_op jit(solution)/shard_map/reduce_scatter | solution.py:73
  590.7 1.6 fusion.22
  (60 shorter events, 22.0 us)
Async XLA Ops:
  7.2 1.0 copy-start
  7.2 81.8 %all-reduce.6.cloned.1.call-start = ((), (), s32[]{:S(2)}) async-start(), calls=%async_computation.6 | async-start | bytes 1048576 | tf_op jit(solution)/shard_map/psum | solution.py:12
  16.6 137.1 %reduce-scatter.19.cloned.1.call-start = ((), (), s32[]{:S(2)}) async-start(), calls=%async_computation.15 | async-start | bytes 589824
  16.6 7.3 %copy-start.7 = (bf16[1024,256]{1,0:T(8,128)(2,1)S(1)}, bf16[1024,256]{1,0:T(8,128)(2,1)}, u32[]{:S(2)}) copy-start(bf16[1024,256]{1,0:T(8,128)(2,1)} %param.31) | copy-start | bytes 1572868
  30.7 152.0 %reduce-scatter.11.cloned.1.call-start = ((), (), s32[]{:S(2)}) async-start(), calls=%async_computation.7 | async-start | bytes 655360 | tf_op jit(solution)/shard_map/reduce_scatter | solution.py:42
  100.9 118.7 %all-reduce.12.cloned.1.call-start = ((), (), s32[]{:S(2)}) async-start(), calls=%async_computation.12 | async-start | bytes 1048576 | tf_op jit(solution)/shard_map/psum | solution.py:12
  182.7 112.2 %all-reduce.8.cloned.1.call-start = ((), (), s32[]{:S(2)}) async-start(), calls=%async_computation.8 | async-start | bytes 1048576 | tf_op jit(solution)/shard_map/psum | solution.py:12
  192.6 166.5 %reduce-scatter.21.cloned.1.call-start = ((), (), s32[]{:S(2)}) async-start(), calls=%async_computation.16 | async-start | bytes 589824
  224.9 163.4 %reduce-scatter.13.cloned.1.call-start = ((), (), s32[]{:S(2)}) async-start(), calls=%async_computation.9 | async-start | bytes 655360 | tf_op jit(solution)/shard_map/reduce_scatter | solution.py:42
  307.1 118.1 %all-reduce.14.cloned.1.call-start = ((), (), s32[]{:S(2)}) async-start(), calls=%async_computation.13 | async-start | bytes 1048576 | tf_op jit(solution)/shard_map/psum | solution.py:12
  388.3 112.0 %all-reduce.10.cloned.1.call-start = ((), (), s32[]{:S(2)}) async-start(), calls=%async_computation.10 | async-start | bytes 1048576 | tf_op jit(solution)/shard_map/psum | solution.py:12
  398.2 168.4 %reduce-scatter.17.cloned.1.call-start = ((), (), s32[]{:S(2)}) async-start(), calls=%async_computation.14 | async-start | bytes 1179648 | tf_op jit(solution)/shard_map/reduce_scatter | solution.py:121
  429.0 161.8 %reduce-scatter.15.cloned.1.call-start = ((), (), s32[]{:S(2)}) async-start(), calls=%async_computation.11 | async-start | bytes 655360 | tf_op jit(solution)/shard_map/reduce_scatter | solution.py:73
  500.2 2.4 copy-start.8
  500.2 2.4 copy-start.9
Sparse Core Ops, SparseCore 0:
  16.7 72.2 all-reduce.5
  92.7 61.0 reduce-scatter.18
  156.8 21.6 reduce-scatter.10
  182.8 36.7 all-reduce.11
  223.3 71.5 all-reduce.7
  298.1 61.0 reduce-scatter.20
  362.3 21.6 reduce-scatter.12
  388.4 36.7 all-reduce.13
  428.6 71.5 all-reduce.9
  503.9 62.6 reduce-scatter.16
  569.0 21.6 reduce-scatter.14
where the time goes:
time: 602 us; the launch traced here: 599 us
  waiting for transfers between devices  442 us (73%)
  blocking collectives  77.8 us (13%)
  local copies, waits for them, and re-layouts  46.5 us (8%)
  between operations  14 us (2%)
  other arithmetic  11 us (2%)
  matrix products  7.12 us (1%)
    psum x5, waiting for transfers between devices, broadcast(): return lax.psum(jnp.where(mine, array, jnp.zeros_like(array)), axis)  253 us
    unnamed x13, waiting for transfers between devices  105 us
    reduce_scatter x1, waiting for transfers between devices, local(): lax.psum_scatter(back_partial.astype(jnp.bfloat16), 'row', scatter_dimens...  61.2 us
    all_gather x2, blocking collectives, local(): collected = lax.all_gather(rounded, 'row', axis=1, tiled=True)  56.3 us
    reduce_scatter x1, waiting for transfers between devices, local(): lax.psum_scatter(partial_value.astype(jnp.bfloat16), 'col', scatter_dimen...  22.6 us
    all_gather x3, blocking collectives, local(): gathered = lax.all_gather(residue, 'col', axis=1, tiled=True)  21.5 us
    another operation x7, local copies, waits for them, and re-layouts  16.3 us
    unnamed x13, local copies, waits for them, and re-layouts  13.3 us
  transfers between devices with their start and end apart: 11, of which 9 were waited for; matrix products, arithmetic and copies ran while one was open for 10% of the time, Pallas kernels for 0%

commit v1 on v0

v1 whole, which is shorter than its diff:
```python
import functools

import jax
import jax.numpy as jnp
from jax import lax
from jax.experimental import pallas as pl
from jax.experimental.pallas import tpu as pltpu
from jax.sharding import PartitionSpec as P

NB = 1024
STEPS = 3
BOTH = ("row", "col")
BF16, F32 = jnp.bfloat16, jnp.float32


def nn(a, b):
    return jnp.dot(a, b, preferred_element_type=F32)


def nt(a, b):
    return lax.dot_general(a, b, (((1,), (1,)), ((), ())), preferred_element_type=F32)


def flip(x):
    return jnp.transpose(x.astype(F32))


class Copies:
    def __init__(self, sems):
        self.sems = sems
        self.used = 0

    def branch(self):
        self.used = 0

    def start(self, src, dst):
        copy = pltpu.make_async_copy(src, dst, self.sems.at[self.used])
        copy.start()
        self.used += 1
        return copy


def call(kernel, ins, outs, scratch, sems, aliases=None, limit=16, order=()):
    any_space = pl.BlockSpec(memory_space=pl.ANY)
    used, ins = len(ins), list(ins) + list(order)
    outs = list(outs) + [((8, 128), F32)]

    def body(*refs):
        n = len(ins) + len(outs)
        kernel(*refs[:used], *refs[len(ins) : n - 1], *refs[n:])

    return pl.pallas_call(
        body,
        out_shape=[jax.ShapeDtypeStruct(s, d) for s, d in outs],
        in_specs=[any_space] * len(ins),
        out_specs=[any_space] * len(outs),
        scratch_shapes=[pltpu.VMEM(s, d) for s, d in scratch] + [pltpu.SemaphoreType.DMA((sems,))],
        input_output_aliases=aliases or {},
        compiler_params=pltpu.CompilerParams(vmem_limit_bytes=limit << 20),
        cost_estimate=pl.CostEstimate(flops=0, bytes_accessed=0, transcendentals=0),
    )(*ins)


def local(factor, diag_inv, rhs, forward_values):
    rows = lax.axis_size("row")
    cols = lax.axis_size("col")
    cb = factor.shape[1] // NB
    wide = rhs.shape[1]
    assert factor.shape[0] == NB and rows % 4 == 0 and cols % 2 == 0 and rows >= 8 and cb <= 2
    share = wide // cols
    row_share = wide // rows
    piece = cb * row_share
    last = rows - 1
    pairs = rows // 2
    all_cols = range(cols)
    evens = range(0, cols, 2)
    group = lambda j: j // cb
    g0, g1, g2, g5, g6 = group(0), group(1), group(2), group(last - 2), group(last - 1)
    evens5 = [d for d in evens if d // 2 != g5 // 2]
    full, square, tall = (wide, NB), (NB, NB), (NB, wide)
    pair_piece = (2, piece, NB)

    def place():
        return lax.axis_index("row"), lax.axis_index("col")

    def send(x, pairs):
        return lax.ppermute(x, BOTH, [(a * cols + b, d * cols + e) for (a, b), (d, e) in pairs])

    def block(ref, j):
        return ref.at[:, pl.ds((j % cb) * NB, NB)]

    def multiply(q_ref, v, fac, limit):
        _, c = place()
        for b in range(cb):
            q = nn(v, fac[b])
            q = jnp.where(c * cb + b < limit, q, 0.0).astype(BF16)
            q_ref[:, :, b * row_share : (b + 1) * row_share, :] = q.reshape(pairs, 2, row_share, NB)

    def rolled(cp, buf, outs):
        _, c = place()
        return [
            cp.start(buf.at[pl.ds(pl.multiple_of(lax.rem(c + s, cols) * share, share), share)], outs[s])
            for s in all_cols
        ]

    def wait(copies):
        for o in copies:
            o.wait()

    def route(cases, shape, order=(), through=(), times=1):
        n, m = len(cases), len(through)

        def kernel(*refs):
            outs, buf, sems = refs[n + m : n + m + times], refs[-2], refs[-1]
            r, c = place()
            cp = Copies(sems)
            for (cond, _), ref in zip(cases, refs):
                cp.branch()

                @pl.when(cond(r, c))
                def _(ref=ref):
                    cp.start(ref, buf).wait()
                    wait([cp.start(buf, out) for out in outs])

        return call(
            kernel,
            [v for _, v in cases] + list(through),
            [(shape, BF16)] * times + [(x.shape, x.dtype) for x in through],
            [(shape, BF16)],
            1 + times,
            aliases={n + k: times + k for k in range(m)},
            order=order,
        )

    def at(row, col):
        return lambda r, c: (r == row) & (c == col)

    def kernel0(fac, inv, rh, fv, x_out, v_out, y_out, dbuf, lbuf, rbuf, xbuf, vbuf, sems):
        r, c = place()
        cp = Copies(sems)

        @pl.when(r == 0)
        def _():
            ins = [cp.start(rh, rbuf), cp.start(inv, dbuf)]
            ins[0].wait()
            z = flip(rbuf[...]).astype(BF16)
            ins[1].wait()
            xbuf[...] = nt(z, dbuf[...]).astype(BF16)
            own = xbuf.at[pl.ds(pl.multiple_of(c * share, share), share)]
            wait([cp.start(xbuf, x_out), cp.start(own, y_out)])

        cp.branch()

        @pl.when(r == last)
        def _():
            ins = [cp.start(fv, rbuf), cp.start(inv, dbuf)]
            for g, j in ((g6, last - 1), (g5, last - 2)):

                @pl.when(c == g)
                def _(j=j):
                    pltpu.make_async_copy(block(fac, j), lbuf, sems.at[4]).start()

            ins[0].wait()
            w = flip(rbuf[...]).astype(BF16)
            ins[1].wait()
            vbuf[...] = nn(w, dbuf[...])
            v = cp.start(vbuf, v_out)

            @pl.when((c == g6) | (c == g5))
            def _():
                pltpu.make_async_copy(block(fac, 0), lbuf, sems.at[4]).wait()
                xbuf[...] = nn(vbuf[...].astype(BF16), lbuf[...]).astype(BF16)
                cp.start(xbuf, x_out).wait()

            v.wait()

    x1, v7, y0_own, _ = call(
        kernel0,
        [factor, diag_inv, rhs, forward_values],
        [(full, BF16), (full, F32), ((share, NB), BF16)],
        [(square, BF16), (square, BF16), (tall, BF16), (full, BF16), (full, F32)],
        5,
        limit=60,
    )
    q_more = [send(x1, [((last, g6), (last - 1, d)), ((last, g5), (last - 2, d))]) for d in evens5[1:]]
    a1 = send(x1, [((0, g0), (1, g0)), ((last, g6), (last - 1, g5)), ((last, g5), (last - 2, evens5[0]))])
    a2 = send(x1, [((0, g0), (2, g0)), ((last, g6), (last - 1, evens5[0])), ((last, g5), (last - 2, g5))])
    t6_parts = [a2] + q_more
    q75_parts = [a1] + q_more
    entry = [0, 3] + [2 * d for d in range(2, pairs)]
    y0_z = {e: send(y0_own, [((0, b), (e, b)) for b in all_cols]) for e in entry[1:]}

    def kernel7(v_in, fac, *rest):
        sol_out, bq, (fbuf, vbuf, qbuf, sbuf, zbuf, sems) = rest[0], rest[1 : 1 + pairs], rest[1 + pairs :]
        r, _ = place()
        cp = Copies(sems)

        @pl.when(r == last)
        def _():
            fs = [cp.start(fac.at[:, pl.ds(k * NB, NB)], fbuf.at[k]) for k in range(cb)]
            cp.start(v_in, vbuf).wait()
            wait(fs)
            v = vbuf[...]
            multiply(qbuf, v.astype(BF16), fbuf, last)
            done = [cp.start(qbuf.at[d], bq[d]) for d in range(pairs)]
            sbuf[...] = jnp.transpose(v)
            wait(done + [cp.start(sbuf, sol_out)])

        cp.branch()

        @pl.when(r < last - 2)
        def _():
            zbuf[...] = jnp.zeros_like(zbuf)
            wait([cp.start(zbuf, sol_out.at[pl.ds(k * wide, wide)]) for k in range(NB // wide)])

    sol, *bq, tok = call(
        kernel7,
        [v7, factor],
        [(tall, F32)] + [(pair_piece, BF16)] * pairs,
        [((cb, NB, NB), BF16), (full, F32), ((pairs, 2, piece, NB), BF16), (tall, F32), ((wide, wide), F32)],
        2 + cb + pairs,
    )

    y0_cases = [(lambda r, c: r == 0, y0_own)] + [(lambda r, c, e=e: r == e, v) for e, v in y0_z.items()]
    y0_in, tok = route(y0_cases, (share, NB), order=[tok])
    y0_out = send(y0_in, [((e, b), (e ^ 1, b)) for e in entry for b in all_cols])

    def kernel1(p1, fac, inv, rh, fv, x_out, *rest):
        outs, (dbuf, lbuf, rbuf, abuf, xbuf, sems) = rest[:cols], rest[cols:]
        r, c = place()
        cp = Copies(sems)

        @pl.when((r == 1) & (c == g0))
        def _():
            ins = [cp.start(rh, rbuf), cp.start(p1, abuf), cp.start(block(fac, 0), lbuf), cp.start(inv, dbuf)]
            ins[0].wait()
            z = flip(rbuf[...])
            ins[1].wait()
            ins[2].wait()
            z = z - nt(abuf[...], lbuf[...]).astype(BF16).astype(F32)
            ins[3].wait()
            xbuf[...] = nt(z.astype(BF16), dbuf[...]).astype(BF16)
            wait([cp.start(xbuf, x_out)] + rolled(cp, xbuf, outs))

        cp.branch()

        @pl.when((r == last - 1) & (c == g5))
        def _():
            ins = [cp.start(fv, rbuf), cp.start(p1, abuf), cp.start(inv, dbuf), cp.start(block(fac, last - 2), lbuf)]
            ins[0].wait()
            w = flip(rbuf[...])
            ins[1].wait()
            w = w - abuf[...].astype(F32)
            ins[2].wait()
            v = nn(w.astype(BF16), dbuf[...]).astype(BF16)
            ins[3].wait()
            xbuf[...] = nn(v, lbuf[...]).astype(BF16)
            cp.start(xbuf, x_out).wait()

    x3, *parts, tok = call(
        kernel1,
        [a1, factor, diag_inv, rhs, forward_values],
        [(full, BF16)] + [((share, NB), BF16)] * cols,
        [(square, BF16), (square, BF16), (tall, BF16), (full, BF16), (full, BF16)],
        5 + cols,
        order=[tok],
    )
    a3 = send(x3, [((1, g0), (2, g1)), ((last - 1, g5), (last - 2, g5))])
    a4 = [send(x3, [((last - 1, g5), (last - 2, d))]) for d in evens5]

    def within_chip(row, owner):
        own = [((row, owner), (row, owner ^ 1))]
        return own + [((row, d), (row, d + 1)) for d in evens if d // 2 != owner // 2]

    def kernels0(p1, p2, fac, *rest):
        more, (out, lbuf, abuf, xbuf, sems) = rest[: len(evens5) - 1], rest[len(evens5) - 1 :]
        r, c = place()
        cp = Copies(sems)

        @pl.when((r == 2) & (c == g0))
        def _():
            wait([cp.start(p2, abuf), cp.start(block(fac, 0), lbuf)])
            xbuf[...] = nt(abuf[...], lbuf[...]).astype(BF16)
            cp.start(xbuf, out).wait()

        for col, ref in zip([g5] + evens5, [p1, p2] + list(more)):
            cp.branch()

            @pl.when((r == last - 1) & (c == col))
            def _(ref=ref):
                cp.start(ref, xbuf).wait()
                cp.start(xbuf, out).wait()

    t6_even, tok = call(
        kernels0,
        [a1, a2, factor] + q_more,
        [(full, BF16)],
        [(square, BF16), (full, BF16), (full, BF16)],
        3,
        order=[tok],
    )
    s0 = t6_even if g0 == g1 else send(t6_even, [((2, g0), (2, g1))])

    t6_odd = send(t6_even, within_chip(last - 1, g5))

    def is_entry(r, c):
        return ((r % 2 == 0) & (r != 2)) | (r == 3)

    y0_mine, tok = route(
        [(is_entry, y0_in), (lambda r, c: jnp.logical_not(is_entry(r, c)), y0_out)], (share, NB), [tok]
    )

    def kernel2(p0, p1, fac, inv, rh, *rest):
        outs, (dbuf, lbuf, rbuf, abuf, bbuf, xbuf, sems) = rest[cols : 2 * cols], rest[2 * cols :]
        r, c = place()
        cp = Copies(sems)

        @pl.when((r == 2) & (c == g1))
        def _():
            ins = [cp.start(rh, rbuf), cp.start(p1, abuf), cp.start(block(fac, 1), lbuf), cp.start(p0, bbuf), cp.start(inv, dbuf)]
            ins[0].wait()
            z = flip(rbuf[...])
            wait(ins[1:4])
            s = nt(abuf[...], lbuf[...]) + bbuf[...].astype(F32)
            z = z - s.astype(BF16).astype(F32)
            ins[4].wait()
            xbuf[...] = nt(z.astype(BF16), dbuf[...]).astype(BF16)
            wait(rolled(cp, xbuf, outs))

    *parts, tok = call(
        kernel2,
        [s0, a3, factor, diag_inv, rhs] + parts,
        [((share, NB), BF16)] * cols,
        [(square, BF16), (square, BF16), (tall, BF16), (full, BF16), (full, BF16), (full, BF16)],
        5 + cols,
        aliases={5 + k: k for k in range(cols)},
        order=[tok],
    )
    dealt = [send(parts[s], [((1, g0), (1, (g0 + s) % cols)), ((2, g1), (2, (g1 + s) % cols))]) for s in range(1, cols)]

    cases = [(at(1, g0), parts[0]), (at(2, g1), parts[0])]
    for s in range(1, cols):
        cases += [(at(1, (g0 + s) % cols), dealt[s - 1]), (at(2, (g1 + s) % cols), dealt[s - 1])]
    y_own, tok = route(cases, (share, NB), order=[tok])
    to_odd = [pairs - 1] + [d for d in range(1, pairs - 1)]
    to_even = [pairs - 1, 0] + [d for d in range(2, pairs - 1)]
    y_z = [
        send(y_own, [((1, b), (2 * d + 1, b)) for b in all_cols] + [((2, b), (2 * e, b)) for b in all_cols])
        for d, e in zip(to_odd, to_even)
    ]

    def kernelt(*refs):
        n = len(evens5) + 1
        first, second, (_, out, _, abuf, bbuf, sems) = refs[:n], refs[n : 2 * n], refs[2 * n :]
        r, c = place()
        cp = Copies(sems)
        for col, x, q in zip([g5] + evens5, first, second):
            cp.branch()

            @pl.when((r == last - 2) & (c == col))
            def _(x=x, q=q):
                wait([cp.start(x, abuf), cp.start(q, bbuf)])
                abuf[...] = (abuf[...].astype(F32) + bbuf[...].astype(F32)).astype(BF16)
                cp.start(abuf, out).wait()

    t5_even, y0_mine, tok = call(
        kernelt,
        [a3] + a4 + [a2] + q75_parts + [y0_mine],
        [(full, BF16), ((share, NB), BF16)],
        [(full, BF16), (full, BF16)],
        3,
        aliases={2 * len(evens5) + 2: 1},
        order=[tok],
    )
    t5_odd = send(t5_even, within_chip(last - 2, g5))

    y0_all = lax.all_gather(y0_mine, "col", axis=0, tiled=True)
    cases = [(lambda r, c: (r == 1) | (r == 2), y_own)]
    for d, e, v in zip(to_odd, to_even, y_z):
        cases.append((lambda r, c, d=d, e=e: (r == 2 * d + 1) | (r == 2 * e), v))
    y_mine, y_near, tok = route(cases, (share, NB), order=[tok, y0_all], times=2)
    all_swap = [((a, b), (a ^ 1, b)) for a in range(rows) for b in all_cols]
    y_other = send(y_mine, all_swap)

    i = last - 2
    slots = {d: d + 1 for d in range(pairs - 2)}
    slots.update({pairs - 1: 0, pairs - 2: pairs - 1})
    own_slots = {d: d for d in range(pairs)}

    def lands(d):
        return 2 * d if d < (pairs - 2) // 2 else 2 * d + 1

    def kernel5(t6e, t6o, t5e, t5o, fac, inv, fv, *rest):
        n = pairs + 2
        sol_out, outs = rest[n], rest[n + 1 : n + 1 + pairs]
        dbuf, fbuf, rbuf, abuf, qbuf, sbuf, sems = rest[2 * n :]
        r, c = place()
        cp = Copies(sems)
        has = (c == g5) | ((c % 2 == 0) & (c // 2 != g5 // 2))
        sem = sems.at[3 + cb + pairs]

        for row, te, to, to_slot in ((last - 1, t6e, t6o, own_slots), (i, t5e, t5o, slots)):
            cp.branch()

            @pl.when(r == row)
            def _(row=row, te=te, to=to, to_slot=to_slot):
                ins = [cp.start(fv, rbuf), cp.start(inv, dbuf)]
                fs = [cp.start(fac.at[:, pl.ds(k * NB, NB)], fbuf.at[k]) for k in range(cb)]

                @pl.when(has)
                def _():
                    pltpu.make_async_copy(te, abuf, sem).start()

                @pl.when(jnp.logical_not(has))
                def _():
                    pltpu.make_async_copy(to, abuf, sem).start()

                ins[0].wait()
                w = flip(rbuf[...])
                pltpu.make_async_copy(te, abuf, sem).wait()
                w = w - abuf[...].astype(F32)
                ins[1].wait()
                v = nn(w.astype(BF16), dbuf[...])
                wait(fs)
                multiply(qbuf, v.astype(BF16), fbuf, row)
                done = [cp.start(qbuf.at[d], outs[t]) for d, t in to_slot.items()]
                sbuf[...] = jnp.transpose(v)
                wait(done + [cp.start(sbuf, sol_out)])

    sol, *bq, y_near, tok = call(
        kernel5,
        [t6_even, t6_odd, t5_even, t5_odd, factor, diag_inv, forward_values, sol] + bq + [y_near],
        [(tall, F32)] + [(pair_piece, BF16)] * pairs + [((share, NB), BF16)],
        [(square, BF16), ((cb, NB, NB), BF16), (tall, BF16), (full, BF16), ((pairs, 2, piece, NB), BF16), (tall, F32)],
        4 + cb + pairs,
        aliases={7 + k: k for k in range(pairs + 2)},
        order=[tok],
    )
    scattered = []
    for t in range(pairs - 1):
        to = [d for d, k in slots.items() if k == t][0]
        pairs_t = [((last, b), (2 * t + 1, b)) for b in all_cols] + [((last - 1, b), (2 * t, b)) for b in all_cols]
        scattered.append(send(bq[t], pairs_t + [((i, b), (lands(to), b)) for b in all_cols]))

    near_all = lax.all_gather(y_near, "col", axis=0, tiled=True)

    far_all = lax.all_gather(y_other, "col", axis=0, tiled=True)

    def load_by_parity(even, odd, buf, sem):
        r, _ = place()
        for parity, ref in enumerate((even, odd)):

            @pl.when(lax.rem(r, 2) == parity)
            def _(ref=ref):
                pltpu.make_async_copy(ref, buf, sem).start()

        return pltpu.make_async_copy(even, buf, sem)

    def kernelb(own_q, *rest):
        got, (own_out, part_out, bbuf, fbuf, obuf, pbuf, sems) = rest[: pairs - 1], rest[pairs - 1 :]
        r, _ = place()
        cp = Copies(sems)
        pair = r // 2
        refs = list(got) + [own_q]
        for d in range(pairs):
            cp.branch()

            @pl.when(pair == d)
            def _(d=d):
                cp.start(refs[d], bbuf).wait()

            @pl.when(r == lands(d))
            def _(d=d):
                cp.start(refs[slots[d]], fbuf).wait()

        cp.branch()

        takes = functools.reduce(jnp.logical_or, [r == lands(d) for d in range(pairs)])
        for y in (0, 1):
            for more in (False, True):

                @pl.when((lax.rem(r, 2) == y) & (takes if more else jnp.logical_not(takes)))
                def _(y=y, more=more):
                    ours, theirs = bbuf[y].astype(F32), bbuf[1 - y].astype(F32)
                    if more:
                        ours = ours + fbuf[y].astype(F32)
                        theirs = theirs + fbuf[1 - y].astype(F32)
                    obuf[...] = ours
                    pbuf[...] = theirs.astype(BF16)

        wait([cp.start(pbuf, part_out), cp.start(obuf, own_out)])

    own, part, tok = call(
        kernelb,
        [bq[pairs - 1]] + scattered,
        [((piece, NB), F32), ((piece, NB), BF16)],
        [(pair_piece, BF16), (pair_piece, BF16), ((piece, NB), F32), ((piece, NB), BF16)],
        2,
        order=[tok, near_all, far_all],
    )
    theirs = send(part, all_swap)

    owners = sorted({g0, g1, g2})

    def kernelr(y0, near, far, fac, *rest):
        outs, (lbuf, abuf, pbuf, sems) = rest[:cols], rest[cols:]
        r, c = place()
        cp = Copies(sems)

        for g in owners:
            cp.branch()

            @pl.when(c == g)
            def _(g=g):
                ins = []
                if g == g0:
                    ins.append((0, cp.start(y0, abuf.at[0]), cp.start(block(fac, 0), lbuf.at[0])))
                for k, gk, even, odd in ((1, g1, far, near), (2, g2, near, far)):
                    if gk == g:
                        n = len(ins)
                        a = load_by_parity(even, odd, abuf.at[n], sems.at[4 + cols])
                        ins.append((k, a, cp.start(block(fac, k), lbuf.at[n])))
                total = None
                for n, (k, a, b) in enumerate(ins):
                    a.wait()
                    b.wait()
                    p = jnp.where(r > k, nt(abuf[n], lbuf[n]), 0.0)
                    total = p if total is None else total + p
                pbuf[...] = total.astype(BF16)
                wait(rolled(cp, pbuf, outs))

    *p_parts, tok = call(
        kernelr,
        [y0_all, near_all, far_all, factor],
        [((share, NB), BF16)] * cols,
        [((2, NB, NB), BF16), ((2,) + full, BF16), (full, BF16)],
        5 + cols,
        order=[tok],
    )
    p_got = [
        send(p_parts[s], [((a, g), (a, (g + s) % cols)) for a in range(1, rows) for g in owners]) for s in range(1, cols)
    ]

    def kernelo(y0, near, far, rh, own_p, fs_out, side_out, abuf, tbuf, rbuf, pbuf, obuf, sems):
        _, c = place()
        cp = Copies(sems)
        ins = [cp.start(y0, abuf.at[0])]
        ins.append(load_by_parity(far, near, abuf.at[1], sems.at[7]))
        ins.append(load_by_parity(near, far, abuf.at[2], sems.at[8]))
        more = [cp.start(rh, rbuf), cp.start(own_p, pbuf)]
        done = []
        for k in range(STEPS):
            ins[k].wait()
            tbuf[k] = flip(abuf[k]).astype(BF16)
            done.append(cp.start(tbuf.at[k], fs_out.at[pl.ds(k * NB, NB)]))
        wait(more)
        side = flip(rbuf[...])
        for d in all_cols:

            @pl.when(c == d)
            def _(d=d):
                base = side[d * share : (d + 1) * share]
                obuf[...] = base - pbuf[...].astype(F32) if d in owners else base

        wait(done + [cp.start(obuf, side_out)])

    solved, side, tok = call(
        kernelo,
        [y0_all, near_all, far_all, rhs, p_parts[0]],
        [((STEPS * NB, wide), BF16), ((share, NB), F32)],
        [((STEPS,) + full, BF16), ((STEPS,) + tall, BF16), (tall, BF16), ((share, NB), BF16), ((share, NB), F32)],
        9,
        order=[tok],
    )

    rest = side - sum(x.astype(F32) for x in p_got)
    total = own + theirs.astype(F32)
    sums = jnp.concatenate([total[b * row_share : (b + 1) * row_share] for b in range(cb)], axis=1)
    return (solved, jnp.transpose(rest), jnp.transpose(sums), sol)


def solution(mesh):
    placed = (P("row", "col"), P("row", None), P("row", None), P("row", None))
    return jax.shard_map(
        local,
        mesh=mesh,
        in_specs=placed,
        out_specs=(P(), P("row", "col"), P("col", "row"), P("row", None)),
        check_vma=False,
    )
```

time: 602 us -> 93.2 us (0.15)
  the two profiles are of different devices: /device:TPU:16 before, /device:TPU:11 now
where the time goes in v1:
time: 93.2 us; the launch traced here: 92.7 us
  starting transfers between devices  31.2 us (33%)
  blocking collectives  24.6 us (26%)
  waiting for transfers between devices  23.9 us (26%)
  Pallas kernels  5.21 us (6%)
  local copies, waits for them, and re-layouts  5.17 us (6%)
  other arithmetic  1.52 us (2%)
  between operations  1.08 us (1%)
    ppermute x24, starting transfers between devices, send(): lax.ppermute(x, BOTH, [(a * cols + b, d * cols + e) for (a, b), (d, e) in...  31.2 us
    ppermute x24, waiting for transfers between devices, send(): lax.ppermute(x, BOTH, [(a * cols + b, d * cols + e) for (a, b), (d, e) in...  23.9 us
    all_gather x1, blocking collectives, local(): y0_all = lax.all_gather(y0_mine, 'col', axis=0, tiled=True)  9.63 us
    all_gather x1, blocking collectives, local(): far_all = lax.all_gather(y_other, 'col', axis=0, tiled=True)  7.66 us
    all_gather x1, blocking collectives, local(): near_all = lax.all_gather(y_near, 'col', axis=0, tiled=True)  7.28 us
    pallas_call x14, Pallas kernels, call(): pl.pallas_call(body, out_shape=[jax.ShapeDtypeStruct(s, d) for s, d in ou...  5.21 us
    unnamed x14, local copies, waits for them, and re-layouts  5.15 us
  transfers between devices with their start and end apart: 24, of which 5 were waited for; matrix products, arithmetic and copies ran while one was open for 1% of the time, Pallas kernels for 5%

profile of v1, /device:TPU:11, one launch (start us, length us, event | category | flops | bytes accessed | tf_op | source)
XLA Modules:
  0.0 92.7 jit_solution(15001369184712938015)
XLA Ops:
  0.7 0.8 collective-permute-start
  3.6 0.7 collective-permute-start.6
  4.3 2.2 %copy-done = bf16[1024,2048]{1,0:T(8,128)(2,1)S(1)} copy-done((bf16[1024,2048]{1,0:T(8,128)(2,1)S(1)}, bf16[1024,2048]{1,0:T(8,128)(2,1)}, u32[]{:S(2)}) %copy-start) | copy-done | bytes 4194328
  6.5 1.2 %copy-done.5 = f32[256,1024]{1,0:T(8,128)S(1)} copy-done((f32[256,1024]{1,0:T(8,128)S(1)}, f32[256,1024]{1,0:T(8,128)}, u32[]{:S(2)}) %copy-start.5) | copy-done | bytes 1048600
  7.7 1.0 %shard_map.76 = (f32[1024,256]{1,0:T(8,128)}, bf16[2,64,1024]{2,1,0:T(8,128)(2,1)S(1)}, bf16[2,64,1024]{2,1,0:T(8,128)(2,1)S(1)}, bf16[2,64,1024]{2,1,0:T(8,128)...) custom-call(f32[256,1024]{1,0:T(8,128)S(1)} %copy-done.5, bf16[1024,2048]{1,0:T(8,128)(2,1)S(1)} %copy-done), custom_call_target="tpu_custom_call" | custom-call | tf_op jit(solution)/shard_map/pallas_call | solution.py:52
  8.8 1.7 %copy-done.6 = bf16[64,1024]{1,0:T(8,128)(2,1)S(1)} copy-done((bf16[64,1024]{1,0:T(8,128)(2,1)S(1)}, bf16[64,1024]{1,0:T(8,128)(2,1)}, u32[]{:S(2)}) %copy-start.6) | copy-done | bytes 131096
  10.7 0.7 collective-permute-start.4
  11.4 0.7 collective-permute-start.5
  12.1 1.3 %collective-permute-start.7 = (bf16[64,1024]{1,0:T(8,128)(2,1)S(1)}, bf16[64,1024]{1,0:T(8,128)(2,1)S(1)}, u32[]{:S(2)}, u32[]{:S(2)}) collective-permute-start(bf16[64,1024]{1,0:T(8,128)(2,1)S(1)} %get-tuple-element.61.refs_0_), channel_id=1, source_target_pairs={{0,4},{1,5},{2,6},{3,7},{12,8},{13,9},{14,10},{15,11},{16,20},{17,... | collective-permute-start | bytes 393224 | tf_op jit(solution)/shard_map/ppermute | solution.py:87
  13.5 4.5 %collective-permute-done.7.refs_1_ = bf16[64,1024]{1,0:T(8,128)(2,1)S(1)} collective-permute-done((bf16[64,1024]{1,0:T(8,128)(2,1)S(1)}, bf16[64,1024]{1,0:T(8,128)(2,1)S(1)}, u32[]{:S(2)}, u32[]{:S(2)}) %collective-permute-start.7) | collective-permute-done | bytes 131104 | tf_op jit(solution)/shard_map/ppermute | solution.py:87
  18.4 1.3 %collective-permute-start.10 = (bf16[64,1024]{1,0:T(8,128)(2,1)S(1)}, bf16[64,1024]{1,0:T(8,128)(2,1)S(1)}, u32[]{:S(2)}, u32[]{:S(2)}) collective-permute-start(bf16[64,1024]{1,0:T(8,128)(2,1)S(1)} %get-tuple-element.74), channel_id=1, source_target_pairs={{4,7},{8,11}} | collective-permute-start | bytes 393224 | tf_op jit(solution)/shard_map/ppermute | solution.py:87
  21.1 0.7 collective-permute-start.11
  21.8 12.2 %collective-permute-done.10.refs_6_.refs_7_ = bf16[64,1024]{1,0:T(8,128)(2,1)S(1)} collective-permute-done((bf16[64,1024]{1,0:T(8,128)(2,1)S(1)}, bf16[64,1024]{1,0:T(8,128)(2,1)S(1)}, u32[]{:S(2)}, u32[]{:S(2)}) %collective-permute-start.10) | collective-permute-done | bytes 131104 | tf_op jit(solution)/shard_map/ppermute | solution.py:87
  34.4 0.7 collective-permute-start.12
  35.1 1.3 %collective-permute-start.13 = (bf16[64,1024]{1,0:T(8,128)(2,1)S(1)}, bf16[64,1024]{1,0:T(8,128)(2,1)S(1)}, u32[]{:S(2)}, u32[]{:S(2)}) collective-permute-start(bf16[64,1024]{1,0:T(8,128)(2,1)S(1)} %get-tuple-element.84.refs_0_), channel_id=1, source_target_pairs={{4,28},{5,29},{6,30},{7,31},{8,24},{9,25},{10,26},{11,27}} | collective-permute-start | bytes 393224 | tf_op jit(solution)/shard_map/ppermute | solution.py:87
  36.4 1.3 %collective-permute-start.14 = (bf16[64,1024]{1,0:T(8,128)(2,1)S(1)}, bf16[64,1024]{1,0:T(8,128)(2,1)S(1)}, u32[]{:S(2)}, u32[]{:S(2)}) collective-permute-start(bf16[64,1024]{1,0:T(8,128)(2,1)S(1)} %get-tuple-element.84.refs_0_), channel_id=1, source_target_pairs={{4,12},{5,13},{6,14},{7,15},{8,0},{9,1},{10,2},{11,3}} | collective-permute-start | bytes 393224 | tf_op jit(solution)/shard_map/ppermute | solution.py:87
  37.7 1.3 %collective-permute-start.15 = (bf16[64,1024]{1,0:T(8,128)(2,1)S(1)}, bf16[64,1024]{1,0:T(8,128)(2,1)S(1)}, u32[]{:S(2)}, u32[]{:S(2)}) collective-permute-start(bf16[64,1024]{1,0:T(8,128)(2,1)S(1)} %get-tuple-element.84.refs_0_), channel_id=1, source_target_pairs={{4,20},{5,21},{6,22},{7,23},{8,16},{9,17},{10,18},{11,19}} | collective-permute-start | bytes 393224 | tf_op jit(solution)/shard_map/ppermute | solution.py:87
  39.0 9.6 %all_gather.9.refs_5_.refs_0_ = bf16[256,1024]{1,0:T(8,128)(2,1)S(1)} all-gather(bf16[64,1024]{1,0:T(8,128)(2,1)S(1)} %get-tuple-element.77), channel_id=1, replica_groups=mesh['row'=8,'col'=4] {'col'}, dimensions={0}, use_global_device_ids=true | all-gather | bytes 655360 | tf_op jit(solution)/shard_map/all_gather | solution.py:377
  49.6 0.7 collective-permute-start.17
  50.3 1.3 %collective-permute-start.18 = (bf16[2,64,1024]{2,1,0:T(8,128)(2,1)S(1)}, bf16[2,64,1024]{2,1,0:T(8,128)(2,1)S(1)}, u32[]{:S(2)}, u32[]{:S(2)}) collective-permute-start(bf16[2,64,1024]{2,1,0:T(8,128)(2,1)S(1)} %get-tuple-element.92), channel_id=1, source_target_pairs={{28,12},{29,13},{30,14},{31,15},{24,8},{25,9},{26,10},{27,11},{20,... | collective-permute-start | bytes 786440 | tf_op jit(solution)/shard_map/ppermute | solution.py:87
  51.6 0.7 collective-permute-start.19
  52.3 1.9 %collective-permute-done.16 = bf16[64,1024]{1,0:T(8,128)(2,1)S(1)} collective-permute-done((bf16[64,1024]{1,0:T(8,128)(2,1)S(1)}, bf16[64,1024]{1,0:T(8,128)(2,1)S(1)}, u32[]{:S(2)}, u32[]{:S(2)}) %collective-permute-start.16) | collective-permute-done | bytes 131104 | tf_op jit(solution)/shard_map/ppermute | solution.py:87
  54.2 7.7 %all_gather.11.refs_6_.refs_2_ = bf16[256,1024]{1,0:T(8,128)(2,1)S(1)} all-gather(bf16[64,1024]{1,0:T(8,128)(2,1)S(1)} %collective-permute-done.16), channel_id=1, replica_groups=mesh['row'=8,'col'=4] {'col'}, dimensions={0}, use_global_device_ids=true | all-gather | bytes 655360 | tf_op jit(solution)/shard_map/all_gather | solution.py:447
  61.9 7.3 %all_gather.10.refs_5_.refs_1_ = bf16[256,1024]{1,0:T(8,128)(2,1)S(1)} all-gather(bf16[64,1024]{1,0:T(8,128)(2,1)S(1)} %get-tuple-element.88), channel_id=1, replica_groups=mesh['row'=8,'col'=4] {'col'}, dimensions={0}, use_global_device_ids=true | all-gather | bytes 655360 | tf_op jit(solution)/shard_map/all_gather | solution.py:445
  69.5 11.1 %collective-permute-start.23 = (bf16[64,1024]{1,0:T(8,128)(2,1)S(1)}, bf16[64,1024]{1,0:T(8,128)(2,1)S(1)}, u32[]{:S(2)}, u32[]{:S(2)}) collective-permute-start(bf16[64,1024]{1,0:T(8,128)(2,1)S(1)} %get-tuple-element.104), channel_id=1, source_target_pairs={{0,4},{1,5},{2,6},{3,7},{4,0},{5,1},{6,2},{7,3},{8,12},{9,13},{10,... | collective-permute-start | bytes 393224 | tf_op jit(solution)/shard_map/ppermute | solution.py:87
  81.4 1.3 %collective-permute-start.21 = (bf16[64,1024]{1,0:T(8,128)(2,1)S(1)}, bf16[64,1024]{1,0:T(8,128)(2,1)S(1)}, u32[]{:S(2)}, u32[]{:S(2)}) collective-permute-start(bf16[64,1024]{1,0:T(8,128)(2,1)S(1)} %get-tuple-element.101), channel_id=1, source_target_pairs={{4,6},{5,7},{8,10},{9,11},{12,14},{13,15},{16,18},{17,19},{20,22},... | collective-permute-start | bytes 393224 | tf_op jit(solution)/shard_map/ppermute | solution.py:87
  82.7 1.3 %collective-permute-start.22 = (bf16[64,1024]{1,0:T(8,128)(2,1)S(1)}, bf16[64,1024]{1,0:T(8,128)(2,1)S(1)}, u32[]{:S(2)}, u32[]{:S(2)}) collective-permute-start(bf16[64,1024]{1,0:T(8,128)(2,1)S(1)} %get-tuple-element.102), channel_id=1, source_target_pairs={{4,7},{5,4},{8,11},{9,8},{12,15},{13,12},{16,19},{17,16},{20,23},{... | collective-permute-start | bytes 393224 | tf_op jit(solution)/shard_map/ppermute | solution.py:87
  84.0 1.8 %shard_map.88 = (bf16[3072,256]{1,0:T(8,128)(2,1)}, f32[64,1024]{1,0:T(8,128)S(1)}, f32[8,128]{1,0:T(8,128)}) custom-call(bf16[256,1024]{1,0:T(8,128)(2,1)S(1)} %all_gather.9.refs_5_.refs_0_, bf16[256,1024]{1,0:T(8,128)(2,1)S(1)} %all_gather.10.refs_5_.refs_1_, bf16[256,1024]{1,0:T(8,128)(2,1)S(1)} %all_gather.11.refs_6_.refs_2_, ...), custom_call_target="tpu_custom_call" | custom-call | tf_op jit(solution)/shard_map/pallas_call | solution.py:52
  85.9 0.7 maximum_bitcast_fusion
  86.6 2.4 %collective-permute-done.21 = bf16[64,1024]{1,0:T(8,128)(2,1)S(1)} collective-permute-done((bf16[64,1024]{1,0:T(8,128)(2,1)S(1)}, bf16[64,1024]{1,0:T(8,128)(2,1)S(1)}, u32[]{:S(2)}, u32[]{:S(2)}) %collective-permute-start.21) | collective-permute-done | bytes 131104 | tf_op jit(solution)/shard_map/ppermute | solution.py:87
  89.0 2.9 %collective-permute-done.22 = bf16[64,1024]{1,0:T(8,128)(2,1)S(1)} collective-permute-done((bf16[64,1024]{1,0:T(8,128)(2,1)S(1)}, bf16[64,1024]{1,0:T(8,128)(2,1)S(1)}, u32[]{:S(2)}, u32[]{:S(2)}) %collective-permute-start.22) | collective-permute-done | bytes 131104 | tf_op jit(solution)/shard_map/ppermute | solution.py:87
  91.9 0.8 subtract_bitcast_fusion
  (51 shorter events, 6.6 us)
Async XLA Ops:
  0.6 9.9 %copy-start.2 = (bf16[1024,1024]{1,0:T(8,128)(2,1)S(1)}, bf16[1024,1024]{1,0:T(8,128)(2,1)}, u32[]{:S(2)}) copy-start(bf16[1024,1024]{1,0:T(8,128)(2,1)} %refs_5_.1) | copy-start | bytes 6291460
  0.7 9.8 %collective-permute-start = (bf16[256,1024]{1,0:T(8,128)(2,1)}, bf16[256,1024]{1,0:T(8,128)(2,1)S(1)}, u32[]{:S(2)}, u32[]{:S(2)}) collective-permute-start(bf16[256,1024]{1,0:T(8,128)(2,1)} %get-tuple-element.55), channel_id=1, source_target_pairs={{0,4},{31,26},{30,20}} | collective-permute-start | bytes 1572872 | tf_op jit(solution)/shard_map/ppermute | solution.py:87
  1.5 7.2 %collective-permute-start.1 = (bf16[64,1024]{1,0:T(8,128)(2,1)}, bf16[64,1024]{1,0:T(8,128)(2,1)S(1)}, u32[]{:S(2)}, u32[]{:S(2)}) collective-permute-start(bf16[64,1024]{1,0:T(8,128)(2,1)} %get-tuple-element.56.refs_0_), channel_id=1, source_target_pairs={{0,12},{1,13},{2,14},{3,15}} | collective-permute-start | bytes 393224 | tf_op jit(solution)/shard_map/ppermute | solution.py:87
  2.2 6.5 %collective-permute-start.2 = (bf16[64,1024]{1,0:T(8,128)(2,1)}, bf16[64,1024]{1,0:T(8,128)(2,1)S(1)}, u32[]{:S(2)}, u32[]{:S(2)}) collective-permute-start(bf16[64,1024]{1,0:T(8,128)(2,1)} %get-tuple-element.56.refs_0_), channel_id=1, source_target_pairs={{0,16},{1,17},{2,18},{3,19}} | collective-permute-start | bytes 393224 | tf_op jit(solution)/shard_map/ppermute | solution.py:87
  2.9 5.9 %collective-permute-start.3 = (bf16[64,1024]{1,0:T(8,128)(2,1)}, bf16[64,1024]{1,0:T(8,128)(2,1)S(1)}, u32[]{:S(2)}, u32[]{:S(2)}) collective-permute-start(bf16[64,1024]{1,0:T(8,128)(2,1)} %get-tuple-element.56.refs_0_), channel_id=1, source_target_pairs={{0,24},{1,25},{2,26},{3,27}} | collective-permute-start | bytes 393224 | tf_op jit(solution)/shard_map/ppermute | solution.py:87
  3.6 9.8 %collective-permute-start.6 = (bf16[256,1024]{1,0:T(8,128)(2,1)}, bf16[256,1024]{1,0:T(8,128)(2,1)S(1)}, u32[]{:S(2)}, u32[]{:S(2)}) collective-permute-start(bf16[256,1024]{1,0:T(8,128)(2,1)} %get-tuple-element.55), channel_id=1, source_target_pairs={{0,8},{31,24},{30,22}} | collective-permute-start | bytes 1572872 | tf_op jit(solution)/shard_map/ppermute | solution.py:87
  4.3 2.2 %copy-start = (bf16[1024,2048]{1,0:T(8,128)(2,1)S(1)}, bf16[1024,2048]{1,0:T(8,128)(2,1)}, u32[]{:S(2)}) copy-start(bf16[1024,2048]{1,0:T(8,128)(2,1)} %refs_3_.8) | copy-start | bytes 12582916
  6.5 1.2 %copy-start.5 = (f32[256,1024]{1,0:T(8,128)S(1)}, f32[256,1024]{1,0:T(8,128)}, u32[]{:S(2)}) copy-start(f32[256,1024]{1,0:T(8,128)} %get-tuple-element.57.refs_0_) | copy-start | bytes 3145732
  7.7 2.8 %copy-start.1 = (bf16[1024,2048]{1,0:T(8,128)(2,1)S(1)}, bf16[1024,2048]{1,0:T(8,128)(2,1)}, u32[]{:S(2)}) copy-start(bf16[1024,2048]{1,0:T(8,128)(2,1)} %refs_3_.8) | copy-start | bytes 12582916
  7.7 2.9 %copy-start.3 = (bf16[1024,256]{1,0:T(8,128)(2,1)S(1)}, bf16[1024,256]{1,0:T(8,128)(2,1)}, u32[]{:S(2)}) copy-start(bf16[1024,256]{1,0:T(8,128)(2,1)} %refs_3_.9) | copy-start | bytes 1572868
  7.7 2.9 %copy-start.4 = (bf16[1024,256]{1,0:T(8,128)(2,1)S(1)}, bf16[1024,256]{1,0:T(8,128)(2,1)}, u32[]{:S(2)}) copy-start(bf16[1024,256]{1,0:T(8,128)(2,1)} %refs_6_.1) | copy-start | bytes 1572868
  8.8 1.7 %copy-start.6 = (bf16[64,1024]{1,0:T(8,128)(2,1)S(1)}, bf16[64,1024]{1,0:T(8,128)(2,1)}, u32[]{:S(2)}) copy-start(bf16[64,1024]{1,0:T(8,128)(2,1)} %get-tuple-element.56.refs_0_) | copy-start | bytes 393220
  10.7 7.6 %collective-permute-start.4 = (bf16[256,1024]{1,0:T(8,128)(2,1)S(1)}, bf16[256,1024]{1,0:T(8,128)(2,1)S(1)}, u32[]{:S(2)}, u32[]{:S(2)}) collective-permute-start(bf16[256,1024]{1,0:T(8,128)(2,1)S(1)} %get-tuple-element.60), channel_id=1, source_target_pairs={{4,8},{26,22}} | collective-permute-start | bytes 1572872 | tf_op jit(solution)/shard_map/ppermute | solution.py:87
  11.4 22.9 %collective-permute-start.5 = (bf16[256,1024]{1,0:T(8,128)(2,1)S(1)}, bf16[256,1024]{1,0:T(8,128)(2,1)S(1)}, u32[]{:S(2)}, u32[]{:S(2)}) collective-permute-start(bf16[256,1024]{1,0:T(8,128)(2,1)S(1)} %get-tuple-element.60), channel_id=1, source_target_pairs={{26,20}} | collective-permute-start | bytes 1572872 | tf_op jit(solution)/shard_map/ppermute | solution.py:87
  12.1 5.9 %collective-permute-start.7 = (bf16[64,1024]{1,0:T(8,128)(2,1)S(1)}, bf16[64,1024]{1,0:T(8,128)(2,1)S(1)}, u32[]{:S(2)}, u32[]{:S(2)}) collective-permute-start(bf16[64,1024]{1,0:T(8,128)(2,1)S(1)} %get-tuple-element.61.refs_0_), channel_id=1, source_target_pairs={{0,4},{1,5},{2,6},{3,7},{12,8},{13,9},{14,10},{15,11},{16,20},{17,... | collective-permute-start | bytes 393224 | tf_op jit(solution)/shard_map/ppermute | solution.py:87
  18.4 15.5 %collective-permute-start.10 = (bf16[64,1024]{1,0:T(8,128)(2,1)S(1)}, bf16[64,1024]{1,0:T(8,128)(2,1)S(1)}, u32[]{:S(2)}, u32[]{:S(2)}) collective-permute-start(bf16[64,1024]{1,0:T(8,128)(2,1)S(1)} %get-tuple-element.74), channel_id=1, source_target_pairs={{4,7},{8,11}} | collective-permute-start | bytes 393224 | tf_op jit(solution)/shard_map/ppermute | solution.py:87
  19.7 14.2 %collective-permute-start.8 = (bf16[64,1024]{1,0:T(8,128)(2,1)S(1)}, bf16[64,1024]{1,0:T(8,128)(2,1)S(1)}, u32[]{:S(2)}, u32[]{:S(2)}) collective-permute-start(bf16[64,1024]{1,0:T(8,128)(2,1)S(1)} %get-tuple-element.72), channel_id=1, source_target_pairs={{4,5},{8,9}} | collective-permute-start | bytes 393224 | tf_op jit(solution)/shard_map/ppermute | solution.py:87
  20.4 13.5 %collective-permute-start.9 = (bf16[64,1024]{1,0:T(8,128)(2,1)S(1)}, bf16[64,1024]{1,0:T(8,128)(2,1)S(1)}, u32[]{:S(2)}, u32[]{:S(2)}) collective-permute-start(bf16[64,1024]{1,0:T(8,128)(2,1)S(1)} %get-tuple-element.73), channel_id=1, source_target_pairs={{4,6},{8,10}} | collective-permute-start | bytes 393224 | tf_op jit(solution)/shard_map/ppermute | solution.py:87
  21.1 28.2 %collective-permute-start.11 = (bf16[256,1024]{1,0:T(8,128)(2,1)S(1)}, bf16[256,1024]{1,0:T(8,128)(2,1)S(1)}, u32[]{:S(2)}, u32[]{:S(2)}) collective-permute-start(bf16[256,1024]{1,0:T(8,128)(2,1)S(1)} %get-tuple-element.65.refs_0_), channel_id=1, source_target_pairs={{26,27},{24,25}} | collective-permute-start | bytes 1572872 | tf_op jit(solution)/shard_map/ppermute | solution.py:87
  34.4 14.9 %collective-permute-start.12 = (bf16[256,1024]{1,0:T(8,128)(2,1)S(1)}, bf16[256,1024]{1,0:T(8,128)(2,1)S(1)}, u32[]{:S(2)}, u32[]{:S(2)}) collective-permute-start(bf16[256,1024]{1,0:T(8,128)(2,1)S(1)} %get-tuple-element.78.refs_2_), channel_id=1, source_target_pairs={{22,23},{20,21}} | collective-permute-start | bytes 1572872 | tf_op jit(solution)/shard_map/ppermute | solution.py:87
  35.1 13.5 %collective-permute-start.13 = (bf16[64,1024]{1,0:T(8,128)(2,1)S(1)}, bf16[64,1024]{1,0:T(8,128)(2,1)S(1)}, u32[]{:S(2)}, u32[]{:S(2)}) collective-permute-start(bf16[64,1024]{1,0:T(8,128)(2,1)S(1)} %get-tuple-element.84.refs_0_), channel_id=1, source_target_pairs={{4,28},{5,29},{6,30},{7,31},{8,24},{9,25},{10,26},{11,27}} | collective-permute-start | bytes 393224 | tf_op jit(solution)/shard_map/ppermute | solution.py:87
  36.4 12.2 %collective-permute-start.14 = (bf16[64,1024]{1,0:T(8,128)(2,1)S(1)}, bf16[64,1024]{1,0:T(8,128)(2,1)S(1)}, u32[]{:S(2)}, u32[]{:S(2)}) collective-permute-start(bf16[64,1024]{1,0:T(8,128)(2,1)S(1)} %get-tuple-element.84.refs_0_), channel_id=1, source_target_pairs={{4,12},{5,13},{6,14},{7,15},{8,0},{9,1},{10,2},{11,3}} | collective-permute-start | bytes 393224 | tf_op jit(solution)/shard_map/ppermute | solution.py:87
  37.7 10.9 %collective-permute-start.15 = (bf16[64,1024]{1,0:T(8,128)(2,1)S(1)}, bf16[64,1024]{1,0:T(8,128)(2,1)S(1)}, u32[]{:S(2)}, u32[]{:S(2)}) collective-permute-start(bf16[64,1024]{1,0:T(8,128)(2,1)S(1)} %get-tuple-element.84.refs_0_), channel_id=1, source_target_pairs={{4,20},{5,21},{6,22},{7,23},{8,16},{9,17},{10,18},{11,19}} | collective-permute-start | bytes 393224 | tf_op jit(solution)/shard_map/ppermute | solution.py:87
  49.2 5.0 %collective-permute-start.16 = (bf16[64,1024]{1,0:T(8,128)(2,1)S(1)}, bf16[64,1024]{1,0:T(8,128)(2,1)S(1)}, u32[]{:S(2)}, u32[]{:S(2)}) collective-permute-start(bf16[64,1024]{1,0:T(8,128)(2,1)S(1)} %get-tuple-element.89), channel_id=1, source_target_pairs={{0,4},{1,5},{2,6},{3,7},{4,0},{5,1},{6,2},{7,3},{8,12},{9,13},{10,... | collective-permute-start | bytes 393224 | tf_op jit(solution)/shard_map/ppermute | solution.py:87
  49.6 19.5 %collective-permute-start.17 = (bf16[2,64,1024]{2,1,0:T(8,128)(2,1)S(1)}, bf16[2,64,1024]{2,1,0:T(8,128)(2,1)S(1)}, u32[]{:S(2)}, u32[]{:S(2)}) collective-permute-start(bf16[2,64,1024]{2,1,0:T(8,128)(2,1)S(1)} %get-tuple-element.91), channel_id=1, source_target_pairs={{28,4},{29,5},{30,6},{31,7},{24,0},{25,1},{26,2},{27,3},{20,28},{2... | collective-permute-start | bytes 786440 | tf_op jit(solution)/shard_map/ppermute | solution.py:87
  50.3 18.9 %collective-permute-start.18 = (bf16[2,64,1024]{2,1,0:T(8,128)(2,1)S(1)}, bf16[2,64,1024]{2,1,0:T(8,128)(2,1)S(1)}, u32[]{:S(2)}, u32[]{:S(2)}) collective-permute-start(bf16[2,64,1024]{2,1,0:T(8,128)(2,1)S(1)} %get-tuple-element.92), channel_id=1, source_target_pairs={{28,12},{29,13},{30,14},{31,15},{24,8},{25,9},{26,10},{27,11},{20,... | collective-permute-start | bytes 786440 | tf_op jit(solution)/shard_map/ppermute | solution.py:87
  51.6 17.6 %collective-permute-start.19 = (bf16[2,64,1024]{2,1,0:T(8,128)(2,1)S(1)}, bf16[2,64,1024]{2,1,0:T(8,128)(2,1)S(1)}, u32[]{:S(2)}, u32[]{:S(2)}) collective-permute-start(bf16[2,64,1024]{2,1,0:T(8,128)(2,1)S(1)} %get-tuple-element.93), channel_id=1, source_target_pairs={{28,20},{29,21},{30,22},{31,23},{24,16},{25,17},{26,18},{27,19},{2... | collective-permute-start | bytes 786440 | tf_op jit(solution)/shard_map/ppermute | solution.py:87
  69.5 16.3 %collective-permute-start.23 = (bf16[64,1024]{1,0:T(8,128)(2,1)S(1)}, bf16[64,1024]{1,0:T(8,128)(2,1)S(1)}, u32[]{:S(2)}, u32[]{:S(2)}) collective-permute-start(bf16[64,1024]{1,0:T(8,128)(2,1)S(1)} %get-tuple-element.104), channel_id=1, source_target_pairs={{0,4},{1,5},{2,6},{3,7},{4,0},{5,1},{6,2},{7,3},{8,12},{9,13},{10,... | collective-permute-start | bytes 393224 | tf_op jit(solution)/shard_map/ppermute | solution.py:87
  80.7 5.9 %collective-permute-start.20 = (bf16[64,1024]{1,0:T(8,128)(2,1)S(1)}, bf16[64,1024]{1,0:T(8,128)(2,1)S(1)}, u32[]{:S(2)}, u32[]{:S(2)}) collective-permute-start(bf16[64,1024]{1,0:T(8,128)(2,1)S(1)} %get-tuple-element.100), channel_id=1, source_target_pairs={{4,5},{5,6},{8,9},{9,10},{12,13},{13,14},{16,17},{17,18},{20,21},{... | collective-permute-start | bytes 393224 | tf_op jit(solution)/shard_map/ppermute | solution.py:87
  81.4 7.6 %collective-permute-start.21 = (bf16[64,1024]{1,0:T(8,128)(2,1)S(1)}, bf16[64,1024]{1,0:T(8,128)(2,1)S(1)}, u32[]{:S(2)}, u32[]{:S(2)}) collective-permute-start(bf16[64,1024]{1,0:T(8,128)(2,1)S(1)} %get-tuple-element.101), channel_id=1, source_target_pairs={{4,6},{5,7},{8,10},{9,11},{12,14},{13,15},{16,18},{17,19},{20,22},... | collective-permute-start | bytes 393224 | tf_op jit(solution)/shard_map/ppermute | solution.py:87
  82.7 9.2 %collective-permute-start.22 = (bf16[64,1024]{1,0:T(8,128)(2,1)S(1)}, bf16[64,1024]{1,0:T(8,128)(2,1)S(1)}, u32[]{:S(2)}, u32[]{:S(2)}) collective-permute-start(bf16[64,1024]{1,0:T(8,128)(2,1)S(1)} %get-tuple-element.102), channel_id=1, source_target_pairs={{4,7},{5,4},{8,11},{9,8},{12,15},{13,12},{16,19},{17,16},{20,23},{... | collective-permute-start | bytes 393224 | tf_op jit(solution)/shard_map/ppermute | solution.py:87

commit v2 on v1

--- a/solution.py
+++ b/solution.py
@@ -303,13 +303,6 @@
 
     t6_odd = send(t6_even, within_chip(last - 1, g5))
 
-    def is_entry(r, c):
-        return ((r % 2 == 0) & (r != 2)) | (r == 3)
-
-    y0_mine, tok = route(
-        [(is_entry, y0_in), (lambda r, c: jnp.logical_not(is_entry(r, c)), y0_out)], (share, NB), [tok]
-    )
-
     def kernel2(p0, p1, fac, inv, rh, *rest):
         outs, (dbuf, lbuf, rbuf, abuf, bbuf, xbuf, sems) = rest[cols : 2 * cols], rest[2 * cols :]
         r, c = place()
@@ -338,41 +331,23 @@
     )
     dealt = [send(parts[s], [((1, g0), (1, (g0 + s) % cols)), ((2, g1), (2, (g1 + s) % cols))]) for s in range(1, cols)]
 
+    def is_entry(r, c):
+        return ((r % 2 == 0) & (r != 2)) | (r == 3)
+
+    y0_mine, tok = route(
+        [(is_entry, y0_in), (lambda r, c: jnp.logical_not(is_entry(r, c)), y0_out)], (share, NB), [tok]
+    )
+
     cases = [(at(1, g0), parts[0]), (at(2, g1), parts[0])]
     for s in range(1, cols):
         cases += [(at(1, (g0 + s) % cols), dealt[s - 1]), (at(2, (g1 + s) % cols), dealt[s - 1])]
-    y_own, tok = route(cases, (share, NB), order=[tok])
+    y_own, y0_mine, tok = route(cases, (share, NB), order=[tok], through=[y0_mine])
     to_odd = [pairs - 1] + [d for d in range(1, pairs - 1)]
     to_even = [pairs - 1, 0] + [d for d in range(2, pairs - 1)]
     y_z = [
         send(y_own, [((1, b), (2 * d + 1, b)) for b in all_cols] + [((2, b), (2 * e, b)) for b in all_cols])
         for d, e in zip(to_odd, to_even)
     ]
-
-    def kernelt(*refs):
-        n = len(evens5) + 1
-        first, second, (_, out, _, abuf, bbuf, sems) = refs[:n], refs[n : 2 * n], refs[2 * n :]
-        r, c = place()
-        cp = Copies(sems)
-        for col, x, q in zip([g5] + evens5, first, second):
-            cp.branch()
-
-            @pl.when((r == last - 2) & (c == col))
-            def _(x=x, q=q):
-                wait([cp.start(x, abuf), cp.start(q, bbuf)])
-                abuf[...] = (abuf[...].astype(F32) + bbuf[...].astype(F32)).astype(BF16)
-                cp.start(abuf, out).wait()
-
-    t5_even, y0_mine, tok = call(
-        kernelt,
-        [a3] + a4 + [a2] + q75_parts + [y0_mine],
-        [(full, BF16), ((share, NB), BF16)],
-        [(full, BF16), (full, BF16)],
-        3,
-        aliases={2 * len(evens5) + 2: 1},
-        order=[tok],
-    )
-    t5_odd = send(t5_even, within_chip(last - 2, g5))
 
     y0_all = lax.all_gather(y0_mine, "col", axis=0, tiled=True)
     cases = [(lambda r, c: (r == 1) | (r == 2), y_own)]
@@ -381,6 +356,33 @@
     y_mine, y_near, tok = route(cases, (share, NB), order=[tok, y0_all], times=2)
     all_swap = [((a, b), (a ^ 1, b)) for a in range(rows) for b in all_cols]
     y_other = send(y_mine, all_swap)
+
+    def kernelt(*refs):
+        n = len(evens5) + 1
+        first, second, (_, out, _, abuf, bbuf, sems) = refs[:n], refs[n : 2 * n], refs[2 * n :]
+        r, c = place()
+        cp = Copies(sems)
+        for col, x, q in zip([g5] + evens5, first, second):
+            cp.branch()
+
+            @pl.when((r == last - 2) & (c == col))
+            def _(x=x, q=q):
+                wait([cp.start(x, abuf), cp.start(q, bbuf)])
+                abuf[...] = (abuf[...].astype(F32) + bbuf[...].astype(F32)).astype(BF16)
+                cp.start(abuf, out).wait()
+
+    t5_even, y_near, tok = call(
+        kernelt,
+        [a3] + a4 + [a2] + q75_parts + [y_near],
+        [(full, BF16), ((share, NB), BF16)],
+        [(full, BF16), (full, BF16)],
+        3,
+        aliases={2 * len(evens5) + 2: 1},
+        order=[tok],
+    )
+    t5_odd = send(t5_even, within_chip(last - 2, g5))
+
+    near_all = lax.all_gather(y_near, "col", axis=0, tiled=True)
 
     i = last - 2
     slots = {d: d + 1 for d in range(pairs - 2)}
@@ -427,14 +429,14 @@
                 sbuf[...] = jnp.transpose(v)
                 wait(done + [cp.start(sbuf, sol_out)])
 
-    sol, *bq, y_near, tok = call(
+    sol, *bq, y_other, tok = call(
         kernel5,
-        [t6_even, t6_odd, t5_even, t5_odd, factor, diag_inv, forward_values, sol] + bq + [y_near],
+        [t6_even, t6_odd, t5_even, t5_odd, factor, diag_inv, forward_values, sol] + bq + [y_other],
         [(tall, F32)] + [(pair_piece, BF16)] * pairs + [((share, NB), BF16)],
         [(square, BF16), ((cb, NB, NB), BF16), (tall, BF16), (full, BF16), ((pairs, 2, piece, NB), BF16), (tall, F32)],
         4 + cb + pairs,
         aliases={7 + k: k for k in range(pairs + 2)},
-        order=[tok],
+        order=[tok, near_all],
     )
     scattered = []
     for t in range(pairs - 1):
@@ -442,8 +444,6 @@
         pairs_t = [((last, b), (2 * t + 1, b)) for b in all_cols] + [((last - 1, b), (2 * t, b)) for b in all_cols]
         scattered.append(send(bq[t], pairs_t + [((i, b), (lands(to), b)) for b in all_cols]))
 
-    near_all = lax.all_gather(y_near, "col", axis=0, tiled=True)
-
     far_all = lax.all_gather(y_other, "col", axis=0, tiled=True)
 
     def load_by_parity(even, odd, buf, sem):
@@ -455,50 +455,6 @@
                 pltpu.make_async_copy(ref, buf, sem).start()
 
         return pltpu.make_async_copy(even, buf, sem)
-
-    def kernelb(own_q, *rest):
-        got, (own_out, part_out, bbuf, fbuf, obuf, pbuf, sems) = rest[: pairs - 1], rest[pairs - 1 :]
-        r, _ = place()
-        cp = Copies(sems)
-        pair = r // 2
-        refs = list(got) + [own_q]
-        for d in range(pairs):
-            cp.branch()
-
-            @pl.when(pair == d)
-            def _(d=d):
-                cp.start(refs[d], bbuf).wait()
-
-            @pl.when(r == lands(d))
-            def _(d=d):
-                cp.start(refs[slots[d]], fbuf).wait()
-
-        cp.branch()
-
-        takes = functools.reduce(jnp.logical_or, [r == lands(d) for d in range(pairs)])
-        for y in (0, 1):
-            for more in (False, True):
-
-                @pl.when((lax.rem(r, 2) == y) & (takes if more else jnp.logical_not(takes)))
-                def _(y=y, more=more):
-                    ours, theirs = bbuf[y].astype(F32), bbuf[1 - y].astype(F32)
-                    if more:
-                        ours = ours + fbuf[y].astype(F32)
-                        theirs = theirs + fbuf[1 - y].astype(F32)
-                    obuf[...] = ours
-                    pbuf[...] = theirs.astype(BF16)
-
-        wait([cp.start(pbuf, part_out), cp.start(obuf, own_out)])
-
-    own, part, tok = call(
-        kernelb,
-        [bq[pairs - 1]] + scattered,
-        [((piece, NB), F32), ((piece, NB), BF16)],
-        [(pair_piece, BF16), (pair_piece, BF16), ((piece, NB), F32), ((piece, NB), BF16)],
-        2,
-        order=[tok, near_all, far_all],
-    )
-    theirs = send(part, all_swap)
 
     owners = sorted({g0, g1, g2})
 
@@ -541,6 +497,50 @@
         send(p_parts[s], [((a, g), (a, (g + s) % cols)) for a in range(1, rows) for g in owners]) for s in range(1, cols)
     ]
 
+    def kernelb(own_q, *rest):
+        got, (own_out, part_out, bbuf, fbuf, obuf, pbuf, sems) = rest[: pairs - 1], rest[pairs - 1 :]
+        r, _ = place()
+        cp = Copies(sems)
+        pair = r // 2
+        refs = list(got) + [own_q]
+        for d in range(pairs):
+            cp.branch()
+
+            @pl.when(pair == d)
+            def _(d=d):
+                cp.start(refs[d], bbuf).wait()
+
+            @pl.when(r == lands(d))
+            def _(d=d):
+                cp.start(refs[slots[d]], fbuf).wait()
+
+        cp.branch()
+
+        takes = functools.reduce(jnp.logical_or, [r == lands(d) for d in range(pairs)])
+        for y in (0, 1):
+            for more in (False, True):
+
+                @pl.when((lax.rem(r, 2) == y) & (takes if more else jnp.logical_not(takes)))
+                def _(y=y, more=more):
+                    ours, theirs = bbuf[y].astype(F32), bbuf[1 - y].astype(F32)
+                    if more:
+                        ours = ours + fbuf[y].astype(F32)
+                        theirs = theirs + fbuf[1 - y].astype(F32)
+                    obuf[...] = ours
+                    pbuf[...] = theirs.astype(BF16)
+
+        wait([cp.start(pbuf, part_out), cp.start(obuf, own_out)])
+
+    own, part, tok = call(
+        kernelb,
+        [bq[pairs - 1]] + scattered,
+        [((piece, NB), F32), ((piece, NB), BF16)],
+        [(pair_piece, BF16), (pair_piece, BF16), ((piece, NB), F32), ((piece, NB), BF16)],
+        2,
+        order=[tok],
+    )
+    theirs = send(part, all_swap)
+
     def kernelo(y0, near, far, rh, own_p, fs_out, side_out, abuf, tbuf, rbuf, pbuf, obuf, sems):
         _, c = place()
         cp = Copies(sems)

time: 93.2 us -> 88.8 us (0.953)
  the two profiles are of different devices: /device:TPU:11 before, /device:TPU:12 now
where the time goes in v2:
time: 88.8 us; the launch traced here: 88.3 us
  starting transfers between devices  29.9 us (34%)
  waiting for transfers between devices  22.1 us (25%)
  blocking collectives  21.3 us (24%)
  Pallas kernels  8.09 us (9%)
  local copies, waits for them, and re-layouts  4.35 us (5%)
  other arithmetic  1.52 us (2%)
  between operations  1.11 us (1%)
    ppermute x24, starting transfers between devices, send(): lax.ppermute(x, BOTH, [(a * cols + b, d * cols + e) for (a, b), (d, e) in...  29.9 us
    ppermute x24, waiting for transfers between devices, send(): lax.ppermute(x, BOTH, [(a * cols + b, d * cols + e) for (a, b), (d, e) in...  22.1 us
    pallas_call x14, Pallas kernels, call(): pl.pallas_call(body, out_shape=[jax.ShapeDtypeStruct(s, d) for s, d in ou...  8.09 us
    all_gather x1, blocking collectives, local(): far_all = lax.all_gather(y_other, 'col', axis=0, tiled=True)  7.29 us
    all_gather x1, blocking collectives, local(): near_all = lax.all_gather(y_near, 'col', axis=0, tiled=True)  7 us
    all_gather x1, blocking collectives, local(): y0_all = lax.all_gather(y0_mine, 'col', axis=0, tiled=True)  6.96 us
    unnamed x14, local copies, waits for them, and re-layouts  4.33 us
  transfers between devices with their start and end apart: 24, of which 5 were waited for; matrix products, arithmetic and copies ran while one was open for 1% of the time, Pallas kernels for 9%

profile of v2, /device:TPU:12, one launch (start us, length us, event | category | flops | bytes accessed | tf_op | source)
XLA Modules:
  0.0 88.3 jit_solution(7743868459343249249)
XLA Ops:
  0.7 0.8 collective-permute-start
  2.9 1.3 %collective-permute-start.2 = (bf16[64,1024]{1,0:T(8,128)(2,1)}, bf16[64,1024]{1,0:T(8,128)(2,1)S(1)}, u32[]{:S(2)}, u32[]{:S(2)}) collective-permute-start(bf16[64,1024]{1,0:T(8,128)(2,1)} %get-tuple-element.57.refs_0_), channel_id=1, source_target_pairs={{0,12},{1,13},{2,14},{3,15}} | collective-permute-start | bytes 393224 | tf_op jit(solution)/shard_map/ppermute | solution.py:87
  4.2 0.7 collective-permute-start.1
  4.9 2.2 %copy-done = bf16[1024,2048]{1,0:T(8,128)(2,1)S(1)} copy-done((bf16[1024,2048]{1,0:T(8,128)(2,1)S(1)}, bf16[1024,2048]{1,0:T(8,128)(2,1)}, u32[]{:S(2)}) %copy-start) | copy-done | bytes 4194328
  7.1 1.2 %copy-done.5 = f32[256,1024]{1,0:T(8,128)S(1)} copy-done((f32[256,1024]{1,0:T(8,128)S(1)}, f32[256,1024]{1,0:T(8,128)}, u32[]{:S(2)}) %copy-start.5) | copy-done | bytes 1048600
  8.3 1.0 %shard_map.76 = (f32[1024,256]{1,0:T(8,128)}, bf16[2,64,1024]{2,1,0:T(8,128)(2,1)S(1)}, bf16[2,64,1024]{2,1,0:T(8,128)(2,1)S(1)}, bf16[2,64,1024]{2,1,0:T(8,128)...) custom-call(f32[256,1024]{1,0:T(8,128)S(1)} %copy-done.5, bf16[1024,2048]{1,0:T(8,128)(2,1)S(1)} %copy-done), custom_call_target="tpu_custom_call" | custom-call | tf_op jit(solution)/shard_map/pallas_call | solution.py:52
  9.4 7.1 %collective-permute-done.2.refs_1_ = bf16[64,1024]{1,0:T(8,128)(2,1)S(1)} collective-permute-done((bf16[64,1024]{1,0:T(8,128)(2,1)}, bf16[64,1024]{1,0:T(8,128)(2,1)S(1)}, u32[]{:S(2)}, u32[]{:S(2)}) %collective-permute-start.2) | collective-permute-done | bytes 131104 | tf_op jit(solution)/shard_map/ppermute | solution.py:87
  16.5 0.9 %copy-done.6 = bf16[64,1024]{1,0:T(8,128)(2,1)S(1)} copy-done((bf16[64,1024]{1,0:T(8,128)(2,1)S(1)}, bf16[64,1024]{1,0:T(8,128)(2,1)}, u32[]{:S(2)}) %copy-start.6) | copy-done | bytes 131096
  17.9 0.7 collective-permute-start.5
  18.6 0.7 collective-permute-start.10
  19.3 1.3 %collective-permute-start.9 = (bf16[64,1024]{1,0:T(8,128)(2,1)S(1)}, bf16[64,1024]{1,0:T(8,128)(2,1)S(1)}, u32[]{:S(2)}, u32[]{:S(2)}) collective-permute-start(bf16[64,1024]{1,0:T(8,128)(2,1)S(1)} %get-tuple-element.73.refs_0_), channel_id=1, source_target_pairs={{0,4},{1,5},{2,6},{3,7},{12,8},{13,9},{14,10},{15,11},{16,20},{17,... | collective-permute-start | bytes 393224 | tf_op jit(solution)/shard_map/ppermute | solution.py:87
  22.8 3.1 %collective-permute-done.9.refs_1_ = bf16[64,1024]{1,0:T(8,128)(2,1)S(1)} collective-permute-done((bf16[64,1024]{1,0:T(8,128)(2,1)S(1)}, bf16[64,1024]{1,0:T(8,128)(2,1)S(1)}, u32[]{:S(2)}, u32[]{:S(2)}) %collective-permute-start.9) | collective-permute-done | bytes 131104 | tf_op jit(solution)/shard_map/ppermute | solution.py:87
  25.9 0.7 collective-permute-start.14
  27.7 1.3 %collective-permute-start.12 = (bf16[64,1024]{1,0:T(8,128)(2,1)S(1)}, bf16[64,1024]{1,0:T(8,128)(2,1)S(1)}, u32[]{:S(2)}, u32[]{:S(2)}) collective-permute-start(bf16[64,1024]{1,0:T(8,128)(2,1)S(1)} %get-tuple-element.78.refs_0_), channel_id=1, source_target_pairs={{4,12},{5,13},{6,14},{7,15},{8,0},{9,1},{10,2},{11,3}} | collective-permute-start | bytes 393224 | tf_op jit(solution)/shard_map/ppermute | solution.py:87
  29.7 7.0 %all_gather.9.refs_5_.refs_0_ = bf16[256,1024]{1,0:T(8,128)(2,1)S(1)} all-gather(bf16[64,1024]{1,0:T(8,128)(2,1)S(1)} %get-tuple-element.77), channel_id=1, replica_groups=mesh['row'=8,'col'=4] {'col'}, dimensions={0}, use_global_device_ids=true | all-gather | bytes 655360 | tf_op jit(solution)/shard_map/all_gather | solution.py:352
  36.7 1.2 %collective-permute-done.12.refs_2_ = bf16[64,1024]{1,0:T(8,128)(2,1)S(1)} collective-permute-done((bf16[64,1024]{1,0:T(8,128)(2,1)S(1)}, bf16[64,1024]{1,0:T(8,128)(2,1)S(1)}, u32[]{:S(2)}, u32[]{:S(2)}) %collective-permute-start.12) | collective-permute-done | bytes 131104 | tf_op jit(solution)/shard_map/ppermute | solution.py:87
  38.5 0.7 collective-permute-start.15
  39.2 9.2 %collective-permute-start.16 = (bf16[64,1024]{1,0:T(8,128)(2,1)S(1)}, bf16[64,1024]{1,0:T(8,128)(2,1)S(1)}, u32[]{:S(2)}, u32[]{:S(2)}) collective-permute-start(bf16[64,1024]{1,0:T(8,128)(2,1)S(1)} %get-tuple-element.89), channel_id=1, source_target_pairs={{0,4},{1,5},{2,6},{3,7},{4,0},{5,1},{6,2},{7,3},{8,12},{9,13},{10,... | collective-permute-start | bytes 393224 | tf_op jit(solution)/shard_map/ppermute | solution.py:87
  48.4 7.0 %all_gather.10.refs_14_.refs_1_ = bf16[256,1024]{1,0:T(8,128)(2,1)S(1)} all-gather(bf16[64,1024]{1,0:T(8,128)(2,1)S(1)} %get-tuple-element.82), channel_id=1, replica_groups=mesh['row'=8,'col'=4] {'col'}, dimensions={0}, use_global_device_ids=true | all-gather | bytes 655360 | tf_op jit(solution)/shard_map/all_gather | solution.py:385
  55.7 0.7 collective-permute-start.17
  56.4 1.3 %collective-permute-start.18 = (bf16[2,64,1024]{2,1,0:T(8,128)(2,1)S(1)}, bf16[2,64,1024]{2,1,0:T(8,128)(2,1)S(1)}, u32[]{:S(2)}, u32[]{:S(2)}) collective-permute-start(bf16[2,64,1024]{2,1,0:T(8,128)(2,1)S(1)} %get-tuple-element.96), channel_id=1, source_target_pairs={{28,12},{29,13},{30,14},{31,15},{24,8},{25,9},{26,10},{27,11},{20,... | collective-permute-start | bytes 786440 | tf_op jit(solution)/shard_map/ppermute | solution.py:87
  57.7 1.3 %collective-permute-start.19 = (bf16[2,64,1024]{2,1,0:T(8,128)(2,1)S(1)}, bf16[2,64,1024]{2,1,0:T(8,128)(2,1)S(1)}, u32[]{:S(2)}, u32[]{:S(2)}) collective-permute-start(bf16[2,64,1024]{2,1,0:T(8,128)(2,1)S(1)} %get-tuple-element.97), channel_id=1, source_target_pairs={{28,20},{29,21},{30,22},{31,23},{24,16},{25,17},{26,18},{27,19},{2... | collective-permute-start | bytes 786440 | tf_op jit(solution)/shard_map/ppermute | solution.py:87
  59.0 7.3 %all_gather.11.refs_2_ = bf16[256,1024]{1,0:T(8,128)(2,1)S(1)} all-gather(bf16[64,1024]{1,0:T(8,128)(2,1)S(1)} %get-tuple-element.91), channel_id=1, replica_groups=mesh['row'=8,'col'=4] {'col'}, dimensions={0}, use_global_device_ids=true | all-gather | bytes 655360 | tf_op jit(solution)/shard_map/all_gather | solution.py:447
  66.3 2.9 %shard_map.86 = (bf16[64,1024]{1,0:T(8,128)(2,1)S(1)}, bf16[64,1024]{1,0:T(8,128)(2,1)S(1)}, bf16[64,1024]{1,0:T(8,128)(2,1)S(1)}, bf16[64,1024]{1,0:T(8,128)(2,1)S(1)}, f32[8,128]{1,0:T(8,128)S(1)}) custom-call(bf16[256,1024]{1,0:T(8,128)(2,1)S(1)} %all_gather.9.refs_5_.refs_0_, bf16[256,1024]{1,0:T(8,128)(2,1)S(1)} %all_gather.10.refs_14_.refs_1_, ...), custom_call_target="tpu_custom_call" | custom-call | tf_op jit(solution)/shard_map/pallas_call | solution.py:52
  69.2 1.3 %collective-permute-start.20 = (bf16[64,1024]{1,0:T(8,128)(2,1)S(1)}, bf16[64,1024]{1,0:T(8,128)(2,1)S(1)}, u32[]{:S(2)}, u32[]{:S(2)}) collective-permute-start(bf16[64,1024]{1,0:T(8,128)(2,1)S(1)} %get-tuple-element.102), channel_id=1, source_target_pairs={{4,5},{5,6},{8,9},{9,10},{12,13},{13,14},{16,17},{17,18},{20,21},{... | collective-permute-start | bytes 393224 | tf_op jit(solution)/shard_map/ppermute | solution.py:87
  70.5 1.3 %collective-permute-start.21 = (bf16[64,1024]{1,0:T(8,128)(2,1)S(1)}, bf16[64,1024]{1,0:T(8,128)(2,1)S(1)}, u32[]{:S(2)}, u32[]{:S(2)}) collective-permute-start(bf16[64,1024]{1,0:T(8,128)(2,1)S(1)} %get-tuple-element.103), channel_id=1, source_target_pairs={{4,6},{5,7},{8,10},{9,11},{12,14},{13,15},{16,18},{17,19},{20,22},... | collective-permute-start | bytes 393224 | tf_op jit(solution)/shard_map/ppermute | solution.py:87
  71.8 1.9 %collective-permute-start.22 = (bf16[64,1024]{1,0:T(8,128)(2,1)S(1)}, bf16[64,1024]{1,0:T(8,128)(2,1)S(1)}, u32[]{:S(2)}, u32[]{:S(2)}) collective-permute-start(bf16[64,1024]{1,0:T(8,128)(2,1)S(1)} %get-tuple-element.104), channel_id=1, source_target_pairs={{4,7},{5,4},{8,11},{9,8},{12,15},{13,12},{16,19},{17,16},{20,23},{... | collective-permute-start | bytes 393224 | tf_op jit(solution)/shard_map/ppermute | solution.py:87
  73.7 7.9 %collective-permute-done.19.refs_3_ = bf16[2,64,1024]{2,1,0:T(8,128)(2,1)S(1)} collective-permute-done((bf16[2,64,1024]{2,1,0:T(8,128)(2,1)S(1)}, bf16[2,64,1024]{2,1,0:T(8,128)(2,1)S(1)}, u32[]{:S(2)}, u32[]{:S(2)}) %collective-permute-start.19) | collective-permute-done | bytes 262176 | tf_op jit(solution)/shard_map/ppermute | solution.py:87
  82.0 1.8 %shard_map.88 = (bf16[3072,256]{1,0:T(8,128)(2,1)}, f32[64,1024]{1,0:T(8,128)S(1)}, f32[8,128]{1,0:T(8,128)}) custom-call(bf16[256,1024]{1,0:T(8,128)(2,1)S(1)} %all_gather.9.refs_5_.refs_0_, bf16[256,1024]{1,0:T(8,128)(2,1)S(1)} %all_gather.10.refs_14_.refs_1_, bf16[256,1024]{1,0:T(8,128)(2,1)S(1)} %all_gather.11.refs_2_, bf16[1024,256]{1,0:T(8,128)(2,1)S(1)} %copy-done.3, ...), custom_call_target="tpu_custom_call" | custom-call | tf_op jit(solution)/shard_map/pallas_call | solution.py:52
  83.9 0.8 subtract_bitcast_fusion
  84.7 2.8 %collective-permute-done.23 = bf16[64,1024]{1,0:T(8,128)(2,1)S(1)} collective-permute-done((bf16[64,1024]{1,0:T(8,128)(2,1)S(1)}, bf16[64,1024]{1,0:T(8,128)(2,1)S(1)}, u32[]{:S(2)}, u32[]{:S(2)}) %collective-permute-start.23) | collective-permute-done | bytes 131104 | tf_op jit(solution)/shard_map/ppermute | solution.py:87
  87.5 0.7 maximum_bitcast_fusion
  (51 shorter events, 7.2 us)
Async XLA Ops:
  0.6 17.1 %copy-start.2 = (bf16[1024,1024]{1,0:T(8,128)(2,1)S(1)}, bf16[1024,1024]{1,0:T(8,128)(2,1)}, u32[]{:S(2)}) copy-start(bf16[1024,1024]{1,0:T(8,128)(2,1)} %refs_5_.1) | copy-start | bytes 6291460
  0.7 17.0 %collective-permute-start = (bf16[256,1024]{1,0:T(8,128)(2,1)}, bf16[256,1024]{1,0:T(8,128)(2,1)S(1)}, u32[]{:S(2)}, u32[]{:S(2)}) collective-permute-start(bf16[256,1024]{1,0:T(8,128)(2,1)} %get-tuple-element.56), channel_id=1, source_target_pairs={{0,4},{31,26},{30,20}} | collective-permute-start | bytes 1572872 | tf_op jit(solution)/shard_map/ppermute | solution.py:87
  1.5 7.8 %collective-permute-start.4 = (bf16[64,1024]{1,0:T(8,128)(2,1)}, bf16[64,1024]{1,0:T(8,128)(2,1)S(1)}, u32[]{:S(2)}, u32[]{:S(2)}) collective-permute-start(bf16[64,1024]{1,0:T(8,128)(2,1)} %get-tuple-element.57.refs_0_), channel_id=1, source_target_pairs={{0,24},{1,25},{2,26},{3,27}} | collective-permute-start | bytes 393224 | tf_op jit(solution)/shard_map/ppermute | solution.py:87
  2.2 7.2 %collective-permute-start.3 = (bf16[64,1024]{1,0:T(8,128)(2,1)}, bf16[64,1024]{1,0:T(8,128)(2,1)S(1)}, u32[]{:S(2)}, u32[]{:S(2)}) collective-permute-start(bf16[64,1024]{1,0:T(8,128)(2,1)} %get-tuple-element.57.refs_0_), channel_id=1, source_target_pairs={{0,16},{1,17},{2,18},{3,19}} | collective-permute-start | bytes 393224 | tf_op jit(solution)/shard_map/ppermute | solution.py:87
  2.9 13.6 %collective-permute-start.2 = (bf16[64,1024]{1,0:T(8,128)(2,1)}, bf16[64,1024]{1,0:T(8,128)(2,1)S(1)}, u32[]{:S(2)}, u32[]{:S(2)}) collective-permute-start(bf16[64,1024]{1,0:T(8,128)(2,1)} %get-tuple-element.57.refs_0_), channel_id=1, source_target_pairs={{0,12},{1,13},{2,14},{3,15}} | collective-permute-start | bytes 393224 | tf_op jit(solution)/shard_map/ppermute | solution.py:87
  4.2 16.4 %collective-permute-start.1 = (bf16[256,1024]{1,0:T(8,128)(2,1)}, bf16[256,1024]{1,0:T(8,128)(2,1)S(1)}, u32[]{:S(2)}, u32[]{:S(2)}) collective-permute-start(bf16[256,1024]{1,0:T(8,128)(2,1)} %get-tuple-element.56), channel_id=1, source_target_pairs={{0,8},{31,24},{30,22}} | collective-permute-start | bytes 1572872 | tf_op jit(solution)/shard_map/ppermute | solution.py:87
  4.9 2.2 %copy-start = (bf16[1024,2048]{1,0:T(8,128)(2,1)S(1)}, bf16[1024,2048]{1,0:T(8,128)(2,1)}, u32[]{:S(2)}) copy-start(bf16[1024,2048]{1,0:T(8,128)(2,1)} %refs_3_.8) | copy-start | bytes 12582916
  7.1 1.2 %copy-start.5 = (f32[256,1024]{1,0:T(8,128)S(1)}, f32[256,1024]{1,0:T(8,128)}, u32[]{:S(2)}) copy-start(f32[256,1024]{1,0:T(8,128)} %get-tuple-element.58.refs_0_) | copy-start | bytes 3145732
  8.3 9.4 %copy-start.1 = (bf16[1024,2048]{1,0:T(8,128)(2,1)S(1)}, bf16[1024,2048]{1,0:T(8,128)(2,1)}, u32[]{:S(2)}) copy-start(bf16[1024,2048]{1,0:T(8,128)(2,1)} %refs_3_.8) | copy-start | bytes 12582916
  8.3 9.4 %copy-start.3 = (bf16[1024,256]{1,0:T(8,128)(2,1)S(1)}, bf16[1024,256]{1,0:T(8,128)(2,1)}, u32[]{:S(2)}) copy-start(bf16[1024,256]{1,0:T(8,128)(2,1)} %refs_3_.9) | copy-start | bytes 1572868
  8.3 9.4 %copy-start.4 = (bf16[1024,256]{1,0:T(8,128)(2,1)S(1)}, bf16[1024,256]{1,0:T(8,128)(2,1)}, u32[]{:S(2)}) copy-start(bf16[1024,256]{1,0:T(8,128)(2,1)} %refs_6_.1) | copy-start | bytes 1572868
  16.5 0.9 %copy-start.6 = (bf16[64,1024]{1,0:T(8,128)(2,1)S(1)}, bf16[64,1024]{1,0:T(8,128)(2,1)}, u32[]{:S(2)}) copy-start(bf16[64,1024]{1,0:T(8,128)(2,1)} %get-tuple-element.57.refs_0_) | copy-start | bytes 393220
  17.9 2.8 %collective-permute-start.5 = (bf16[256,1024]{1,0:T(8,128)(2,1)S(1)}, bf16[256,1024]{1,0:T(8,128)(2,1)S(1)}, u32[]{:S(2)}, u32[]{:S(2)}) collective-permute-start(bf16[256,1024]{1,0:T(8,128)(2,1)S(1)} %get-tuple-element.63), channel_id=1, source_target_pairs={{4,8},{26,22}} | collective-permute-start | bytes 1572872 | tf_op jit(solution)/shard_map/ppermute | solution.py:87
  18.6 19.8 %collective-permute-start.10 = (bf16[256,1024]{1,0:T(8,128)(2,1)S(1)}, bf16[256,1024]{1,0:T(8,128)(2,1)S(1)}, u32[]{:S(2)}, u32[]{:S(2)}) collective-permute-start(bf16[256,1024]{1,0:T(8,128)(2,1)S(1)} %get-tuple-element.63), channel_id=1, source_target_pairs={{26,20}} | collective-permute-start | bytes 1572872 | tf_op jit(solution)/shard_map/ppermute | solution.py:87
  19.3 6.6 %collective-permute-start.9 = (bf16[64,1024]{1,0:T(8,128)(2,1)S(1)}, bf16[64,1024]{1,0:T(8,128)(2,1)S(1)}, u32[]{:S(2)}, u32[]{:S(2)}) collective-permute-start(bf16[64,1024]{1,0:T(8,128)(2,1)S(1)} %get-tuple-element.73.refs_0_), channel_id=1, source_target_pairs={{0,4},{1,5},{2,6},{3,7},{12,8},{13,9},{14,10},{15,11},{16,20},{17,... | collective-permute-start | bytes 393224 | tf_op jit(solution)/shard_map/ppermute | solution.py:87
  20.8 6.2 %collective-permute-start.6 = (bf16[64,1024]{1,0:T(8,128)(2,1)S(1)}, bf16[64,1024]{1,0:T(8,128)(2,1)S(1)}, u32[]{:S(2)}, u32[]{:S(2)}) collective-permute-start(bf16[64,1024]{1,0:T(8,128)(2,1)S(1)} %get-tuple-element.70), channel_id=1, source_target_pairs={{4,5},{8,9}} | collective-permute-start | bytes 393224 | tf_op jit(solution)/shard_map/ppermute | solution.py:87
  21.5 5.5 %collective-permute-start.7 = (bf16[64,1024]{1,0:T(8,128)(2,1)S(1)}, bf16[64,1024]{1,0:T(8,128)(2,1)S(1)}, u32[]{:S(2)}, u32[]{:S(2)}) collective-permute-start(bf16[64,1024]{1,0:T(8,128)(2,1)S(1)} %get-tuple-element.71), channel_id=1, source_target_pairs={{4,6},{8,10}} | collective-permute-start | bytes 393224 | tf_op jit(solution)/shard_map/ppermute | solution.py:87
  22.1 4.8 %collective-permute-start.8 = (bf16[64,1024]{1,0:T(8,128)(2,1)S(1)}, bf16[64,1024]{1,0:T(8,128)(2,1)S(1)}, u32[]{:S(2)}, u32[]{:S(2)}) collective-permute-start(bf16[64,1024]{1,0:T(8,128)(2,1)S(1)} %get-tuple-element.72), channel_id=1, source_target_pairs={{4,7},{8,11}} | collective-permute-start | bytes 393224 | tf_op jit(solution)/shard_map/ppermute | solution.py:87
  25.9 29.5 %collective-permute-start.14 = (bf16[256,1024]{1,0:T(8,128)(2,1)S(1)}, bf16[256,1024]{1,0:T(8,128)(2,1)S(1)}, u32[]{:S(2)}, u32[]{:S(2)}) collective-permute-start(bf16[256,1024]{1,0:T(8,128)(2,1)S(1)} %get-tuple-element.62.refs_0_), channel_id=1, source_target_pairs={{26,27},{24,25}} | collective-permute-start | bytes 1572872 | tf_op jit(solution)/shard_map/ppermute | solution.py:87
  27.1 9.6 %collective-permute-start.13 = (bf16[64,1024]{1,0:T(8,128)(2,1)S(1)}, bf16[64,1024]{1,0:T(8,128)(2,1)S(1)}, u32[]{:S(2)}, u32[]{:S(2)}) collective-permute-start(bf16[64,1024]{1,0:T(8,128)(2,1)S(1)} %get-tuple-element.78.refs_0_), channel_id=1, source_target_pairs={{4,20},{5,21},{6,22},{7,23},{8,16},{9,17},{10,18},{11,19}} | collective-permute-start | bytes 393224 | tf_op jit(solution)/shard_map/ppermute | solution.py:87
  27.7 10.1 %collective-permute-start.12 = (bf16[64,1024]{1,0:T(8,128)(2,1)S(1)}, bf16[64,1024]{1,0:T(8,128)(2,1)S(1)}, u32[]{:S(2)}, u32[]{:S(2)}) collective-permute-start(bf16[64,1024]{1,0:T(8,128)(2,1)S(1)} %get-tuple-element.78.refs_0_), channel_id=1, source_target_pairs={{4,12},{5,13},{6,14},{7,15},{8,0},{9,1},{10,2},{11,3}} | collective-permute-start | bytes 393224 | tf_op jit(solution)/shard_map/ppermute | solution.py:87
  29.0 8.8 %collective-permute-start.11 = (bf16[64,1024]{1,0:T(8,128)(2,1)S(1)}, bf16[64,1024]{1,0:T(8,128)(2,1)S(1)}, u32[]{:S(2)}, u32[]{:S(2)}) collective-permute-start(bf16[64,1024]{1,0:T(8,128)(2,1)S(1)} %get-tuple-element.78.refs_0_), channel_id=1, source_target_pairs={{4,28},{5,29},{6,30},{7,31},{8,24},{9,25},{10,26},{11,27}} | collective-permute-start | bytes 393224 | tf_op jit(solution)/shard_map/ppermute | solution.py:87
  38.5 16.9 %collective-permute-start.15 = (bf16[256,1024]{1,0:T(8,128)(2,1)S(1)}, bf16[256,1024]{1,0:T(8,128)(2,1)S(1)}, u32[]{:S(2)}, u32[]{:S(2)}) collective-permute-start(bf16[256,1024]{1,0:T(8,128)(2,1)S(1)} %get-tuple-element.83.refs_2_), channel_id=1, source_target_pairs={{22,23},{20,21}} | collective-permute-start | bytes 1572872 | tf_op jit(solution)/shard_map/ppermute | solution.py:87
  39.2 16.2 %collective-permute-start.16 = (bf16[64,1024]{1,0:T(8,128)(2,1)S(1)}, bf16[64,1024]{1,0:T(8,128)(2,1)S(1)}, u32[]{:S(2)}, u32[]{:S(2)}) collective-permute-start(bf16[64,1024]{1,0:T(8,128)(2,1)S(1)} %get-tuple-element.89), channel_id=1, source_target_pairs={{0,4},{1,5},{2,6},{3,7},{4,0},{5,1},{6,2},{7,3},{8,12},{9,13},{10,... | collective-permute-start | bytes 393224 | tf_op jit(solution)/shard_map/ppermute | solution.py:87
  55.7 16.1 %collective-permute-start.17 = (bf16[2,64,1024]{2,1,0:T(8,128)(2,1)S(1)}, bf16[2,64,1024]{2,1,0:T(8,128)(2,1)S(1)}, u32[]{:S(2)}, u32[]{:S(2)}) collective-permute-start(bf16[2,64,1024]{2,1,0:T(8,128)(2,1)S(1)} %get-tuple-element.95), channel_id=1, source_target_pairs={{28,4},{29,5},{30,6},{31,7},{24,0},{25,1},{26,2},{27,3},{20,28},{2... | collective-permute-start | bytes 786440 | tf_op jit(solution)/shard_map/ppermute | solution.py:87
  56.4 17.3 %collective-permute-start.18 = (bf16[2,64,1024]{2,1,0:T(8,128)(2,1)S(1)}, bf16[2,64,1024]{2,1,0:T(8,128)(2,1)S(1)}, u32[]{:S(2)}, u32[]{:S(2)}) collective-permute-start(bf16[2,64,1024]{2,1,0:T(8,128)(2,1)S(1)} %get-tuple-element.96), channel_id=1, source_target_pairs={{28,12},{29,13},{30,14},{31,15},{24,8},{25,9},{26,10},{27,11},{20,... | collective-permute-start | bytes 786440 | tf_op jit(solution)/shard_map/ppermute | solution.py:87
  57.7 24.0 %collective-permute-start.19 = (bf16[2,64,1024]{2,1,0:T(8,128)(2,1)S(1)}, bf16[2,64,1024]{2,1,0:T(8,128)(2,1)S(1)}, u32[]{:S(2)}, u32[]{:S(2)}) collective-permute-start(bf16[2,64,1024]{2,1,0:T(8,128)(2,1)S(1)} %get-tuple-element.97), channel_id=1, source_target_pairs={{28,20},{29,21},{30,22},{31,23},{24,16},{25,17},{26,18},{27,19},{2... | collective-permute-start | bytes 786440 | tf_op jit(solution)/shard_map/ppermute | solution.py:87
  69.2 14.7 %collective-permute-start.20 = (bf16[64,1024]{1,0:T(8,128)(2,1)S(1)}, bf16[64,1024]{1,0:T(8,128)(2,1)S(1)}, u32[]{:S(2)}, u32[]{:S(2)}) collective-permute-start(bf16[64,1024]{1,0:T(8,128)(2,1)S(1)} %get-tuple-element.102), channel_id=1, source_target_pairs={{4,5},{5,6},{8,9},{9,10},{12,13},{13,14},{16,17},{17,18},{20,21},{... | collective-permute-start | bytes 393224 | tf_op jit(solution)/shard_map/ppermute | solution.py:87
  70.5 13.4 %collective-permute-start.21 = (bf16[64,1024]{1,0:T(8,128)(2,1)S(1)}, bf16[64,1024]{1,0:T(8,128)(2,1)S(1)}, u32[]{:S(2)}, u32[]{:S(2)}) collective-permute-start(bf16[64,1024]{1,0:T(8,128)(2,1)S(1)} %get-tuple-element.103), channel_id=1, source_target_pairs={{4,6},{5,7},{8,10},{9,11},{12,14},{13,15},{16,18},{17,19},{20,22},... | collective-permute-start | bytes 393224 | tf_op jit(solution)/shard_map/ppermute | solution.py:87
  71.8 12.1 %collective-permute-start.22 = (bf16[64,1024]{1,0:T(8,128)(2,1)S(1)}, bf16[64,1024]{1,0:T(8,128)(2,1)S(1)}, u32[]{:S(2)}, u32[]{:S(2)}) collective-permute-start(bf16[64,1024]{1,0:T(8,128)(2,1)S(1)} %get-tuple-element.104), channel_id=1, source_target_pairs={{4,7},{5,4},{8,11},{9,8},{12,15},{13,12},{16,19},{17,16},{20,23},{... | collective-permute-start | bytes 393224 | tf_op jit(solution)/shard_map/ppermute | solution.py:87
  82.0 5.5 %collective-permute-start.23 = (bf16[64,1024]{1,0:T(8,128)(2,1)S(1)}, bf16[64,1024]{1,0:T(8,128)(2,1)S(1)}, u32[]{:S(2)}, u32[]{:S(2)}) collective-permute-start(bf16[64,1024]{1,0:T(8,128)(2,1)S(1)} %get-tuple-element.106), channel_id=1, source_target_pairs={{0,4},{1,5},{2,6},{3,7},{4,0},{5,1},{6,2},{7,3},{8,12},{9,13},{10,... | collective-permute-start | bytes 393224 | tf_op jit(solution)/shard_map/ppermute | solution.py:87

commit v3 on v2

--- a/solution.py
+++ b/solution.py
@@ -1,5 +1,3 @@
-import functools
-
 import jax
 import jax.numpy as jnp
 from jax import lax
@@ -191,7 +189,8 @@
     y0_z = {e: send(y0_own, [((0, b), (e, b)) for b in all_cols]) for e in entry[1:]}
 
     def kernel7(v_in, fac, *rest):
-        sol_out, bq, (fbuf, vbuf, qbuf, sbuf, zbuf, sems) = rest[0], rest[1 : 1 + pairs], rest[1 + pairs :]
+        sol_out, e_out, bq = rest[0], rest[1], rest[2 : 2 + pairs]
+        fbuf, vbuf, qbuf, sbuf, zbuf, sems = rest[2 + pairs :]
         r, _ = place()
         cp = Copies(sems)
 
@@ -203,6 +202,7 @@
             v = vbuf[...]
             multiply(qbuf, v.astype(BF16), fbuf, last)
             done = [cp.start(qbuf.at[d], bq[d]) for d in range(pairs)]
+            done.append(cp.start(qbuf.at[pl.ds(0, pairs - 2)], e_out))
             sbuf[...] = jnp.transpose(v)
             wait(done + [cp.start(sbuf, sol_out)])
 
@@ -213,13 +213,14 @@
             zbuf[...] = jnp.zeros_like(zbuf)
             wait([cp.start(zbuf, sol_out.at[pl.ds(k * wide, wide)]) for k in range(NB // wide)])
 
-    sol, *bq, tok = call(
+    sol, sevens, *bq, tok = call(
         kernel7,
         [v7, factor],
-        [(tall, F32)] + [(pair_piece, BF16)] * pairs,
+        [(tall, F32), ((pairs - 2,) + pair_piece, BF16)] + [(pair_piece, BF16)] * pairs,
         [((cb, NB, NB), BF16), (full, F32), ((pairs, 2, piece, NB), BF16), (tall, F32), ((wide, wide), F32)],
-        2 + cb + pairs,
-    )
+        3 + cb + pairs,
+    )
+    sevens = send(sevens, [((last, b), (last - 2, b)) for b in all_cols])
 
     y0_cases = [(lambda r, c: r == 0, y0_own)] + [(lambda r, c, e=e: r == e, v) for e, v in y0_z.items()]
     y0_in, tok = route(y0_cases, (share, NB), order=[tok])
@@ -342,8 +343,8 @@
     for s in range(1, cols):
         cases += [(at(1, (g0 + s) % cols), dealt[s - 1]), (at(2, (g1 + s) % cols), dealt[s - 1])]
     y_own, y0_mine, tok = route(cases, (share, NB), order=[tok], through=[y0_mine])
-    to_odd = [pairs - 1] + [d for d in range(1, pairs - 1)]
-    to_even = [pairs - 1, 0] + [d for d in range(2, pairs - 1)]
+    to_odd = list(range(1, pairs))
+    to_even = [0] + list(range(2, pairs))
     y_z = [
         send(y_own, [((1, b), (2 * d + 1, b)) for b in all_cols] + [((2, b), (2 * e, b)) for b in all_cols])
         for d, e in zip(to_odd, to_even)
@@ -357,9 +358,50 @@
     all_swap = [((a, b), (a ^ 1, b)) for a in range(rows) for b in all_cols]
     y_other = send(y_mine, all_swap)
 
+    i = last - 2
+    slots = {d: d + 1 for d in range(pairs - 2)}
+    slots.update({pairs - 1: 0, pairs - 2: pairs - 1})
+    own_slots = {d: d for d in range(pairs)}
+
+    def solve(cp, te, to, fac, inv, fv, sol_out, outs, row, to_slot, scratch, sems, more=None):
+        dbuf, fbuf, rbuf, abuf, qbuf, sbuf = scratch
+        _, c = place()
+        has = (c == g5) | ((c % 2 == 0) & (c // 2 != g5 // 2))
+        sem = sems.at[4 + cb + pairs]
+        ins = [cp.start(fv, rbuf), cp.start(inv, dbuf)]
+        fs = [cp.start(fac.at[:, pl.ds(k * NB, NB)], fbuf.at[k]) for k in range(cb)]
+        if more is not None:
+            fs.append(cp.start(*more))
+
+        @pl.when(has)
+        def _():
+            pltpu.make_async_copy(te, abuf, sem).start()
+
+        @pl.when(jnp.logical_not(has))
+        def _():
+            pltpu.make_async_copy(to, abuf, sem).start()
+
+        ins[0].wait()
+        w = flip(rbuf[...])
+        pltpu.make_async_copy(te, abuf, sem).wait()
+        w = w - abuf[...].astype(F32)
+        ins[1].wait()
+        v = nn(w.astype(BF16), dbuf[...])
+        wait(fs)
+        multiply(qbuf, v.astype(BF16), fbuf, row)
+        if more is not None:
+            for d in range(pairs - 2):
+                qbuf[d] = (qbuf[d].astype(F32) + more[1][d].astype(F32)).astype(BF16)
+        done = [cp.start(qbuf.at[d], outs[t]) for d, t in to_slot.items()]
+        sbuf[...] = jnp.transpose(v)
+        wait(done + [cp.start(sbuf, sol_out)])
+
+    solve_scratch = [(square, BF16), ((cb, NB, NB), BF16), (tall, BF16), (full, BF16), ((pairs, 2, piece, NB), BF16), (tall, F32)]
+
     def kernelt(*refs):
         n = len(evens5) + 1
-        first, second, (_, out, _, abuf, bbuf, sems) = refs[:n], refs[n : 2 * n], refs[2 * n :]
+        first, second, refs = refs[:n], refs[n : 2 * n], refs[2 * n :]
+        out, abuf, bbuf, sems = refs[2], refs[-3], refs[-2], refs[-1]
         r, c = place()
         cp = Copies(sems)
         for col, x, q in zip([g5] + evens5, first, second):
@@ -371,78 +413,52 @@
                 abuf[...] = (abuf[...].astype(F32) + bbuf[...].astype(F32)).astype(BF16)
                 cp.start(abuf, out).wait()
 
-    t5_even, y_near, tok = call(
+    n_first = 2 * len(evens5) + 2
+    t5_even, y_near, sevens, tok = call(
         kernelt,
-        [a3] + a4 + [a2] + q75_parts + [y_near],
-        [(full, BF16), ((share, NB), BF16)],
+        [a3] + a4 + [a2] + q75_parts + [y_near, sevens],
+        [(full, BF16), ((share, NB), BF16), (sevens.shape, BF16)],
         [(full, BF16), (full, BF16)],
         3,
-        aliases={2 * len(evens5) + 2: 1},
+        aliases={n_first: 1, n_first + 1: 2},
         order=[tok],
     )
     t5_odd = send(t5_even, within_chip(last - 2, g5))
 
     near_all = lax.all_gather(y_near, "col", axis=0, tiled=True)
 
-    i = last - 2
-    slots = {d: d + 1 for d in range(pairs - 2)}
-    slots.update({pairs - 1: 0, pairs - 2: pairs - 1})
-    own_slots = {d: d for d in range(pairs)}
-
-    def lands(d):
-        return 2 * d if d < (pairs - 2) // 2 else 2 * d + 1
-
-    def kernel5(t6e, t6o, t5e, t5o, fac, inv, fv, *rest):
+    def kernel5(t6e, t6o, t5e, t5o, seven, fac, inv, fv, *rest):
         n = pairs + 2
         sol_out, outs = rest[n], rest[n + 1 : n + 1 + pairs]
-        dbuf, fbuf, rbuf, abuf, qbuf, sbuf, sems = rest[2 * n :]
-        r, c = place()
-        cp = Copies(sems)
-        has = (c == g5) | ((c % 2 == 0) & (c // 2 != g5 // 2))
-        sem = sems.at[3 + cb + pairs]
-
-        for row, te, to, to_slot in ((last - 1, t6e, t6o, own_slots), (i, t5e, t5o, slots)):
-            cp.branch()
-
-            @pl.when(r == row)
-            def _(row=row, te=te, to=to, to_slot=to_slot):
-                ins = [cp.start(fv, rbuf), cp.start(inv, dbuf)]
-                fs = [cp.start(fac.at[:, pl.ds(k * NB, NB)], fbuf.at[k]) for k in range(cb)]
-
-                @pl.when(has)
-                def _():
-                    pltpu.make_async_copy(te, abuf, sem).start()
-
-                @pl.when(jnp.logical_not(has))
-                def _():
-                    pltpu.make_async_copy(to, abuf, sem).start()
-
-                ins[0].wait()
-                w = flip(rbuf[...])
-                pltpu.make_async_copy(te, abuf, sem).wait()
-                w = w - abuf[...].astype(F32)
-                ins[1].wait()
-                v = nn(w.astype(BF16), dbuf[...])
-                wait(fs)
-                multiply(qbuf, v.astype(BF16), fbuf, row)
-                done = [cp.start(qbuf.at[d], outs[t]) for d, t in to_slot.items()]
-                sbuf[...] = jnp.transpose(v)
-                wait(done + [cp.start(sbuf, sol_out)])
+        scratch, ebuf, sems = rest[2 * n : -2], rest[-2], rest[-1]
+        r, _ = place()
+        cp = Copies(sems)
+
+        @pl.when(r == last - 1)
+        def _():
+            solve(cp, t6e, t6o, fac, inv, fv, sol_out, outs, last - 1, own_slots, scratch, sems)
+
+        cp.branch()
+
+        @pl.when(r == i)
+        def _():
+            solve(cp, t5e, t5o, fac, inv, fv, sol_out, outs, i, slots, scratch, sems, (seven, ebuf))
 
     sol, *bq, y_other, tok = call(
         kernel5,
-        [t6_even, t6_odd, t5_even, t5_odd, factor, diag_inv, forward_values, sol] + bq + [y_other],
+        [t6_even, t6_odd, t5_even, t5_odd, sevens, factor, diag_inv, forward_values, sol] + bq + [y_other],
         [(tall, F32)] + [(pair_piece, BF16)] * pairs + [((share, NB), BF16)],
-        [(square, BF16), ((cb, NB, NB), BF16), (tall, BF16), (full, BF16), ((pairs, 2, piece, NB), BF16), (tall, F32)],
-        4 + cb + pairs,
-        aliases={7 + k: k for k in range(pairs + 2)},
+        solve_scratch + [((pairs - 2,) + pair_piece, BF16)],
+        5 + cb + pairs,
+        aliases={8 + k: k for k in range(pairs + 2)},
         order=[tok, near_all],
     )
     scattered = []
     for t in range(pairs - 1):
         to = [d for d, k in slots.items() if k == t][0]
-        pairs_t = [((last, b), (2 * t + 1, b)) for b in all_cols] + [((last - 1, b), (2 * t, b)) for b in all_cols]
-        scattered.append(send(bq[t], pairs_t + [((i, b), (lands(to), b)) for b in all_cols]))
+        pairs_t = [((last - 1, b), (2 * t, b)) for b in all_cols]
+        pairs_t += [((last, b), (2 * t + 1, b)) for b in all_cols if t == pairs - 2]
+        scattered.append(send(bq[t], pairs_t + [((i, b), (2 * to + 1, b)) for b in all_cols]))
 
     far_all = lax.all_gather(y_other, "col", axis=0, tiled=True)
 
@@ -501,34 +517,44 @@
         got, (own_out, part_out, bbuf, fbuf, obuf, pbuf, sems) = rest[: pairs - 1], rest[pairs - 1 :]
         r, _ = place()
         cp = Copies(sems)
-        pair = r // 2
         refs = list(got) + [own_q]
         for d in range(pairs):
             cp.branch()
 
-            @pl.when(pair == d)
+            @pl.when(r == 2 * d)
             def _(d=d):
                 cp.start(refs[d], bbuf).wait()
 
-            @pl.when(r == lands(d))
+            @pl.when(r == 2 * d + 1)
             def _(d=d):
                 cp.start(refs[slots[d]], fbuf).wait()
 
         cp.branch()
 
-        takes = functools.reduce(jnp.logical_or, [r == lands(d) for d in range(pairs)])
-        for y in (0, 1):
-            for more in (False, True):
-
-                @pl.when((lax.rem(r, 2) == y) & (takes if more else jnp.logical_not(takes)))
-                def _(y=y, more=more):
-                    ours, theirs = bbuf[y].astype(F32), bbuf[1 - y].astype(F32)
-                    if more:
-                        ours = ours + fbuf[y].astype(F32)
-                        theirs = theirs + fbuf[1 - y].astype(F32)
-                    obuf[...] = ours
-                    pbuf[...] = theirs.astype(BF16)
-
+        @pl.when(r == last)
+        def _():
+            cp.start(own_q, bbuf).wait()
+
+        @pl.when(r == last - 2)
+        def _():
+            cp.start(refs[pairs - 2], bbuf).wait()
+
+        @pl.when(lax.rem(r, 2) == 0)
+        def _():
+            obuf[...] = bbuf[0].astype(F32)
+            pbuf[...] = bbuf[1]
+
+        @pl.when((lax.rem(r, 2) == 1) & (r < last - 2))
+        def _():
+            obuf[...] = fbuf[1].astype(F32)
+            pbuf[...] = fbuf[0]
+
+        @pl.when((lax.rem(r, 2) == 1) & (r >= last - 2))
+        def _():
+            obuf[...] = fbuf[1].astype(F32) + bbuf[1].astype(F32)
+            pbuf[...] = (fbuf[0].astype(F32) + bbuf[0].astype(F32)).astype(BF16)
+
+        cp.branch()
         wait([cp.start(pbuf, part_out), cp.start(obuf, own_out)])
 
     own, part, tok = call(

time: 88.8 us -> 84.1 us (0.947)
  the two profiles are of different devices: /device:TPU:12 before, /device:TPU:16 now
where the time goes in v3:
time: 84.1 us; the launch traced here: 83.3 us
  starting transfers between devices  27.3 us (32%)
  blocking collectives  23.8 us (28%)
  waiting for transfers between devices  17.3 us (21%)
  Pallas kernels  8.03 us (10%)
  local copies, waits for them, and re-layouts  4.35 us (5%)
  other arithmetic  1.52 us (2%)
  between operations  1.11 us (1%)
    ppermute x25, starting transfers between devices, send(): lax.ppermute(x, BOTH, [(a * cols + b, d * cols + e) for (a, b), (d, e) in...  27.3 us
    ppermute x25, waiting for transfers between devices, send(): lax.ppermute(x, BOTH, [(a * cols + b, d * cols + e) for (a, b), (d, e) in...  17.3 us
    all_gather x1, blocking collectives, local(): y0_all = lax.all_gather(y0_mine, 'col', axis=0, tiled=True)  8.81 us
    pallas_call x14, Pallas kernels, call(): pl.pallas_call(body, out_shape=[jax.ShapeDtypeStruct(s, d) for s, d in ou...  8.03 us
    all_gather x1, blocking collectives, local(): near_all = lax.all_gather(y_near, 'col', axis=0, tiled=True)  7.66 us
    all_gather x1, blocking collectives, local(): far_all = lax.all_gather(y_other, 'col', axis=0, tiled=True)  7.29 us
    unnamed x14, local copies, waits for them, and re-layouts  4.33 us
  transfers between devices with their start and end apart: 25, of which 5 were waited for; matrix products, arithmetic and copies ran while one was open for 1% of the time, Pallas kernels for 9%

profile of v3, /device:TPU:16, one launch (start us, length us, event | category | flops | bytes accessed | tf_op | source)
XLA Modules:
  0.0 83.3 jit_solution(10997102725443552935)
XLA Ops:
  0.7 0.8 collective-permute-start
  2.2 1.3 %collective-permute-start.3 = (bf16[64,1024]{1,0:T(8,128)(2,1)}, bf16[64,1024]{1,0:T(8,128)(2,1)S(1)}, u32[]{:S(2)}, u32[]{:S(2)}) collective-permute-start(bf16[64,1024]{1,0:T(8,128)(2,1)} %get-tuple-element.59.refs_0_), channel_id=1, source_target_pairs={{0,16},{1,17},{2,18},{3,19}} | collective-permute-start | bytes 393224 | tf_op jit(solution)/shard_map/ppermute | solution.py:85
  4.2 0.7 collective-permute-start.1
  4.9 2.2 %copy-done = bf16[1024,2048]{1,0:T(8,128)(2,1)S(1)} copy-done((bf16[1024,2048]{1,0:T(8,128)(2,1)S(1)}, bf16[1024,2048]{1,0:T(8,128)(2,1)}, u32[]{:S(2)}) %copy-start) | copy-done | bytes 4194328
  7.1 1.2 %copy-done.5 = f32[256,1024]{1,0:T(8,128)S(1)} copy-done((f32[256,1024]{1,0:T(8,128)S(1)}, f32[256,1024]{1,0:T(8,128)}, u32[]{:S(2)}) %copy-start.5) | copy-done | bytes 1048600
  8.3 1.1 %shard_map.76 = (f32[1024,256]{1,0:T(8,128)}, bf16[2,2,64,1024]{3,2,1,0:T(8,128)(2,1)S(1)}, bf16[2,64,1024]{2,1,0:T(8,128)(2,1)S(1)}, bf16[2,64,1024]{2,1,0:T(8,...) custom-call(f32[256,1024]{1,0:T(8,128)S(1)} %copy-done.5, ...), custom_call_target="tpu_custom_call" | custom-call | tf_op jit(solution)/shard_map/pallas_call | solution.py:50
  9.4 5.4 %collective-permute-done.3.refs_2_ = bf16[64,1024]{1,0:T(8,128)(2,1)S(1)} collective-permute-done((bf16[64,1024]{1,0:T(8,128)(2,1)}, bf16[64,1024]{1,0:T(8,128)(2,1)S(1)}, u32[]{:S(2)}, u32[]{:S(2)}) %collective-permute-start.3) | collective-permute-done | bytes 131104 | tf_op jit(solution)/shard_map/ppermute | solution.py:85
  14.8 0.9 %copy-done.6 = bf16[64,1024]{1,0:T(8,128)(2,1)S(1)} copy-done((bf16[64,1024]{1,0:T(8,128)(2,1)S(1)}, bf16[64,1024]{1,0:T(8,128)(2,1)}, u32[]{:S(2)}) %copy-start.6) | copy-done | bytes 131096
  16.2 0.7 collective-permute-start.5
  16.9 0.7 collective-permute-start.14
  17.6 0.7 collective-permute-start.10
  18.3 4.8 %collective-permute-start.9 = (bf16[64,1024]{1,0:T(8,128)(2,1)S(1)}, bf16[64,1024]{1,0:T(8,128)(2,1)S(1)}, u32[]{:S(2)}, u32[]{:S(2)}) collective-permute-start(bf16[64,1024]{1,0:T(8,128)(2,1)S(1)} %get-tuple-element.75.refs_0_), channel_id=1, source_target_pairs={{0,4},{1,5},{2,6},{3,7},{12,8},{13,9},{14,10},{15,11},{16,20},{17,... | collective-permute-start | bytes 393224 | tf_op jit(solution)/shard_map/ppermute | solution.py:85
  24.6 1.0 %collective-permute-done.9.refs_1_ = bf16[64,1024]{1,0:T(8,128)(2,1)S(1)} collective-permute-done((bf16[64,1024]{1,0:T(8,128)(2,1)S(1)}, bf16[64,1024]{1,0:T(8,128)(2,1)S(1)}, u32[]{:S(2)}, u32[]{:S(2)}) %collective-permute-start.9) | collective-permute-done | bytes 131104 | tf_op jit(solution)/shard_map/ppermute | solution.py:85
  27.4 1.3 %collective-permute-start.12 = (bf16[64,1024]{1,0:T(8,128)(2,1)S(1)}, bf16[64,1024]{1,0:T(8,128)(2,1)S(1)}, u32[]{:S(2)}, u32[]{:S(2)}) collective-permute-start(bf16[64,1024]{1,0:T(8,128)(2,1)S(1)} %get-tuple-element.80.refs_0_), channel_id=1, source_target_pairs={{4,20},{5,21},{6,22},{7,23},{8,16},{9,17},{10,18},{11,19}} | collective-permute-start | bytes 393224 | tf_op jit(solution)/shard_map/ppermute | solution.py:85
  29.4 8.8 %all_gather.9.refs_5_.refs_0_ = bf16[256,1024]{1,0:T(8,128)(2,1)S(1)} all-gather(bf16[64,1024]{1,0:T(8,128)(2,1)S(1)} %get-tuple-element.79), channel_id=1, replica_groups=mesh['row'=8,'col'=4] {'col'}, dimensions={0}, use_global_device_ids=true | all-gather | bytes 655360 | tf_op jit(solution)/shard_map/all_gather | solution.py:353
  38.2 0.7 collective-permute-start.15
  38.9 2.2 %collective-permute-done.12.refs_2_ = bf16[64,1024]{1,0:T(8,128)(2,1)S(1)} collective-permute-done((bf16[64,1024]{1,0:T(8,128)(2,1)S(1)}, bf16[64,1024]{1,0:T(8,128)(2,1)S(1)}, u32[]{:S(2)}, u32[]{:S(2)}) %collective-permute-start.12) | collective-permute-done | bytes 131104 | tf_op jit(solution)/shard_map/ppermute | solution.py:85
  41.7 0.7 collective-permute-start.16
  42.4 2.1 %collective-permute-start.17 = (bf16[64,1024]{1,0:T(8,128)(2,1)S(1)}, bf16[64,1024]{1,0:T(8,128)(2,1)S(1)}, u32[]{:S(2)}, u32[]{:S(2)}) collective-permute-start(bf16[64,1024]{1,0:T(8,128)(2,1)S(1)} %get-tuple-element.93), channel_id=1, source_target_pairs={{0,4},{1,5},{2,6},{3,7},{4,0},{5,1},{6,2},{7,3},{8,12},{9,13},{10,... | collective-permute-start | bytes 393224 | tf_op jit(solution)/shard_map/ppermute | solution.py:85
  44.6 7.7 %all_gather.10.refs_15_.refs_1_ = bf16[256,1024]{1,0:T(8,128)(2,1)S(1)} all-gather(bf16[64,1024]{1,0:T(8,128)(2,1)S(1)} %get-tuple-element.85), channel_id=1, replica_groups=mesh['row'=8,'col'=4] {'col'}, dimensions={0}, use_global_device_ids=true | all-gather | bytes 655360 | tf_op jit(solution)/shard_map/all_gather | solution.py:428
  53.9 1.3 %collective-permute-start.20 = (bf16[2,64,1024]{2,1,0:T(8,128)(2,1)S(1)}, bf16[2,64,1024]{2,1,0:T(8,128)(2,1)S(1)}, u32[]{:S(2)}, u32[]{:S(2)}) collective-permute-start(bf16[2,64,1024]{2,1,0:T(8,128)(2,1)S(1)} %get-tuple-element.101), channel_id=1, source_target_pairs={{24,16},{25,17},{26,18},{27,19},{28,20},{29,21},{30,22},{31,23},{2... | collective-permute-start | bytes 786440 | tf_op jit(solution)/shard_map/ppermute | solution.py:85
  55.2 7.3 %all_gather.11.refs_2_ = bf16[256,1024]{1,0:T(8,128)(2,1)S(1)} all-gather(bf16[64,1024]{1,0:T(8,128)(2,1)S(1)} %get-tuple-element.95), channel_id=1, replica_groups=mesh['row'=8,'col'=4] {'col'}, dimensions={0}, use_global_device_ids=true | all-gather | bytes 655360 | tf_op jit(solution)/shard_map/all_gather | solution.py:463
  62.5 2.9 %shard_map.86 = (bf16[64,1024]{1,0:T(8,128)(2,1)S(1)}, bf16[64,1024]{1,0:T(8,128)(2,1)S(1)}, bf16[64,1024]{1,0:T(8,128)(2,1)S(1)}, bf16[64,1024]{1,0:T(8,128)(2,1)S(1)}, f32[8,128]{1,0:T(8,128)S(1)}) custom-call(bf16[256,1024]{1,0:T(8,128)(2,1)S(1)} %all_gather.9.refs_5_.refs_0_, bf16[256,1024]{1,0:T(8,128)(2,1)S(1)} %all_gather.10.refs_15_.refs_1_, ...), custom_call_target="tpu_custom_call" | custom-call | tf_op jit(solution)/shard_map/pallas_call | solution.py:50
  65.4 1.3 %collective-permute-start.21 = (bf16[64,1024]{1,0:T(8,128)(2,1)S(1)}, bf16[64,1024]{1,0:T(8,128)(2,1)S(1)}, u32[]{:S(2)}, u32[]{:S(2)}) collective-permute-start(bf16[64,1024]{1,0:T(8,128)(2,1)S(1)} %get-tuple-element.106), channel_id=1, source_target_pairs={{4,5},{5,6},{8,9},{9,10},{12,13},{13,14},{16,17},{17,18},{20,21},{... | collective-permute-start | bytes 393224 | tf_op jit(solution)/shard_map/ppermute | solution.py:85
  66.7 1.3 %collective-permute-start.22 = (bf16[64,1024]{1,0:T(8,128)(2,1)S(1)}, bf16[64,1024]{1,0:T(8,128)(2,1)S(1)}, u32[]{:S(2)}, u32[]{:S(2)}) collective-permute-start(bf16[64,1024]{1,0:T(8,128)(2,1)S(1)} %get-tuple-element.107), channel_id=1, source_target_pairs={{4,6},{5,7},{8,10},{9,11},{12,14},{13,15},{16,18},{17,19},{20,22},... | collective-permute-start | bytes 393224 | tf_op jit(solution)/shard_map/ppermute | solution.py:85
  68.0 1.9 %collective-permute-start.23 = (bf16[64,1024]{1,0:T(8,128)(2,1)S(1)}, bf16[64,1024]{1,0:T(8,128)(2,1)S(1)}, u32[]{:S(2)}, u32[]{:S(2)}) collective-permute-start(bf16[64,1024]{1,0:T(8,128)(2,1)S(1)} %get-tuple-element.108), channel_id=1, source_target_pairs={{4,7},{5,4},{8,11},{9,8},{12,15},{13,12},{16,19},{17,16},{20,23},{... | collective-permute-start | bytes 393224 | tf_op jit(solution)/shard_map/ppermute | solution.py:85
  70.0 7.0 %collective-permute-done.20.refs_3_ = bf16[2,64,1024]{2,1,0:T(8,128)(2,1)S(1)} collective-permute-done((bf16[2,64,1024]{2,1,0:T(8,128)(2,1)S(1)}, bf16[2,64,1024]{2,1,0:T(8,128)(2,1)S(1)}, u32[]{:S(2)}, u32[]{:S(2)}) %collective-permute-start.20) | collective-permute-done | bytes 262176 | tf_op jit(solution)/shard_map/ppermute | solution.py:85
  77.2 1.0 %collective-permute-start.24 = (bf16[64,1024]{1,0:T(8,128)(2,1)S(1)}, bf16[64,1024]{1,0:T(8,128)(2,1)S(1)}, u32[]{:S(2)}, u32[]{:S(2)}) collective-permute-start(bf16[64,1024]{1,0:T(8,128)(2,1)S(1)} %get-tuple-element.110), channel_id=1, source_target_pairs={{0,4},{1,5},{2,6},{3,7},{4,0},{5,1},{6,2},{7,3},{8,12},{9,13},{10,... | collective-permute-start | bytes 393224 | tf_op jit(solution)/shard_map/ppermute | solution.py:85
  78.2 1.8 %shard_map.88 = (bf16[3072,256]{1,0:T(8,128)(2,1)}, f32[64,1024]{1,0:T(8,128)S(1)}, f32[8,128]{1,0:T(8,128)}) custom-call(bf16[256,1024]{1,0:T(8,128)(2,1)S(1)} %all_gather.9.refs_5_.refs_0_, bf16[256,1024]{1,0:T(8,128)(2,1)S(1)} %all_gather.10.refs_15_.refs_1_, bf16[256,1024]{1,0:T(8,128)(2,1)S(1)} %all_gather.11.refs_2_, bf16[1024,256]{1,0:T(8,128)(2,1)S(1)} %copy-done.3, ...), custom_call_target="tpu_custom_call" | custom-call | tf_op jit(solution)/shard_map/pallas_call | solution.py:50
  80.1 0.8 subtract_bitcast_fusion
  80.9 1.7 %collective-permute-done.24 = bf16[64,1024]{1,0:T(8,128)(2,1)S(1)} collective-permute-done((bf16[64,1024]{1,0:T(8,128)(2,1)S(1)}, bf16[64,1024]{1,0:T(8,128)(2,1)S(1)}, u32[]{:S(2)}, u32[]{:S(2)}) %collective-permute-start.24) | collective-permute-done | bytes 131104 | tf_op jit(solution)/shard_map/ppermute | solution.py:85
  82.6 0.7 maximum_bitcast_fusion
  (53 shorter events, 8.4 us)
Async XLA Ops:
  0.6 15.4 %copy-start.2 = (bf16[1024,1024]{1,0:T(8,128)(2,1)S(1)}, bf16[1024,1024]{1,0:T(8,128)(2,1)}, u32[]{:S(2)}) copy-start(bf16[1024,1024]{1,0:T(8,128)(2,1)} %refs_6_.1) | copy-start | bytes 6291460
  0.7 15.3 %collective-permute-start = (bf16[256,1024]{1,0:T(8,128)(2,1)}, bf16[256,1024]{1,0:T(8,128)(2,1)S(1)}, u32[]{:S(2)}, u32[]{:S(2)}) collective-permute-start(bf16[256,1024]{1,0:T(8,128)(2,1)} %get-tuple-element.58), channel_id=1, source_target_pairs={{0,4},{31,26},{30,20}} | collective-permute-start | bytes 1572872 | tf_op jit(solution)/shard_map/ppermute | solution.py:85
  1.5 7.8 %collective-permute-start.4 = (bf16[64,1024]{1,0:T(8,128)(2,1)}, bf16[64,1024]{1,0:T(8,128)(2,1)S(1)}, u32[]{:S(2)}, u32[]{:S(2)}) collective-permute-start(bf16[64,1024]{1,0:T(8,128)(2,1)} %get-tuple-element.59.refs_0_), channel_id=1, source_target_pairs={{0,24},{1,25},{2,26},{3,27}} | collective-permute-start | bytes 393224 | tf_op jit(solution)/shard_map/ppermute | solution.py:85
  2.2 12.5 %collective-permute-start.3 = (bf16[64,1024]{1,0:T(8,128)(2,1)}, bf16[64,1024]{1,0:T(8,128)(2,1)S(1)}, u32[]{:S(2)}, u32[]{:S(2)}) collective-permute-start(bf16[64,1024]{1,0:T(8,128)(2,1)} %get-tuple-element.59.refs_0_), channel_id=1, source_target_pairs={{0,16},{1,17},{2,18},{3,19}} | collective-permute-start | bytes 393224 | tf_op jit(solution)/shard_map/ppermute | solution.py:85
  3.5 11.2 %collective-permute-start.2 = (bf16[64,1024]{1,0:T(8,128)(2,1)}, bf16[64,1024]{1,0:T(8,128)(2,1)S(1)}, u32[]{:S(2)}, u32[]{:S(2)}) collective-permute-start(bf16[64,1024]{1,0:T(8,128)(2,1)} %get-tuple-element.59.refs_0_), channel_id=1, source_target_pairs={{0,12},{1,13},{2,14},{3,15}} | collective-permute-start | bytes 393224 | tf_op jit(solution)/shard_map/ppermute | solution.py:85
  4.2 18.8 %collective-permute-start.1 = (bf16[256,1024]{1,0:T(8,128)(2,1)}, bf16[256,1024]{1,0:T(8,128)(2,1)S(1)}, u32[]{:S(2)}, u32[]{:S(2)}) collective-permute-start(bf16[256,1024]{1,0:T(8,128)(2,1)} %get-tuple-element.58), channel_id=1, source_target_pairs={{0,8},{31,24},{30,22}} | collective-permute-start | bytes 1572872 | tf_op jit(solution)/shard_map/ppermute | solution.py:85
  4.9 2.2 %copy-start = (bf16[1024,2048]{1,0:T(8,128)(2,1)S(1)}, bf16[1024,2048]{1,0:T(8,128)(2,1)}, u32[]{:S(2)}) copy-start(bf16[1024,2048]{1,0:T(8,128)(2,1)} %refs_3_.8) | copy-start | bytes 12582916
  7.1 1.2 %copy-start.5 = (f32[256,1024]{1,0:T(8,128)S(1)}, f32[256,1024]{1,0:T(8,128)}, u32[]{:S(2)}) copy-start(f32[256,1024]{1,0:T(8,128)} %get-tuple-element.60.refs_0_) | copy-start | bytes 3145732
  8.3 7.7 %copy-start.1 = (bf16[1024,2048]{1,0:T(8,128)(2,1)S(1)}, bf16[1024,2048]{1,0:T(8,128)(2,1)}, u32[]{:S(2)}) copy-start(bf16[1024,2048]{1,0:T(8,128)(2,1)} %refs_3_.8) | copy-start | bytes 12582916
  8.3 7.7 %copy-start.3 = (bf16[1024,256]{1,0:T(8,128)(2,1)S(1)}, bf16[1024,256]{1,0:T(8,128)(2,1)}, u32[]{:S(2)}) copy-start(bf16[1024,256]{1,0:T(8,128)(2,1)} %refs_3_.9) | copy-start | bytes 1572868
  8.3 7.7 %copy-start.4 = (bf16[1024,256]{1,0:T(8,128)(2,1)S(1)}, bf16[1024,256]{1,0:T(8,128)(2,1)}, u32[]{:S(2)}) copy-start(bf16[1024,256]{1,0:T(8,128)(2,1)} %refs_7_.1) | copy-start | bytes 1572868
  14.8 0.9 %copy-start.6 = (bf16[64,1024]{1,0:T(8,128)(2,1)S(1)}, bf16[64,1024]{1,0:T(8,128)(2,1)}, u32[]{:S(2)}) copy-start(bf16[64,1024]{1,0:T(8,128)(2,1)} %get-tuple-element.59.refs_0_) | copy-start | bytes 393220
  16.2 7.0 %collective-permute-start.5 = (bf16[256,1024]{1,0:T(8,128)(2,1)S(1)}, bf16[256,1024]{1,0:T(8,128)(2,1)S(1)}, u32[]{:S(2)}, u32[]{:S(2)}) collective-permute-start(bf16[256,1024]{1,0:T(8,128)(2,1)S(1)} %get-tuple-element.65), channel_id=1, source_target_pairs={{4,8},{26,22}} | collective-permute-start | bytes 1572872 | tf_op jit(solution)/shard_map/ppermute | solution.py:85
  16.9 24.8 %collective-permute-start.14 = (bf16[2,2,64,1024]{3,2,1,0:T(8,128)(2,1)S(1)}, bf16[2,2,64,1024]{3,2,1,0:T(8,128)(2,1)S(1)}, u32[]{:S(2)}, u32[]{:S(2)}) collective-permute-start(bf16[2,2,64,1024]{3,2,1,0:T(8,128)(2,1)S(1)} %get-tuple-element.83), channel_id=1, source_target_pairs={{28,20},{29,21},{30,22},{31,23}} | collective-permute-start | bytes 1572872 | tf_op jit(solution)/shard_map/ppermute | solution.py:85
  17.6 24.1 %collective-permute-start.10 = (bf16[256,1024]{1,0:T(8,128)(2,1)S(1)}, bf16[256,1024]{1,0:T(8,128)(2,1)S(1)}, u32[]{:S(2)}, u32[]{:S(2)}) collective-permute-start(bf16[256,1024]{1,0:T(8,128)(2,1)S(1)} %get-tuple-element.65), channel_id=1, source_target_pairs={{26,20}} | collective-permute-start | bytes 1572872 | tf_op jit(solution)/shard_map/ppermute | solution.py:85
  18.3 7.3 %collective-permute-start.9 = (bf16[64,1024]{1,0:T(8,128)(2,1)S(1)}, bf16[64,1024]{1,0:T(8,128)(2,1)S(1)}, u32[]{:S(2)}, u32[]{:S(2)}) collective-permute-start(bf16[64,1024]{1,0:T(8,128)(2,1)S(1)} %get-tuple-element.75.refs_0_), channel_id=1, source_target_pairs={{0,4},{1,5},{2,6},{3,7},{12,8},{13,9},{14,10},{15,11},{16,20},{17,... | collective-permute-start | bytes 393224 | tf_op jit(solution)/shard_map/ppermute | solution.py:85
  23.2 3.4 %collective-permute-start.6 = (bf16[64,1024]{1,0:T(8,128)(2,1)S(1)}, bf16[64,1024]{1,0:T(8,128)(2,1)S(1)}, u32[]{:S(2)}, u32[]{:S(2)}) collective-permute-start(bf16[64,1024]{1,0:T(8,128)(2,1)S(1)} %get-tuple-element.72), channel_id=1, source_target_pairs={{4,5},{8,9}} | collective-permute-start | bytes 393224 | tf_op jit(solution)/shard_map/ppermute | solution.py:85
  23.9 2.7 %collective-permute-start.7 = (bf16[64,1024]{1,0:T(8,128)(2,1)S(1)}, bf16[64,1024]{1,0:T(8,128)(2,1)S(1)}, u32[]{:S(2)}, u32[]{:S(2)}) collective-permute-start(bf16[64,1024]{1,0:T(8,128)(2,1)S(1)} %get-tuple-element.73), channel_id=1, source_target_pairs={{4,6},{8,10}} | collective-permute-start | bytes 393224 | tf_op jit(solution)/shard_map/ppermute | solution.py:85
  25.5 1.1 %collective-permute-start.8 = (bf16[64,1024]{1,0:T(8,128)(2,1)S(1)}, bf16[64,1024]{1,0:T(8,128)(2,1)S(1)}, u32[]{:S(2)}, u32[]{:S(2)}) collective-permute-start(bf16[64,1024]{1,0:T(8,128)(2,1)S(1)} %get-tuple-element.74), channel_id=1, source_target_pairs={{4,7},{8,11}} | collective-permute-start | bytes 393224 | tf_op jit(solution)/shard_map/ppermute | solution.py:85
  26.7 11.5 %collective-permute-start.13 = (bf16[64,1024]{1,0:T(8,128)(2,1)S(1)}, bf16[64,1024]{1,0:T(8,128)(2,1)S(1)}, u32[]{:S(2)}, u32[]{:S(2)}) collective-permute-start(bf16[64,1024]{1,0:T(8,128)(2,1)S(1)} %get-tuple-element.80.refs_0_), channel_id=1, source_target_pairs={{4,28},{5,29},{6,30},{7,31},{8,24},{9,25},{10,26},{11,27}} | collective-permute-start | bytes 393224 | tf_op jit(solution)/shard_map/ppermute | solution.py:85
  27.4 13.7 %collective-permute-start.12 = (bf16[64,1024]{1,0:T(8,128)(2,1)S(1)}, bf16[64,1024]{1,0:T(8,128)(2,1)S(1)}, u32[]{:S(2)}, u32[]{:S(2)}) collective-permute-start(bf16[64,1024]{1,0:T(8,128)(2,1)S(1)} %get-tuple-element.80.refs_0_), channel_id=1, source_target_pairs={{4,20},{5,21},{6,22},{7,23},{8,16},{9,17},{10,18},{11,19}} | collective-permute-start | bytes 393224 | tf_op jit(solution)/shard_map/ppermute | solution.py:85
  28.7 12.4 %collective-permute-start.11 = (bf16[64,1024]{1,0:T(8,128)(2,1)S(1)}, bf16[64,1024]{1,0:T(8,128)(2,1)S(1)}, u32[]{:S(2)}, u32[]{:S(2)}) collective-permute-start(bf16[64,1024]{1,0:T(8,128)(2,1)S(1)} %get-tuple-element.80.refs_0_), channel_id=1, source_target_pairs={{4,12},{5,13},{6,14},{7,15},{8,0},{9,1},{10,2},{11,3}} | collective-permute-start | bytes 393224 | tf_op jit(solution)/shard_map/ppermute | solution.py:85
  38.2 14.0 %collective-permute-start.15 = (bf16[256,1024]{1,0:T(8,128)(2,1)S(1)}, bf16[256,1024]{1,0:T(8,128)(2,1)S(1)}, u32[]{:S(2)}, u32[]{:S(2)}) collective-permute-start(bf16[256,1024]{1,0:T(8,128)(2,1)S(1)} %get-tuple-element.64.refs_0_), channel_id=1, source_target_pairs={{26,27},{24,25}} | collective-permute-start | bytes 1572872 | tf_op jit(solution)/shard_map/ppermute | solution.py:85
  41.7 10.5 %collective-permute-start.16 = (bf16[256,1024]{1,0:T(8,128)(2,1)S(1)}, bf16[256,1024]{1,0:T(8,128)(2,1)S(1)}, u32[]{:S(2)}, u32[]{:S(2)}) collective-permute-start(bf16[256,1024]{1,0:T(8,128)(2,1)S(1)} %get-tuple-element.86.refs_2_), channel_id=1, source_target_pairs={{22,23},{20,21}} | collective-permute-start | bytes 1572872 | tf_op jit(solution)/shard_map/ppermute | solution.py:85
  42.4 9.8 %collective-permute-start.17 = (bf16[64,1024]{1,0:T(8,128)(2,1)S(1)}, bf16[64,1024]{1,0:T(8,128)(2,1)S(1)}, u32[]{:S(2)}, u32[]{:S(2)}) collective-permute-start(bf16[64,1024]{1,0:T(8,128)(2,1)S(1)} %get-tuple-element.93), channel_id=1, source_target_pairs={{0,4},{1,5},{2,6},{3,7},{4,0},{5,1},{6,2},{7,3},{8,12},{9,13},{10,... | collective-permute-start | bytes 393224 | tf_op jit(solution)/shard_map/ppermute | solution.py:85
  52.5 15.5 %collective-permute-start.18 = (bf16[2,64,1024]{2,1,0:T(8,128)(2,1)S(1)}, bf16[2,64,1024]{2,1,0:T(8,128)(2,1)S(1)}, u32[]{:S(2)}, u32[]{:S(2)}) collective-permute-start(bf16[2,64,1024]{2,1,0:T(8,128)(2,1)S(1)} %get-tuple-element.99), channel_id=1, source_target_pairs={{24,0},{25,1},{26,2},{27,3},{20,28},{21,29},{22,30},{23,31}} | collective-permute-start | bytes 786440 | tf_op jit(solution)/shard_map/ppermute | solution.py:85
  53.2 16.7 %collective-permute-start.19 = (bf16[2,64,1024]{2,1,0:T(8,128)(2,1)S(1)}, bf16[2,64,1024]{2,1,0:T(8,128)(2,1)S(1)}, u32[]{:S(2)}, u32[]{:S(2)}) collective-permute-start(bf16[2,64,1024]{2,1,0:T(8,128)(2,1)S(1)} %get-tuple-element.100), channel_id=1, source_target_pairs={{24,8},{25,9},{26,10},{27,11},{20,4},{21,5},{22,6},{23,7}} | collective-permute-start | bytes 786440 | tf_op jit(solution)/shard_map/ppermute | solution.py:85
  53.9 23.0 %collective-permute-start.20 = (bf16[2,64,1024]{2,1,0:T(8,128)(2,1)S(1)}, bf16[2,64,1024]{2,1,0:T(8,128)(2,1)S(1)}, u32[]{:S(2)}, u32[]{:S(2)}) collective-permute-start(bf16[2,64,1024]{2,1,0:T(8,128)(2,1)S(1)} %get-tuple-element.101), channel_id=1, source_target_pairs={{24,16},{25,17},{26,18},{27,19},{28,20},{29,21},{30,22},{31,23},{2... | collective-permute-start | bytes 786440 | tf_op jit(solution)/shard_map/ppermute | solution.py:85
  65.4 14.7 %collective-permute-start.21 = (bf16[64,1024]{1,0:T(8,128)(2,1)S(1)}, bf16[64,1024]{1,0:T(8,128)(2,1)S(1)}, u32[]{:S(2)}, u32[]{:S(2)}) collective-permute-start(bf16[64,1024]{1,0:T(8,128)(2,1)S(1)} %get-tuple-element.106), channel_id=1, source_target_pairs={{4,5},{5,6},{8,9},{9,10},{12,13},{13,14},{16,17},{17,18},{20,21},{... | collective-permute-start | bytes 393224 | tf_op jit(solution)/shard_map/ppermute | solution.py:85
  66.7 13.4 %collective-permute-start.22 = (bf16[64,1024]{1,0:T(8,128)(2,1)S(1)}, bf16[64,1024]{1,0:T(8,128)(2,1)S(1)}, u32[]{:S(2)}, u32[]{:S(2)}) collective-permute-start(bf16[64,1024]{1,0:T(8,128)(2,1)S(1)} %get-tuple-element.107), channel_id=1, source_target_pairs={{4,6},{5,7},{8,10},{9,11},{12,14},{13,15},{16,18},{17,19},{20,22},... | collective-permute-start | bytes 393224 | tf_op jit(solution)/shard_map/ppermute | solution.py:85
  68.0 12.1 %collective-permute-start.23 = (bf16[64,1024]{1,0:T(8,128)(2,1)S(1)}, bf16[64,1024]{1,0:T(8,128)(2,1)S(1)}, u32[]{:S(2)}, u32[]{:S(2)}) collective-permute-start(bf16[64,1024]{1,0:T(8,128)(2,1)S(1)} %get-tuple-element.108), channel_id=1, source_target_pairs={{4,7},{5,4},{8,11},{9,8},{12,15},{13,12},{16,19},{17,16},{20,23},{... | collective-permute-start | bytes 393224 | tf_op jit(solution)/shard_map/ppermute | solution.py:85
  77.2 5.3 %collective-permute-start.24 = (bf16[64,1024]{1,0:T(8,128)(2,1)S(1)}, bf16[64,1024]{1,0:T(8,128)(2,1)S(1)}, u32[]{:S(2)}, u32[]{:S(2)}) collective-permute-start(bf16[64,1024]{1,0:T(8,128)(2,1)S(1)} %get-tuple-element.110), channel_id=1, source_target_pairs={{0,4},{1,5},{2,6},{3,7},{4,0},{5,1},{6,2},{7,3},{8,12},{9,13},{10,... | collective-permute-start | bytes 393224 | tf_op jit(solution)/shard_map/ppermute | solution.py:85

commit v4 on v3

--- a/solution.py
+++ b/solution.py
@@ -20,7 +20,7 @@
 
 
 def flip(x):
-    return jnp.transpose(x.astype(F32))
+    return jnp.transpose(x).astype(F32)
 
 
 class Copies:
@@ -202,7 +202,7 @@
             v = vbuf[...]
             multiply(qbuf, v.astype(BF16), fbuf, last)
             done = [cp.start(qbuf.at[d], bq[d]) for d in range(pairs)]
-            done.append(cp.start(qbuf.at[pl.ds(0, pairs - 2)], e_out))
+            done.append(cp.start(qbuf.at[pl.ds(0, pairs - 1)], e_out))
             sbuf[...] = jnp.transpose(v)
             wait(done + [cp.start(sbuf, sol_out)])
 
@@ -216,7 +216,7 @@
     sol, sevens, *bq, tok = call(
         kernel7,
         [v7, factor],
-        [(tall, F32), ((pairs - 2,) + pair_piece, BF16)] + [(pair_piece, BF16)] * pairs,
+        [(tall, F32), ((pairs - 1,) + pair_piece, BF16)] + [(pair_piece, BF16)] * pairs,
         [((cb, NB, NB), BF16), (full, F32), ((pairs, 2, piece, NB), BF16), (tall, F32), ((wide, wide), F32)],
         3 + cb + pairs,
     )
@@ -390,7 +390,7 @@
         wait(fs)
         multiply(qbuf, v.astype(BF16), fbuf, row)
         if more is not None:
-            for d in range(pairs - 2):
+            for d in range(pairs - 1):
                 qbuf[d] = (qbuf[d].astype(F32) + more[1][d].astype(F32)).astype(BF16)
         done = [cp.start(qbuf.at[d], outs[t]) for d, t in to_slot.items()]
         sbuf[...] = jnp.transpose(v)
@@ -448,7 +448,7 @@
         kernel5,
         [t6_even, t6_odd, t5_even, t5_odd, sevens, factor, diag_inv, forward_values, sol] + bq + [y_other],
         [(tall, F32)] + [(pair_piece, BF16)] * pairs + [((share, NB), BF16)],
-        solve_scratch + [((pairs - 2,) + pair_piece, BF16)],
+        solve_scratch + [((pairs - 1,) + pair_piece, BF16)],
         5 + cb + pairs,
         aliases={8 + k: k for k in range(pairs + 2)},
         order=[tok, near_all],
@@ -457,7 +457,6 @@
     for t in range(pairs - 1):
         to = [d for d, k in slots.items() if k == t][0]
         pairs_t = [((last - 1, b), (2 * t, b)) for b in all_cols]
-        pairs_t += [((last, b), (2 * t + 1, b)) for b in all_cols if t == pairs - 2]
         scattered.append(send(bq[t], pairs_t + [((i, b), (2 * to + 1, b)) for b in all_cols]))
 
     far_all = lax.all_gather(y_other, "col", axis=0, tiled=True)
@@ -535,21 +534,17 @@
         def _():
             cp.start(own_q, bbuf).wait()
 
-        @pl.when(r == last - 2)
-        def _():
-            cp.start(refs[pairs - 2], bbuf).wait()
-
         @pl.when(lax.rem(r, 2) == 0)
         def _():
             obuf[...] = bbuf[0].astype(F32)
             pbuf[...] = bbuf[1]
 
-        @pl.when((lax.rem(r, 2) == 1) & (r < last - 2))
+        @pl.when((lax.rem(r, 2) == 1) & (r < last))
         def _():
             obuf[...] = fbuf[1].astype(F32)
             pbuf[...] = fbuf[0]
 
-        @pl.when((lax.rem(r, 2) == 1) & (r >= last - 2))
+        @pl.when(r == last)
         def _():
             obuf[...] = fbuf[1].astype(F32) + bbuf[1].astype(F32)
             pbuf[...] = (fbuf[0].astype(F32) + bbuf[0].astype(F32)).astype(BF16)

time: 84.1 us -> 83.6 us (level)
  no operation moved by 1% of the time
where the time goes in v4:
time: 83.6 us; the launch traced here: 83.1 us
  starting transfers between devices  26.7 us (32%)
  blocking collectives  23.8 us (28%)
  waiting for transfers between devices  17.6 us (21%)
  Pallas kernels  7.98 us (10%)
  local copies, waits for them, and re-layouts  4.35 us (5%)
  other arithmetic  1.52 us (2%)
  between operations  1.11 us (1%)
    ppermute x25, starting transfers between devices, send(): lax.ppermute(x, BOTH, [(a * cols + b, d * cols + e) for (a, b), (d, e) in...  26.7 us
    ppermute x25, waiting for transfers between devices, send(): lax.ppermute(x, BOTH, [(a * cols + b, d * cols + e) for (a, b), (d, e) in...  17.6 us
    all_gather x1, blocking collectives, local(): y0_all = lax.all_gather(y0_mine, 'col', axis=0, tiled=True)  8.78 us
    pallas_call x14, Pallas kernels, call(): pl.pallas_call(body, out_shape=[jax.ShapeDtypeStruct(s, d) for s, d in ou...  7.98 us
    all_gather x1, blocking collectives, local(): near_all = lax.all_gather(y_near, 'col', axis=0, tiled=True)  7.73 us
    all_gather x1, blocking collectives, local(): far_all = lax.all_gather(y_other, 'col', axis=0, tiled=True)  7.29 us
    unnamed x14, local copies, waits for them, and re-layouts  4.33 us
  transfers between devices with their start and end apart: 25, of which 5 were waited for; matrix products, arithmetic and copies ran while one was open for 1% of the time, Pallas kernels for 9%

profile of v4, /device:TPU:16, one launch (start us, length us, event | category | flops | bytes accessed | tf_op | source)
XLA Modules:
  0.0 83.1 jit_solution(697133206615016477)
XLA Ops:
  0.7 0.8 collective-permute-start
  2.2 1.3 %collective-permute-start.3 = (bf16[64,1024]{1,0:T(8,128)(2,1)}, bf16[64,1024]{1,0:T(8,128)(2,1)S(1)}, u32[]{:S(2)}, u32[]{:S(2)}) collective-permute-start(bf16[64,1024]{1,0:T(8,128)(2,1)} %get-tuple-element.59.refs_0_), channel_id=1, source_target_pairs={{0,16},{1,17},{2,18},{3,19}} | collective-permute-start | bytes 393224 | tf_op jit(solution)/shard_map/ppermute | solution.py:85
  4.2 0.7 collective-permute-start.1
  4.9 2.2 %copy-done = bf16[1024,2048]{1,0:T(8,128)(2,1)S(1)} copy-done((bf16[1024,2048]{1,0:T(8,128)(2,1)S(1)}, bf16[1024,2048]{1,0:T(8,128)(2,1)}, u32[]{:S(2)}) %copy-start) | copy-done | bytes 4194328
  7.1 1.2 %copy-done.5 = f32[256,1024]{1,0:T(8,128)S(1)} copy-done((f32[256,1024]{1,0:T(8,128)S(1)}, f32[256,1024]{1,0:T(8,128)}, u32[]{:S(2)}) %copy-start.5) | copy-done | bytes 1048600
  8.3 1.1 %shard_map.76 = (f32[1024,256]{1,0:T(8,128)}, bf16[3,2,64,1024]{3,2,1,0:T(8,128)(2,1)S(1)}, bf16[2,64,1024]{2,1,0:T(8,128)(2,1)S(1)}, bf16[2,64,1024]{2,1,0:T(8,...) custom-call(f32[256,1024]{1,0:T(8,128)S(1)} %copy-done.5, ...), custom_call_target="tpu_custom_call" | custom-call | tf_op jit(solution)/shard_map/pallas_call | solution.py:50
  9.4 5.4 %collective-permute-done.3.refs_2_ = bf16[64,1024]{1,0:T(8,128)(2,1)S(1)} collective-permute-done((bf16[64,1024]{1,0:T(8,128)(2,1)}, bf16[64,1024]{1,0:T(8,128)(2,1)S(1)}, u32[]{:S(2)}, u32[]{:S(2)}) %collective-permute-start.3) | collective-permute-done | bytes 131104 | tf_op jit(solution)/shard_map/ppermute | solution.py:85
  14.8 0.9 %copy-done.6 = bf16[64,1024]{1,0:T(8,128)(2,1)S(1)} copy-done((bf16[64,1024]{1,0:T(8,128)(2,1)S(1)}, bf16[64,1024]{1,0:T(8,128)(2,1)}, u32[]{:S(2)}) %copy-start.6) | copy-done | bytes 131096
  16.2 0.7 collective-permute-start.5
  16.9 0.7 collective-permute-start.14
  17.6 0.7 collective-permute-start.10
  18.3 4.8 %collective-permute-start.9 = (bf16[64,1024]{1,0:T(8,128)(2,1)S(1)}, bf16[64,1024]{1,0:T(8,128)(2,1)S(1)}, u32[]{:S(2)}, u32[]{:S(2)}) collective-permute-start(bf16[64,1024]{1,0:T(8,128)(2,1)S(1)} %get-tuple-element.75.refs_0_), channel_id=1, source_target_pairs={{0,4},{1,5},{2,6},{3,7},{12,8},{13,9},{14,10},{15,11},{16,20},{17,... | collective-permute-start | bytes 393224 | tf_op jit(solution)/shard_map/ppermute | solution.py:85
  24.6 1.0 %collective-permute-done.9.refs_1_ = bf16[64,1024]{1,0:T(8,128)(2,1)S(1)} collective-permute-done((bf16[64,1024]{1,0:T(8,128)(2,1)S(1)}, bf16[64,1024]{1,0:T(8,128)(2,1)S(1)}, u32[]{:S(2)}, u32[]{:S(2)}) %collective-permute-start.9) | collective-permute-done | bytes 131104 | tf_op jit(solution)/shard_map/ppermute | solution.py:85
  27.4 1.3 %collective-permute-start.12 = (bf16[64,1024]{1,0:T(8,128)(2,1)S(1)}, bf16[64,1024]{1,0:T(8,128)(2,1)S(1)}, u32[]{:S(2)}, u32[]{:S(2)}) collective-permute-start(bf16[64,1024]{1,0:T(8,128)(2,1)S(1)} %get-tuple-element.80.refs_0_), channel_id=1, source_target_pairs={{4,20},{5,21},{6,22},{7,23},{8,16},{9,17},{10,18},{11,19}} | collective-permute-start | bytes 393224 | tf_op jit(solution)/shard_map/ppermute | solution.py:85
  29.4 8.8 %all_gather.9.refs_5_.refs_0_ = bf16[256,1024]{1,0:T(8,128)(2,1)S(1)} all-gather(bf16[64,1024]{1,0:T(8,128)(2,1)S(1)} %get-tuple-element.79), channel_id=1, replica_groups=mesh['row'=8,'col'=4] {'col'}, dimensions={0}, use_global_device_ids=true | all-gather | bytes 655360 | tf_op jit(solution)/shard_map/all_gather | solution.py:353
  38.1 0.7 collective-permute-start.15
  38.8 2.2 %collective-permute-done.12.refs_2_ = bf16[64,1024]{1,0:T(8,128)(2,1)S(1)} collective-permute-done((bf16[64,1024]{1,0:T(8,128)(2,1)S(1)}, bf16[64,1024]{1,0:T(8,128)(2,1)S(1)}, u32[]{:S(2)}, u32[]{:S(2)}) %collective-permute-start.12) | collective-permute-done | bytes 131104 | tf_op jit(solution)/shard_map/ppermute | solution.py:85
  41.7 0.7 collective-permute-start.16
  42.4 2.2 %collective-permute-start.17 = (bf16[64,1024]{1,0:T(8,128)(2,1)S(1)}, bf16[64,1024]{1,0:T(8,128)(2,1)S(1)}, u32[]{:S(2)}, u32[]{:S(2)}) collective-permute-start(bf16[64,1024]{1,0:T(8,128)(2,1)S(1)} %get-tuple-element.93), channel_id=1, source_target_pairs={{0,4},{1,5},{2,6},{3,7},{4,0},{5,1},{6,2},{7,3},{8,12},{9,13},{10,... | collective-permute-start | bytes 393224 | tf_op jit(solution)/shard_map/ppermute | solution.py:85
  44.5 7.7 %all_gather.10.refs_15_.refs_1_ = bf16[256,1024]{1,0:T(8,128)(2,1)S(1)} all-gather(bf16[64,1024]{1,0:T(8,128)(2,1)S(1)} %get-tuple-element.85), channel_id=1, replica_groups=mesh['row'=8,'col'=4] {'col'}, dimensions={0}, use_global_device_ids=true | all-gather | bytes 655360 | tf_op jit(solution)/shard_map/all_gather | solution.py:428
  52.6 0.7 collective-permute-start.18
  53.9 1.3 %collective-permute-start.20 = (bf16[2,64,1024]{2,1,0:T(8,128)(2,1)S(1)}, bf16[2,64,1024]{2,1,0:T(8,128)(2,1)S(1)}, u32[]{:S(2)}, u32[]{:S(2)}) collective-permute-start(bf16[2,64,1024]{2,1,0:T(8,128)(2,1)S(1)} %get-tuple-element.101), channel_id=1, source_target_pairs={{24,16},{25,17},{26,18},{27,19},{20,12},{21,13},{22,14},{23,15}} | collective-permute-start | bytes 786440 | tf_op jit(solution)/shard_map/ppermute | solution.py:85
  55.2 7.3 %all_gather.11.refs_2_ = bf16[256,1024]{1,0:T(8,128)(2,1)S(1)} all-gather(bf16[64,1024]{1,0:T(8,128)(2,1)S(1)} %get-tuple-element.95), channel_id=1, replica_groups=mesh['row'=8,'col'=4] {'col'}, dimensions={0}, use_global_device_ids=true | all-gather | bytes 655360 | tf_op jit(solution)/shard_map/all_gather | solution.py:462
  62.5 2.9 %shard_map.86 = (bf16[64,1024]{1,0:T(8,128)(2,1)S(1)}, bf16[64,1024]{1,0:T(8,128)(2,1)S(1)}, bf16[64,1024]{1,0:T(8,128)(2,1)S(1)}, bf16[64,1024]{1,0:T(8,128)(2,1)S(1)}, f32[8,128]{1,0:T(8,128)S(1)}) custom-call(bf16[256,1024]{1,0:T(8,128)(2,1)S(1)} %all_gather.9.refs_5_.refs_0_, bf16[256,1024]{1,0:T(8,128)(2,1)S(1)} %all_gather.10.refs_15_.refs_1_, ...), custom_call_target="tpu_custom_call" | custom-call | tf_op jit(solution)/shard_map/pallas_call | solution.py:50
  65.4 1.3 %collective-permute-start.21 = (bf16[64,1024]{1,0:T(8,128)(2,1)S(1)}, bf16[64,1024]{1,0:T(8,128)(2,1)S(1)}, u32[]{:S(2)}, u32[]{:S(2)}) collective-permute-start(bf16[64,1024]{1,0:T(8,128)(2,1)S(1)} %get-tuple-element.106), channel_id=1, source_target_pairs={{4,5},{5,6},{8,9},{9,10},{12,13},{13,14},{16,17},{17,18},{20,21},{... | collective-permute-start | bytes 393224 | tf_op jit(solution)/shard_map/ppermute | solution.py:85
  66.7 1.3 %collective-permute-start.22 = (bf16[64,1024]{1,0:T(8,128)(2,1)S(1)}, bf16[64,1024]{1,0:T(8,128)(2,1)S(1)}, u32[]{:S(2)}, u32[]{:S(2)}) collective-permute-start(bf16[64,1024]{1,0:T(8,128)(2,1)S(1)} %get-tuple-element.107), channel_id=1, source_target_pairs={{4,6},{5,7},{8,10},{9,11},{12,14},{13,15},{16,18},{17,19},{20,22},... | collective-permute-start | bytes 393224 | tf_op jit(solution)/shard_map/ppermute | solution.py:85
  68.1 1.9 %collective-permute-start.23 = (bf16[64,1024]{1,0:T(8,128)(2,1)S(1)}, bf16[64,1024]{1,0:T(8,128)(2,1)S(1)}, u32[]{:S(2)}, u32[]{:S(2)}) collective-permute-start(bf16[64,1024]{1,0:T(8,128)(2,1)S(1)} %get-tuple-element.108), channel_id=1, source_target_pairs={{4,7},{5,4},{8,11},{9,8},{12,15},{13,12},{16,19},{17,16},{20,23},{... | collective-permute-start | bytes 393224 | tf_op jit(solution)/shard_map/ppermute | solution.py:85
  70.0 6.8 %collective-permute-done.20.refs_3_ = bf16[2,64,1024]{2,1,0:T(8,128)(2,1)S(1)} collective-permute-done((bf16[2,64,1024]{2,1,0:T(8,128)(2,1)S(1)}, bf16[2,64,1024]{2,1,0:T(8,128)(2,1)S(1)}, u32[]{:S(2)}, u32[]{:S(2)}) %collective-permute-start.20) | collective-permute-done | bytes 262176 | tf_op jit(solution)/shard_map/ppermute | solution.py:85
  77.5 1.8 %shard_map.88 = (bf16[3072,256]{1,0:T(8,128)(2,1)}, f32[64,1024]{1,0:T(8,128)S(1)}, f32[8,128]{1,0:T(8,128)}) custom-call(bf16[256,1024]{1,0:T(8,128)(2,1)S(1)} %all_gather.9.refs_5_.refs_0_, bf16[256,1024]{1,0:T(8,128)(2,1)S(1)} %all_gather.10.refs_15_.refs_1_, bf16[256,1024]{1,0:T(8,128)(2,1)S(1)} %all_gather.11.refs_2_, bf16[1024,256]{1,0:T(8,128)(2,1)S(1)} %copy-done.3, ...), custom_call_target="tpu_custom_call" | custom-call | tf_op jit(solution)/shard_map/pallas_call | solution.py:50
  79.4 0.8 subtract_bitcast_fusion
  80.1 2.2 %collective-permute-done.24 = bf16[64,1024]{1,0:T(8,128)(2,1)S(1)} collective-permute-done((bf16[64,1024]{1,0:T(8,128)(2,1)S(1)}, bf16[64,1024]{1,0:T(8,128)(2,1)S(1)}, u32[]{:S(2)}, u32[]{:S(2)}) %collective-permute-start.24) | collective-permute-done | bytes 131104 | tf_op jit(solution)/shard_map/ppermute | solution.py:85
  82.4 0.7 maximum_bitcast_fusion
  (53 shorter events, 8.1 us)
Async XLA Ops:
  0.6 15.4 %copy-start.2 = (bf16[1024,1024]{1,0:T(8,128)(2,1)S(1)}, bf16[1024,1024]{1,0:T(8,128)(2,1)}, u32[]{:S(2)}) copy-start(bf16[1024,1024]{1,0:T(8,128)(2,1)} %refs_6_.1) | copy-start | bytes 6291460
  0.7 15.3 %collective-permute-start = (bf16[256,1024]{1,0:T(8,128)(2,1)}, bf16[256,1024]{1,0:T(8,128)(2,1)S(1)}, u32[]{:S(2)}, u32[]{:S(2)}) collective-permute-start(bf16[256,1024]{1,0:T(8,128)(2,1)} %get-tuple-element.58), channel_id=1, source_target_pairs={{0,4},{31,26},{30,20}} | collective-permute-start | bytes 1572872 | tf_op jit(solution)/shard_map/ppermute | solution.py:85
  1.5 7.8 %collective-permute-start.4 = (bf16[64,1024]{1,0:T(8,128)(2,1)}, bf16[64,1024]{1,0:T(8,128)(2,1)S(1)}, u32[]{:S(2)}, u32[]{:S(2)}) collective-permute-start(bf16[64,1024]{1,0:T(8,128)(2,1)} %get-tuple-element.59.refs_0_), channel_id=1, source_target_pairs={{0,24},{1,25},{2,26},{3,27}} | collective-permute-start | bytes 393224 | tf_op jit(solution)/shard_map/ppermute | solution.py:85
  2.2 12.5 %collective-permute-start.3 = (bf16[64,1024]{1,0:T(8,128)(2,1)}, bf16[64,1024]{1,0:T(8,128)(2,1)S(1)}, u32[]{:S(2)}, u32[]{:S(2)}) collective-permute-start(bf16[64,1024]{1,0:T(8,128)(2,1)} %get-tuple-element.59.refs_0_), channel_id=1, source_target_pairs={{0,16},{1,17},{2,18},{3,19}} | collective-permute-start | bytes 393224 | tf_op jit(solution)/shard_map/ppermute | solution.py:85
  3.5 11.2 %collective-permute-start.2 = (bf16[64,1024]{1,0:T(8,128)(2,1)}, bf16[64,1024]{1,0:T(8,128)(2,1)S(1)}, u32[]{:S(2)}, u32[]{:S(2)}) collective-permute-start(bf16[64,1024]{1,0:T(8,128)(2,1)} %get-tuple-element.59.refs_0_), channel_id=1, source_target_pairs={{0,12},{1,13},{2,14},{3,15}} | collective-permute-start | bytes 393224 | tf_op jit(solution)/shard_map/ppermute | solution.py:85
  4.2 18.8 %collective-permute-start.1 = (bf16[256,1024]{1,0:T(8,128)(2,1)}, bf16[256,1024]{1,0:T(8,128)(2,1)S(1)}, u32[]{:S(2)}, u32[]{:S(2)}) collective-permute-start(bf16[256,1024]{1,0:T(8,128)(2,1)} %get-tuple-element.58), channel_id=1, source_target_pairs={{0,8},{31,24},{30,22}} | collective-permute-start | bytes 1572872 | tf_op jit(solution)/shard_map/ppermute | solution.py:85
  4.9 2.2 %copy-start = (bf16[1024,2048]{1,0:T(8,128)(2,1)S(1)}, bf16[1024,2048]{1,0:T(8,128)(2,1)}, u32[]{:S(2)}) copy-start(bf16[1024,2048]{1,0:T(8,128)(2,1)} %refs_3_.8) | copy-start | bytes 12582916
  7.1 1.2 %copy-start.5 = (f32[256,1024]{1,0:T(8,128)S(1)}, f32[256,1024]{1,0:T(8,128)}, u32[]{:S(2)}) copy-start(f32[256,1024]{1,0:T(8,128)} %get-tuple-element.60.refs_0_) | copy-start | bytes 3145732
  8.3 7.7 %copy-start.1 = (bf16[1024,2048]{1,0:T(8,128)(2,1)S(1)}, bf16[1024,2048]{1,0:T(8,128)(2,1)}, u32[]{:S(2)}) copy-start(bf16[1024,2048]{1,0:T(8,128)(2,1)} %refs_3_.8) | copy-start | bytes 12582916
  8.3 7.7 %copy-start.3 = (bf16[1024,256]{1,0:T(8,128)(2,1)S(1)}, bf16[1024,256]{1,0:T(8,128)(2,1)}, u32[]{:S(2)}) copy-start(bf16[1024,256]{1,0:T(8,128)(2,1)} %refs_3_.9) | copy-start | bytes 1572868
  8.3 7.7 %copy-start.4 = (bf16[1024,256]{1,0:T(8,128)(2,1)S(1)}, bf16[1024,256]{1,0:T(8,128)(2,1)}, u32[]{:S(2)}) copy-start(bf16[1024,256]{1,0:T(8,128)(2,1)} %refs_7_.1) | copy-start | bytes 1572868
  14.8 0.9 %copy-start.6 = (bf16[64,1024]{1,0:T(8,128)(2,1)S(1)}, bf16[64,1024]{1,0:T(8,128)(2,1)}, u32[]{:S(2)}) copy-start(bf16[64,1024]{1,0:T(8,128)(2,1)} %get-tuple-element.59.refs_0_) | copy-start | bytes 393220
  16.2 7.0 %collective-permute-start.5 = (bf16[256,1024]{1,0:T(8,128)(2,1)S(1)}, bf16[256,1024]{1,0:T(8,128)(2,1)S(1)}, u32[]{:S(2)}, u32[]{:S(2)}) collective-permute-start(bf16[256,1024]{1,0:T(8,128)(2,1)S(1)} %get-tuple-element.65), channel_id=1, source_target_pairs={{4,8},{26,22}} | collective-permute-start | bytes 1572872 | tf_op jit(solution)/shard_map/ppermute | solution.py:85
  16.9 24.7 %collective-permute-start.14 = (bf16[3,2,64,1024]{3,2,1,0:T(8,128)(2,1)S(1)}, bf16[3,2,64,1024]{3,2,1,0:T(8,128)(2,1)S(1)}, u32[]{:S(2)}, u32[]{:S(2)}) collective-permute-start(bf16[3,2,64,1024]{3,2,1,0:T(8,128)(2,1)S(1)} %get-tuple-element.83), channel_id=1, source_target_pairs={{28,20},{29,21},{30,22},{31,23}} | collective-permute-start | bytes 2359304 | tf_op jit(solution)/shard_map/ppermute | solution.py:85
  17.6 24.0 %collective-permute-start.10 = (bf16[256,1024]{1,0:T(8,128)(2,1)S(1)}, bf16[256,1024]{1,0:T(8,128)(2,1)S(1)}, u32[]{:S(2)}, u32[]{:S(2)}) collective-permute-start(bf16[256,1024]{1,0:T(8,128)(2,1)S(1)} %get-tuple-element.65), channel_id=1, source_target_pairs={{26,20}} | collective-permute-start | bytes 1572872 | tf_op jit(solution)/shard_map/ppermute | solution.py:85
  18.3 7.3 %collective-permute-start.9 = (bf16[64,1024]{1,0:T(8,128)(2,1)S(1)}, bf16[64,1024]{1,0:T(8,128)(2,1)S(1)}, u32[]{:S(2)}, u32[]{:S(2)}) collective-permute-start(bf16[64,1024]{1,0:T(8,128)(2,1)S(1)} %get-tuple-element.75.refs_0_), channel_id=1, source_target_pairs={{0,4},{1,5},{2,6},{3,7},{12,8},{13,9},{14,10},{15,11},{16,20},{17,... | collective-permute-start | bytes 393224 | tf_op jit(solution)/shard_map/ppermute | solution.py:85
  23.2 3.4 %collective-permute-start.6 = (bf16[64,1024]{1,0:T(8,128)(2,1)S(1)}, bf16[64,1024]{1,0:T(8,128)(2,1)S(1)}, u32[]{:S(2)}, u32[]{:S(2)}) collective-permute-start(bf16[64,1024]{1,0:T(8,128)(2,1)S(1)} %get-tuple-element.72), channel_id=1, source_target_pairs={{4,5},{8,9}} | collective-permute-start | bytes 393224 | tf_op jit(solution)/shard_map/ppermute | solution.py:85
  23.9 2.7 %collective-permute-start.7 = (bf16[64,1024]{1,0:T(8,128)(2,1)S(1)}, bf16[64,1024]{1,0:T(8,128)(2,1)S(1)}, u32[]{:S(2)}, u32[]{:S(2)}) collective-permute-start(bf16[64,1024]{1,0:T(8,128)(2,1)S(1)} %get-tuple-element.73), channel_id=1, source_target_pairs={{4,6},{8,10}} | collective-permute-start | bytes 393224 | tf_op jit(solution)/shard_map/ppermute | solution.py:85
  25.5 1.1 %collective-permute-start.8 = (bf16[64,1024]{1,0:T(8,128)(2,1)S(1)}, bf16[64,1024]{1,0:T(8,128)(2,1)S(1)}, u32[]{:S(2)}, u32[]{:S(2)}) collective-permute-start(bf16[64,1024]{1,0:T(8,128)(2,1)S(1)} %get-tuple-element.74), channel_id=1, source_target_pairs={{4,7},{8,11}} | collective-permute-start | bytes 393224 | tf_op jit(solution)/shard_map/ppermute | solution.py:85
  26.7 11.4 %collective-permute-start.13 = (bf16[64,1024]{1,0:T(8,128)(2,1)S(1)}, bf16[64,1024]{1,0:T(8,128)(2,1)S(1)}, u32[]{:S(2)}, u32[]{:S(2)}) collective-permute-start(bf16[64,1024]{1,0:T(8,128)(2,1)S(1)} %get-tuple-element.80.refs_0_), channel_id=1, source_target_pairs={{4,28},{5,29},{6,30},{7,31},{8,24},{9,25},{10,26},{11,27}} | collective-permute-start | bytes 393224 | tf_op jit(solution)/shard_map/ppermute | solution.py:85
  27.4 13.7 %collective-permute-start.12 = (bf16[64,1024]{1,0:T(8,128)(2,1)S(1)}, bf16[64,1024]{1,0:T(8,128)(2,1)S(1)}, u32[]{:S(2)}, u32[]{:S(2)}) collective-permute-start(bf16[64,1024]{1,0:T(8,128)(2,1)S(1)} %get-tuple-element.80.refs_0_), channel_id=1, source_target_pairs={{4,20},{5,21},{6,22},{7,23},{8,16},{9,17},{10,18},{11,19}} | collective-permute-start | bytes 393224 | tf_op jit(solution)/shard_map/ppermute | solution.py:85
  28.7 12.4 %collective-permute-start.11 = (bf16[64,1024]{1,0:T(8,128)(2,1)S(1)}, bf16[64,1024]{1,0:T(8,128)(2,1)S(1)}, u32[]{:S(2)}, u32[]{:S(2)}) collective-permute-start(bf16[64,1024]{1,0:T(8,128)(2,1)S(1)} %get-tuple-element.80.refs_0_), channel_id=1, source_target_pairs={{4,12},{5,13},{6,14},{7,15},{8,0},{9,1},{10,2},{11,3}} | collective-permute-start | bytes 393224 | tf_op jit(solution)/shard_map/ppermute | solution.py:85
  38.1 14.1 %collective-permute-start.15 = (bf16[256,1024]{1,0:T(8,128)(2,1)S(1)}, bf16[256,1024]{1,0:T(8,128)(2,1)S(1)}, u32[]{:S(2)}, u32[]{:S(2)}) collective-permute-start(bf16[256,1024]{1,0:T(8,128)(2,1)S(1)} %get-tuple-element.64.refs_0_), channel_id=1, source_target_pairs={{26,27},{24,25}} | collective-permute-start | bytes 1572872 | tf_op jit(solution)/shard_map/ppermute | solution.py:85
  41.7 10.6 %collective-permute-start.16 = (bf16[256,1024]{1,0:T(8,128)(2,1)S(1)}, bf16[256,1024]{1,0:T(8,128)(2,1)S(1)}, u32[]{:S(2)}, u32[]{:S(2)}) collective-permute-start(bf16[256,1024]{1,0:T(8,128)(2,1)S(1)} %get-tuple-element.86.refs_2_), channel_id=1, source_target_pairs={{22,23},{20,21}} | collective-permute-start | bytes 1572872 | tf_op jit(solution)/shard_map/ppermute | solution.py:85
  42.4 9.9 %collective-permute-start.17 = (bf16[64,1024]{1,0:T(8,128)(2,1)S(1)}, bf16[64,1024]{1,0:T(8,128)(2,1)S(1)}, u32[]{:S(2)}, u32[]{:S(2)}) collective-permute-start(bf16[64,1024]{1,0:T(8,128)(2,1)S(1)} %get-tuple-element.93), channel_id=1, source_target_pairs={{0,4},{1,5},{2,6},{3,7},{4,0},{5,1},{6,2},{7,3},{8,12},{9,13},{10,... | collective-permute-start | bytes 393224 | tf_op jit(solution)/shard_map/ppermute | solution.py:85
  52.6 15.5 %collective-permute-start.18 = (bf16[2,64,1024]{2,1,0:T(8,128)(2,1)S(1)}, bf16[2,64,1024]{2,1,0:T(8,128)(2,1)S(1)}, u32[]{:S(2)}, u32[]{:S(2)}) collective-permute-start(bf16[2,64,1024]{2,1,0:T(8,128)(2,1)S(1)} %get-tuple-element.99), channel_id=1, source_target_pairs={{24,0},{25,1},{26,2},{27,3},{20,28},{21,29},{22,30},{23,31}} | collective-permute-start | bytes 786440 | tf_op jit(solution)/shard_map/ppermute | solution.py:85
  53.3 16.7 %collective-permute-start.19 = (bf16[2,64,1024]{2,1,0:T(8,128)(2,1)S(1)}, bf16[2,64,1024]{2,1,0:T(8,128)(2,1)S(1)}, u32[]{:S(2)}, u32[]{:S(2)}) collective-permute-start(bf16[2,64,1024]{2,1,0:T(8,128)(2,1)S(1)} %get-tuple-element.100), channel_id=1, source_target_pairs={{24,8},{25,9},{26,10},{27,11},{20,4},{21,5},{22,6},{23,7}} | collective-permute-start | bytes 786440 | tf_op jit(solution)/shard_map/ppermute | solution.py:85
  53.9 22.9 %collective-permute-start.20 = (bf16[2,64,1024]{2,1,0:T(8,128)(2,1)S(1)}, bf16[2,64,1024]{2,1,0:T(8,128)(2,1)S(1)}, u32[]{:S(2)}, u32[]{:S(2)}) collective-permute-start(bf16[2,64,1024]{2,1,0:T(8,128)(2,1)S(1)} %get-tuple-element.101), channel_id=1, source_target_pairs={{24,16},{25,17},{26,18},{27,19},{20,12},{21,13},{22,14},{23,15}} | collective-permute-start | bytes 786440 | tf_op jit(solution)/shard_map/ppermute | solution.py:85
  65.4 13.9 %collective-permute-start.21 = (bf16[64,1024]{1,0:T(8,128)(2,1)S(1)}, bf16[64,1024]{1,0:T(8,128)(2,1)S(1)}, u32[]{:S(2)}, u32[]{:S(2)}) collective-permute-start(bf16[64,1024]{1,0:T(8,128)(2,1)S(1)} %get-tuple-element.106), channel_id=1, source_target_pairs={{4,5},{5,6},{8,9},{9,10},{12,13},{13,14},{16,17},{17,18},{20,21},{... | collective-permute-start | bytes 393224 | tf_op jit(solution)/shard_map/ppermute | solution.py:85
  66.7 12.6 %collective-permute-start.22 = (bf16[64,1024]{1,0:T(8,128)(2,1)S(1)}, bf16[64,1024]{1,0:T(8,128)(2,1)S(1)}, u32[]{:S(2)}, u32[]{:S(2)}) collective-permute-start(bf16[64,1024]{1,0:T(8,128)(2,1)S(1)} %get-tuple-element.107), channel_id=1, source_target_pairs={{4,6},{5,7},{8,10},{9,11},{12,14},{13,15},{16,18},{17,19},{20,22},... | collective-permute-start | bytes 393224 | tf_op jit(solution)/shard_map/ppermute | solution.py:85
  68.1 11.3 %collective-permute-start.23 = (bf16[64,1024]{1,0:T(8,128)(2,1)S(1)}, bf16[64,1024]{1,0:T(8,128)(2,1)S(1)}, u32[]{:S(2)}, u32[]{:S(2)}) collective-permute-start(bf16[64,1024]{1,0:T(8,128)(2,1)S(1)} %get-tuple-element.108), channel_id=1, source_target_pairs={{4,7},{5,4},{8,11},{9,8},{12,15},{13,12},{16,19},{17,16},{20,23},{... | collective-permute-start | bytes 393224 | tf_op jit(solution)/shard_map/ppermute | solution.py:85
  77.1 5.2 %collective-permute-start.24 = (bf16[64,1024]{1,0:T(8,128)(2,1)S(1)}, bf16[64,1024]{1,0:T(8,128)(2,1)S(1)}, u32[]{:S(2)}, u32[]{:S(2)}) collective-permute-start(bf16[64,1024]{1,0:T(8,128)(2,1)S(1)} %get-tuple-element.110), channel_id=1, source_target_pairs={{0,4},{1,5},{2,6},{3,7},{4,0},{5,1},{6,2},{7,3},{8,12},{9,13},{10,... | collective-permute-start | bytes 393224 | tf_op jit(solution)/shard_map/ppermute | solution.py:85

commit v5 on v4

--- a/solution.py
+++ b/solution.py
@@ -456,7 +456,7 @@
     scattered = []
     for t in range(pairs - 1):
         to = [d for d, k in slots.items() if k == t][0]
-        pairs_t = [((last - 1, b), (2 * t, b)) for b in all_cols]
+        pairs_t = [((last - 1, b), (2 * t, b)) for b in all_cols if b * cb < last - 1]
         scattered.append(send(bq[t], pairs_t + [((i, b), (2 * to + 1, b)) for b in all_cols]))
 
     far_all = lax.all_gather(y_other, "col", axis=0, tiled=True)

time: 83.6 us -> 83.6 us (level)
  no operation moved by 1% of the time
where the time goes in v5:
time: 83.6 us; the launch traced here: 83.1 us
  starting transfers between devices  26.7 us (32%)
  blocking collectives  23.8 us (28%)
  waiting for transfers between devices  17.6 us (21%)
  Pallas kernels  7.98 us (10%)
  local copies, waits for them, and re-layouts  4.35 us (5%)
  other arithmetic  1.52 us (2%)
  between operations  1.11 us (1%)
    ppermute x25, starting transfers between devices, send(): lax.ppermute(x, BOTH, [(a * cols + b, d * cols + e) for (a, b), (d, e) in...  26.7 us
    ppermute x25, waiting for transfers between devices, send(): lax.ppermute(x, BOTH, [(a * cols + b, d * cols + e) for (a, b), (d, e) in...  17.6 us
    all_gather x1, blocking collectives, local(): y0_all = lax.all_gather(y0_mine, 'col', axis=0, tiled=True)  8.78 us
    pallas_call x14, Pallas kernels, call(): pl.pallas_call(body, out_shape=[jax.ShapeDtypeStruct(s, d) for s, d in ou...  7.98 us
    all_gather x1, blocking collectives, local(): near_all = lax.all_gather(y_near, 'col', axis=0, tiled=True)  7.73 us
    all_gather x1, blocking collectives, local(): far_all = lax.all_gather(y_other, 'col', axis=0, tiled=True)  7.29 us
    unnamed x14, local copies, waits for them, and re-layouts  4.33 us
  transfers between devices with their start and end apart: 25, of which 5 were waited for; matrix products, arithmetic and copies ran while one was open for 1% of the time, Pallas kernels for 9%

profile of v5, /device:TPU:16, one launch (start us, length us, event | category | flops | bytes accessed | tf_op | source)
XLA Modules:
  0.0 83.1 jit_solution(11568994918625321962)
XLA Ops:
  0.7 0.8 collective-permute-start
  2.2 1.3 %collective-permute-start.3 = (bf16[64,1024]{1,0:T(8,128)(2,1)}, bf16[64,1024]{1,0:T(8,128)(2,1)S(1)}, u32[]{:S(2)}, u32[]{:S(2)}) collective-permute-start(bf16[64,1024]{1,0:T(8,128)(2,1)} %get-tuple-element.59.refs_0_), channel_id=1, source_target_pairs={{0,16},{1,17},{2,18},{3,19}} | collective-permute-start | bytes 393224 | tf_op jit(solution)/shard_map/ppermute | solution.py:85
  4.2 0.7 collective-permute-start.1
  4.9 2.2 %copy-done = bf16[1024,2048]{1,0:T(8,128)(2,1)S(1)} copy-done((bf16[1024,2048]{1,0:T(8,128)(2,1)S(1)}, bf16[1024,2048]{1,0:T(8,128)(2,1)}, u32[]{:S(2)}) %copy-start) | copy-done | bytes 4194328
  7.1 1.2 %copy-done.5 = f32[256,1024]{1,0:T(8,128)S(1)} copy-done((f32[256,1024]{1,0:T(8,128)S(1)}, f32[256,1024]{1,0:T(8,128)}, u32[]{:S(2)}) %copy-start.5) | copy-done | bytes 1048600
  8.3 1.1 %shard_map.76 = (f32[1024,256]{1,0:T(8,128)}, bf16[3,2,64,1024]{3,2,1,0:T(8,128)(2,1)S(1)}, bf16[2,64,1024]{2,1,0:T(8,128)(2,1)S(1)}, bf16[2,64,1024]{2,1,0:T(8,...) custom-call(f32[256,1024]{1,0:T(8,128)S(1)} %copy-done.5, ...), custom_call_target="tpu_custom_call" | custom-call | tf_op jit(solution)/shard_map/pallas_call | solution.py:50
  9.4 5.4 %collective-permute-done.3.refs_2_ = bf16[64,1024]{1,0:T(8,128)(2,1)S(1)} collective-permute-done((bf16[64,1024]{1,0:T(8,128)(2,1)}, bf16[64,1024]{1,0:T(8,128)(2,1)S(1)}, u32[]{:S(2)}, u32[]{:S(2)}) %collective-permute-start.3) | collective-permute-done | bytes 131104 | tf_op jit(solution)/shard_map/ppermute | solution.py:85
  14.8 0.9 %copy-done.6 = bf16[64,1024]{1,0:T(8,128)(2,1)S(1)} copy-done((bf16[64,1024]{1,0:T(8,128)(2,1)S(1)}, bf16[64,1024]{1,0:T(8,128)(2,1)}, u32[]{:S(2)}) %copy-start.6) | copy-done | bytes 131096
  16.2 0.7 collective-permute-start.5
  16.9 0.7 collective-permute-start.14
  17.6 0.7 collective-permute-start.10
  18.3 4.8 %collective-permute-start.9 = (bf16[64,1024]{1,0:T(8,128)(2,1)S(1)}, bf16[64,1024]{1,0:T(8,128)(2,1)S(1)}, u32[]{:S(2)}, u32[]{:S(2)}) collective-permute-start(bf16[64,1024]{1,0:T(8,128)(2,1)S(1)} %get-tuple-element.75.refs_0_), channel_id=1, source_target_pairs={{0,4},{1,5},{2,6},{3,7},{12,8},{13,9},{14,10},{15,11},{16,20},{17,... | collective-permute-start | bytes 393224 | tf_op jit(solution)/shard_map/ppermute | solution.py:85
  24.6 1.0 %collective-permute-done.9.refs_1_ = bf16[64,1024]{1,0:T(8,128)(2,1)S(1)} collective-permute-done((bf16[64,1024]{1,0:T(8,128)(2,1)S(1)}, bf16[64,1024]{1,0:T(8,128)(2,1)S(1)}, u32[]{:S(2)}, u32[]{:S(2)}) %collective-permute-start.9) | collective-permute-done | bytes 131104 | tf_op jit(solution)/shard_map/ppermute | solution.py:85
  27.4 1.3 %collective-permute-start.12 = (bf16[64,1024]{1,0:T(8,128)(2,1)S(1)}, bf16[64,1024]{1,0:T(8,128)(2,1)S(1)}, u32[]{:S(2)}, u32[]{:S(2)}) collective-permute-start(bf16[64,1024]{1,0:T(8,128)(2,1)S(1)} %get-tuple-element.80.refs_0_), channel_id=1, source_target_pairs={{4,20},{5,21},{6,22},{7,23},{8,16},{9,17},{10,18},{11,19}} | collective-permute-start | bytes 393224 | tf_op jit(solution)/shard_map/ppermute | solution.py:85
  29.4 8.8 %all_gather.9.refs_5_.refs_0_ = bf16[256,1024]{1,0:T(8,128)(2,1)S(1)} all-gather(bf16[64,1024]{1,0:T(8,128)(2,1)S(1)} %get-tuple-element.79), channel_id=1, replica_groups=mesh['row'=8,'col'=4] {'col'}, dimensions={0}, use_global_device_ids=true | all-gather | bytes 655360 | tf_op jit(solution)/shard_map/all_gather | solution.py:353
  38.1 0.7 collective-permute-start.15
  38.8 2.2 %collective-permute-done.12.refs_2_ = bf16[64,1024]{1,0:T(8,128)(2,1)S(1)} collective-permute-done((bf16[64,1024]{1,0:T(8,128)(2,1)S(1)}, bf16[64,1024]{1,0:T(8,128)(2,1)S(1)}, u32[]{:S(2)}, u32[]{:S(2)}) %collective-permute-start.12) | collective-permute-done | bytes 131104 | tf_op jit(solution)/shard_map/ppermute | solution.py:85
  41.7 0.7 collective-permute-start.16
  42.4 2.2 %collective-permute-start.17 = (bf16[64,1024]{1,0:T(8,128)(2,1)S(1)}, bf16[64,1024]{1,0:T(8,128)(2,1)S(1)}, u32[]{:S(2)}, u32[]{:S(2)}) collective-permute-start(bf16[64,1024]{1,0:T(8,128)(2,1)S(1)} %get-tuple-element.93), channel_id=1, source_target_pairs={{0,4},{1,5},{2,6},{3,7},{4,0},{5,1},{6,2},{7,3},{8,12},{9,13},{10,... | collective-permute-start | bytes 393224 | tf_op jit(solution)/shard_map/ppermute | solution.py:85
  44.5 7.7 %all_gather.10.refs_15_.refs_1_ = bf16[256,1024]{1,0:T(8,128)(2,1)S(1)} all-gather(bf16[64,1024]{1,0:T(8,128)(2,1)S(1)} %get-tuple-element.85), channel_id=1, replica_groups=mesh['row'=8,'col'=4] {'col'}, dimensions={0}, use_global_device_ids=true | all-gather | bytes 655360 | tf_op jit(solution)/shard_map/all_gather | solution.py:428
  52.6 0.7 collective-permute-start.18
  53.9 1.3 %collective-permute-start.20 = (bf16[2,64,1024]{2,1,0:T(8,128)(2,1)S(1)}, bf16[2,64,1024]{2,1,0:T(8,128)(2,1)S(1)}, u32[]{:S(2)}, u32[]{:S(2)}) collective-permute-start(bf16[2,64,1024]{2,1,0:T(8,128)(2,1)S(1)} %get-tuple-element.101), channel_id=1, source_target_pairs={{24,16},{25,17},{26,18},{20,12},{21,13},{22,14},{23,15}} | collective-permute-start | bytes 786440 | tf_op jit(solution)/shard_map/ppermute | solution.py:85
  55.2 7.3 %all_gather.11.refs_2_ = bf16[256,1024]{1,0:T(8,128)(2,1)S(1)} all-gather(bf16[64,1024]{1,0:T(8,128)(2,1)S(1)} %get-tuple-element.95), channel_id=1, replica_groups=mesh['row'=8,'col'=4] {'col'}, dimensions={0}, use_global_device_ids=true | all-gather | bytes 655360 | tf_op jit(solution)/shard_map/all_gather | solution.py:462
  62.5 2.9 %shard_map.86 = (bf16[64,1024]{1,0:T(8,128)(2,1)S(1)}, bf16[64,1024]{1,0:T(8,128)(2,1)S(1)}, bf16[64,1024]{1,0:T(8,128)(2,1)S(1)}, bf16[64,1024]{1,0:T(8,128)(2,1)S(1)}, f32[8,128]{1,0:T(8,128)S(1)}) custom-call(bf16[256,1024]{1,0:T(8,128)(2,1)S(1)} %all_gather.9.refs_5_.refs_0_, bf16[256,1024]{1,0:T(8,128)(2,1)S(1)} %all_gather.10.refs_15_.refs_1_, ...), custom_call_target="tpu_custom_call" | custom-call | tf_op jit(solution)/shard_map/pallas_call | solution.py:50
  65.4 1.3 %collective-permute-start.21 = (bf16[64,1024]{1,0:T(8,128)(2,1)S(1)}, bf16[64,1024]{1,0:T(8,128)(2,1)S(1)}, u32[]{:S(2)}, u32[]{:S(2)}) collective-permute-start(bf16[64,1024]{1,0:T(8,128)(2,1)S(1)} %get-tuple-element.106), channel_id=1, source_target_pairs={{4,5},{5,6},{8,9},{9,10},{12,13},{13,14},{16,17},{17,18},{20,21},{... | collective-permute-start | bytes 393224 | tf_op jit(solution)/shard_map/ppermute | solution.py:85
  66.7 1.3 %collective-permute-start.22 = (bf16[64,1024]{1,0:T(8,128)(2,1)S(1)}, bf16[64,1024]{1,0:T(8,128)(2,1)S(1)}, u32[]{:S(2)}, u32[]{:S(2)}) collective-permute-start(bf16[64,1024]{1,0:T(8,128)(2,1)S(1)} %get-tuple-element.107), channel_id=1, source_target_pairs={{4,6},{5,7},{8,10},{9,11},{12,14},{13,15},{16,18},{17,19},{20,22},... | collective-permute-start | bytes 393224 | tf_op jit(solution)/shard_map/ppermute | solution.py:85
  68.1 1.9 %collective-permute-start.23 = (bf16[64,1024]{1,0:T(8,128)(2,1)S(1)}, bf16[64,1024]{1,0:T(8,128)(2,1)S(1)}, u32[]{:S(2)}, u32[]{:S(2)}) collective-permute-start(bf16[64,1024]{1,0:T(8,128)(2,1)S(1)} %get-tuple-element.108), channel_id=1, source_target_pairs={{4,7},{5,4},{8,11},{9,8},{12,15},{13,12},{16,19},{17,16},{20,23},{... | collective-permute-start | bytes 393224 | tf_op jit(solution)/shard_map/ppermute | solution.py:85
  70.0 6.8 %collective-permute-done.20.refs_3_ = bf16[2,64,1024]{2,1,0:T(8,128)(2,1)S(1)} collective-permute-done((bf16[2,64,1024]{2,1,0:T(8,128)(2,1)S(1)}, bf16[2,64,1024]{2,1,0:T(8,128)(2,1)S(1)}, u32[]{:S(2)}, u32[]{:S(2)}) %collective-permute-start.20) | collective-permute-done | bytes 262176 | tf_op jit(solution)/shard_map/ppermute | solution.py:85
  77.5 1.8 %shard_map.88 = (bf16[3072,256]{1,0:T(8,128)(2,1)}, f32[64,1024]{1,0:T(8,128)S(1)}, f32[8,128]{1,0:T(8,128)}) custom-call(bf16[256,1024]{1,0:T(8,128)(2,1)S(1)} %all_gather.9.refs_5_.refs_0_, bf16[256,1024]{1,0:T(8,128)(2,1)S(1)} %all_gather.10.refs_15_.refs_1_, bf16[256,1024]{1,0:T(8,128)(2,1)S(1)} %all_gather.11.refs_2_, bf16[1024,256]{1,0:T(8,128)(2,1)S(1)} %copy-done.3, ...), custom_call_target="tpu_custom_call" | custom-call | tf_op jit(solution)/shard_map/pallas_call | solution.py:50
  79.4 0.8 subtract_bitcast_fusion
  80.1 2.2 %collective-permute-done.24 = bf16[64,1024]{1,0:T(8,128)(2,1)S(1)} collective-permute-done((bf16[64,1024]{1,0:T(8,128)(2,1)S(1)}, bf16[64,1024]{1,0:T(8,128)(2,1)S(1)}, u32[]{:S(2)}, u32[]{:S(2)}) %collective-permute-start.24) | collective-permute-done | bytes 131104 | tf_op jit(solution)/shard_map/ppermute | solution.py:85
  82.4 0.7 maximum_bitcast_fusion
  (53 shorter events, 8.1 us)
Async XLA Ops:
  0.6 15.4 %copy-start.2 = (bf16[1024,1024]{1,0:T(8,128)(2,1)S(1)}, bf16[1024,1024]{1,0:T(8,128)(2,1)}, u32[]{:S(2)}) copy-start(bf16[1024,1024]{1,0:T(8,128)(2,1)} %refs_6_.1) | copy-start | bytes 6291460
  0.7 15.3 %collective-permute-start = (bf16[256,1024]{1,0:T(8,128)(2,1)}, bf16[256,1024]{1,0:T(8,128)(2,1)S(1)}, u32[]{:S(2)}, u32[]{:S(2)}) collective-permute-start(bf16[256,1024]{1,0:T(8,128)(2,1)} %get-tuple-element.58), channel_id=1, source_target_pairs={{0,4},{31,26},{30,20}} | collective-permute-start | bytes 1572872 | tf_op jit(solution)/shard_map/ppermute | solution.py:85
  1.5 7.8 %collective-permute-start.4 = (bf16[64,1024]{1,0:T(8,128)(2,1)}, bf16[64,1024]{1,0:T(8,128)(2,1)S(1)}, u32[]{:S(2)}, u32[]{:S(2)}) collective-permute-start(bf16[64,1024]{1,0:T(8,128)(2,1)} %get-tuple-element.59.refs_0_), channel_id=1, source_target_pairs={{0,24},{1,25},{2,26},{3,27}} | collective-permute-start | bytes 393224 | tf_op jit(solution)/shard_map/ppermute | solution.py:85
  2.2 12.5 %collective-permute-start.3 = (bf16[64,1024]{1,0:T(8,128)(2,1)}, bf16[64,1024]{1,0:T(8,128)(2,1)S(1)}, u32[]{:S(2)}, u32[]{:S(2)}) collective-permute-start(bf16[64,1024]{1,0:T(8,128)(2,1)} %get-tuple-element.59.refs_0_), channel_id=1, source_target_pairs={{0,16},{1,17},{2,18},{3,19}} | collective-permute-start | bytes 393224 | tf_op jit(solution)/shard_map/ppermute | solution.py:85
  3.5 11.2 %collective-permute-start.2 = (bf16[64,1024]{1,0:T(8,128)(2,1)}, bf16[64,1024]{1,0:T(8,128)(2,1)S(1)}, u32[]{:S(2)}, u32[]{:S(2)}) collective-permute-start(bf16[64,1024]{1,0:T(8,128)(2,1)} %get-tuple-element.59.refs_0_), channel_id=1, source_target_pairs={{0,12},{1,13},{2,14},{3,15}} | collective-permute-start | bytes 393224 | tf_op jit(solution)/shard_map/ppermute | solution.py:85
  4.2 18.8 %collective-permute-start.1 = (bf16[256,1024]{1,0:T(8,128)(2,1)}, bf16[256,1024]{1,0:T(8,128)(2,1)S(1)}, u32[]{:S(2)}, u32[]{:S(2)}) collective-permute-start(bf16[256,1024]{1,0:T(8,128)(2,1)} %get-tuple-element.58), channel_id=1, source_target_pairs={{0,8},{31,24},{30,22}} | collective-permute-start | bytes 1572872 | tf_op jit(solution)/shard_map/ppermute | solution.py:85
  4.9 2.2 %copy-start = (bf16[1024,2048]{1,0:T(8,128)(2,1)S(1)}, bf16[1024,2048]{1,0:T(8,128)(2,1)}, u32[]{:S(2)}) copy-start(bf16[1024,2048]{1,0:T(8,128)(2,1)} %refs_3_.8) | copy-start | bytes 12582916
  7.1 1.2 %copy-start.5 = (f32[256,1024]{1,0:T(8,128)S(1)}, f32[256,1024]{1,0:T(8,128)}, u32[]{:S(2)}) copy-start(f32[256,1024]{1,0:T(8,128)} %get-tuple-element.60.refs_0_) | copy-start | bytes 3145732
  8.3 7.7 %copy-start.1 = (bf16[1024,2048]{1,0:T(8,128)(2,1)S(1)}, bf16[1024,2048]{1,0:T(8,128)(2,1)}, u32[]{:S(2)}) copy-start(bf16[1024,2048]{1,0:T(8,128)(2,1)} %refs_3_.8) | copy-start | bytes 12582916
  8.3 7.7 %copy-start.3 = (bf16[1024,256]{1,0:T(8,128)(2,1)S(1)}, bf16[1024,256]{1,0:T(8,128)(2,1)}, u32[]{:S(2)}) copy-start(bf16[1024,256]{1,0:T(8,128)(2,1)} %refs_3_.9) | copy-start | bytes 1572868
  8.3 7.7 %copy-start.4 = (bf16[1024,256]{1,0:T(8,128)(2,1)S(1)}, bf16[1024,256]{1,0:T(8,128)(2,1)}, u32[]{:S(2)}) copy-start(bf16[1024,256]{1,0:T(8,128)(2,1)} %refs_7_.1) | copy-start | bytes 1572868
  14.8 0.9 %copy-start.6 = (bf16[64,1024]{1,0:T(8,128)(2,1)S(1)}, bf16[64,1024]{1,0:T(8,128)(2,1)}, u32[]{:S(2)}) copy-start(bf16[64,1024]{1,0:T(8,128)(2,1)} %get-tuple-element.59.refs_0_) | copy-start | bytes 393220
  16.2 7.0 %collective-permute-start.5 = (bf16[256,1024]{1,0:T(8,128)(2,1)S(1)}, bf16[256,1024]{1,0:T(8,128)(2,1)S(1)}, u32[]{:S(2)}, u32[]{:S(2)}) collective-permute-start(bf16[256,1024]{1,0:T(8,128)(2,1)S(1)} %get-tuple-element.65), channel_id=1, source_target_pairs={{4,8},{26,22}} | collective-permute-start | bytes 1572872 | tf_op jit(solution)/shard_map/ppermute | solution.py:85
  16.9 24.7 %collective-permute-start.14 = (bf16[3,2,64,1024]{3,2,1,0:T(8,128)(2,1)S(1)}, bf16[3,2,64,1024]{3,2,1,0:T(8,128)(2,1)S(1)}, u32[]{:S(2)}, u32[]{:S(2)}) collective-permute-start(bf16[3,2,64,1024]{3,2,1,0:T(8,128)(2,1)S(1)} %get-tuple-element.83), channel_id=1, source_target_pairs={{28,20},{29,21},{30,22},{31,23}} | collective-permute-start | bytes 2359304 | tf_op jit(solution)/shard_map/ppermute | solution.py:85
  17.6 24.0 %collective-permute-start.10 = (bf16[256,1024]{1,0:T(8,128)(2,1)S(1)}, bf16[256,1024]{1,0:T(8,128)(2,1)S(1)}, u32[]{:S(2)}, u32[]{:S(2)}) collective-permute-start(bf16[256,1024]{1,0:T(8,128)(2,1)S(1)} %get-tuple-element.65), channel_id=1, source_target_pairs={{26,20}} | collective-permute-start | bytes 1572872 | tf_op jit(solution)/shard_map/ppermute | solution.py:85
  18.3 7.3 %collective-permute-start.9 = (bf16[64,1024]{1,0:T(8,128)(2,1)S(1)}, bf16[64,1024]{1,0:T(8,128)(2,1)S(1)}, u32[]{:S(2)}, u32[]{:S(2)}) collective-permute-start(bf16[64,1024]{1,0:T(8,128)(2,1)S(1)} %get-tuple-element.75.refs_0_), channel_id=1, source_target_pairs={{0,4},{1,5},{2,6},{3,7},{12,8},{13,9},{14,10},{15,11},{16,20},{17,... | collective-permute-start | bytes 393224 | tf_op jit(solution)/shard_map/ppermute | solution.py:85
  23.2 3.4 %collective-permute-start.6 = (bf16[64,1024]{1,0:T(8,128)(2,1)S(1)}, bf16[64,1024]{1,0:T(8,128)(2,1)S(1)}, u32[]{:S(2)}, u32[]{:S(2)}) collective-permute-start(bf16[64,1024]{1,0:T(8,128)(2,1)S(1)} %get-tuple-element.72), channel_id=1, source_target_pairs={{4,5},{8,9}} | collective-permute-start | bytes 393224 | tf_op jit(solution)/shard_map/ppermute | solution.py:85
  23.9 2.7 %collective-permute-start.7 = (bf16[64,1024]{1,0:T(8,128)(2,1)S(1)}, bf16[64,1024]{1,0:T(8,128)(2,1)S(1)}, u32[]{:S(2)}, u32[]{:S(2)}) collective-permute-start(bf16[64,1024]{1,0:T(8,128)(2,1)S(1)} %get-tuple-element.73), channel_id=1, source_target_pairs={{4,6},{8,10}} | collective-permute-start | bytes 393224 | tf_op jit(solution)/shard_map/ppermute | solution.py:85
  25.5 1.1 %collective-permute-start.8 = (bf16[64,1024]{1,0:T(8,128)(2,1)S(1)}, bf16[64,1024]{1,0:T(8,128)(2,1)S(1)}, u32[]{:S(2)}, u32[]{:S(2)}) collective-permute-start(bf16[64,1024]{1,0:T(8,128)(2,1)S(1)} %get-tuple-element.74), channel_id=1, source_target_pairs={{4,7},{8,11}} | collective-permute-start | bytes 393224 | tf_op jit(solution)/shard_map/ppermute | solution.py:85
  26.7 11.4 %collective-permute-start.13 = (bf16[64,1024]{1,0:T(8,128)(2,1)S(1)}, bf16[64,1024]{1,0:T(8,128)(2,1)S(1)}, u32[]{:S(2)}, u32[]{:S(2)}) collective-permute-start(bf16[64,1024]{1,0:T(8,128)(2,1)S(1)} %get-tuple-element.80.refs_0_), channel_id=1, source_target_pairs={{4,28},{5,29},{6,30},{7,31},{8,24},{9,25},{10,26},{11,27}} | collective-permute-start | bytes 393224 | tf_op jit(solution)/shard_map/ppermute | solution.py:85
  27.4 13.7 %collective-permute-start.12 = (bf16[64,1024]{1,0:T(8,128)(2,1)S(1)}, bf16[64,1024]{1,0:T(8,128)(2,1)S(1)}, u32[]{:S(2)}, u32[]{:S(2)}) collective-permute-start(bf16[64,1024]{1,0:T(8,128)(2,1)S(1)} %get-tuple-element.80.refs_0_), channel_id=1, source_target_pairs={{4,20},{5,21},{6,22},{7,23},{8,16},{9,17},{10,18},{11,19}} | collective-permute-start | bytes 393224 | tf_op jit(solution)/shard_map/ppermute | solution.py:85
  28.7 12.4 %collective-permute-start.11 = (bf16[64,1024]{1,0:T(8,128)(2,1)S(1)}, bf16[64,1024]{1,0:T(8,128)(2,1)S(1)}, u32[]{:S(2)}, u32[]{:S(2)}) collective-permute-start(bf16[64,1024]{1,0:T(8,128)(2,1)S(1)} %get-tuple-element.80.refs_0_), channel_id=1, source_target_pairs={{4,12},{5,13},{6,14},{7,15},{8,0},{9,1},{10,2},{11,3}} | collective-permute-start | bytes 393224 | tf_op jit(solution)/shard_map/ppermute | solution.py:85
  38.1 14.1 %collective-permute-start.15 = (bf16[256,1024]{1,0:T(8,128)(2,1)S(1)}, bf16[256,1024]{1,0:T(8,128)(2,1)S(1)}, u32[]{:S(2)}, u32[]{:S(2)}) collective-permute-start(bf16[256,1024]{1,0:T(8,128)(2,1)S(1)} %get-tuple-element.64.refs_0_), channel_id=1, source_target_pairs={{26,27},{24,25}} | collective-permute-start | bytes 1572872 | tf_op jit(solution)/shard_map/ppermute | solution.py:85
  41.7 10.6 %collective-permute-start.16 = (bf16[256,1024]{1,0:T(8,128)(2,1)S(1)}, bf16[256,1024]{1,0:T(8,128)(2,1)S(1)}, u32[]{:S(2)}, u32[]{:S(2)}) collective-permute-start(bf16[256,1024]{1,0:T(8,128)(2,1)S(1)} %get-tuple-element.86.refs_2_), channel_id=1, source_target_pairs={{22,23},{20,21}} | collective-permute-start | bytes 1572872 | tf_op jit(solution)/shard_map/ppermute | solution.py:85
  42.4 9.9 %collective-permute-start.17 = (bf16[64,1024]{1,0:T(8,128)(2,1)S(1)}, bf16[64,1024]{1,0:T(8,128)(2,1)S(1)}, u32[]{:S(2)}, u32[]{:S(2)}) collective-permute-start(bf16[64,1024]{1,0:T(8,128)(2,1)S(1)} %get-tuple-element.93), channel_id=1, source_target_pairs={{0,4},{1,5},{2,6},{3,7},{4,0},{5,1},{6,2},{7,3},{8,12},{9,13},{10,... | collective-permute-start | bytes 393224 | tf_op jit(solution)/shard_map/ppermute | solution.py:85
  52.6 15.5 %collective-permute-start.18 = (bf16[2,64,1024]{2,1,0:T(8,128)(2,1)S(1)}, bf16[2,64,1024]{2,1,0:T(8,128)(2,1)S(1)}, u32[]{:S(2)}, u32[]{:S(2)}) collective-permute-start(bf16[2,64,1024]{2,1,0:T(8,128)(2,1)S(1)} %get-tuple-element.99), channel_id=1, source_target_pairs={{24,0},{25,1},{26,2},{20,28},{21,29},{22,30},{23,31}} | collective-permute-start | bytes 786440 | tf_op jit(solution)/shard_map/ppermute | solution.py:85
  53.3 16.7 %collective-permute-start.19 = (bf16[2,64,1024]{2,1,0:T(8,128)(2,1)S(1)}, bf16[2,64,1024]{2,1,0:T(8,128)(2,1)S(1)}, u32[]{:S(2)}, u32[]{:S(2)}) collective-permute-start(bf16[2,64,1024]{2,1,0:T(8,128)(2,1)S(1)} %get-tuple-element.100), channel_id=1, source_target_pairs={{24,8},{25,9},{26,10},{20,4},{21,5},{22,6},{23,7}} | collective-permute-start | bytes 786440 | tf_op jit(solution)/shard_map/ppermute | solution.py:85
  53.9 22.9 %collective-permute-start.20 = (bf16[2,64,1024]{2,1,0:T(8,128)(2,1)S(1)}, bf16[2,64,1024]{2,1,0:T(8,128)(2,1)S(1)}, u32[]{:S(2)}, u32[]{:S(2)}) collective-permute-start(bf16[2,64,1024]{2,1,0:T(8,128)(2,1)S(1)} %get-tuple-element.101), channel_id=1, source_target_pairs={{24,16},{25,17},{26,18},{20,12},{21,13},{22,14},{23,15}} | collective-permute-start | bytes 786440 | tf_op jit(solution)/shard_map/ppermute | solution.py:85
  65.4 13.9 %collective-permute-start.21 = (bf16[64,1024]{1,0:T(8,128)(2,1)S(1)}, bf16[64,1024]{1,0:T(8,128)(2,1)S(1)}, u32[]{:S(2)}, u32[]{:S(2)}) collective-permute-start(bf16[64,1024]{1,0:T(8,128)(2,1)S(1)} %get-tuple-element.106), channel_id=1, source_target_pairs={{4,5},{5,6},{8,9},{9,10},{12,13},{13,14},{16,17},{17,18},{20,21},{... | collective-permute-start | bytes 393224 | tf_op jit(solution)/shard_map/ppermute | solution.py:85
  66.7 12.6 %collective-permute-start.22 = (bf16[64,1024]{1,0:T(8,128)(2,1)S(1)}, bf16[64,1024]{1,0:T(8,128)(2,1)S(1)}, u32[]{:S(2)}, u32[]{:S(2)}) collective-permute-start(bf16[64,1024]{1,0:T(8,128)(2,1)S(1)} %get-tuple-element.107), channel_id=1, source_target_pairs={{4,6},{5,7},{8,10},{9,11},{12,14},{13,15},{16,18},{17,19},{20,22},... | collective-permute-start | bytes 393224 | tf_op jit(solution)/shard_map/ppermute | solution.py:85
  68.1 11.3 %collective-permute-start.23 = (bf16[64,1024]{1,0:T(8,128)(2,1)S(1)}, bf16[64,1024]{1,0:T(8,128)(2,1)S(1)}, u32[]{:S(2)}, u32[]{:S(2)}) collective-permute-start(bf16[64,1024]{1,0:T(8,128)(2,1)S(1)} %get-tuple-element.108), channel_id=1, source_target_pairs={{4,7},{5,4},{8,11},{9,8},{12,15},{13,12},{16,19},{17,16},{20,23},{... | collective-permute-start | bytes 393224 | tf_op jit(solution)/shard_map/ppermute | solution.py:85
  77.1 5.2 %collective-permute-start.24 = (bf16[64,1024]{1,0:T(8,128)(2,1)S(1)}, bf16[64,1024]{1,0:T(8,128)(2,1)S(1)}, u32[]{:S(2)}, u32[]{:S(2)}) collective-permute-start(bf16[64,1024]{1,0:T(8,128)(2,1)S(1)} %get-tuple-element.110), channel_id=1, source_target_pairs={{0,4},{1,5},{2,6},{3,7},{4,0},{5,1},{6,2},{7,3},{8,12},{9,13},{10,... | collective-permute-start | bytes 393224 | tf_op jit(solution)/shard_map/ppermute | solution.py:85
